TPU v7x, 256 devices: a whole 4x4x8 slice. The times are simulated.
256 devices in a mesh: dp: 16 (over z, core), seq: 16 (over x, y).
Axes of the slice: x: 4, y: 4, z: 8, core: 2. Of those that a mesh axis runs over, the one named last changes fastest.
Arguments:
- queries: bfloat16 [16, 2048, 2048], P('dp', 'seq'), may hold values from -30 to 30
- keys_in: bfloat16 [16, 2048, 2048], P('dp', 'seq'), may hold values from -30 to 30
- values_in: bfloat16 [16, 2048, 2048], P('dp', 'seq'), may hold values from -1.5 to 1.5
- saved_out: bfloat16 [16, 2048, 2048], P('dp', 'seq'), may hold values from -0.75 to 0.75
- out_grad: bfloat16 [16, 2048, 3200], P('dp', 'seq'), may hold values from -6 to 6
- out_weight: bfloat16 [2048, 3200], P('seq'), may hold values from -0.125 to 0.125
- image_units: int32 [16, 8], P('dp'), may hold values from 1 to 32, 128 in all within a row
Outputs:
- query_grad: bfloat16 [16, 2048, 2048], P('dp', 'seq')
- key_grad: bfloat16 [16, 2048, 2048], P('dp', 'seq')
- value_grad: bfloat16 [16, 2048, 2048], P('dp', 'seq')
- weight_grad: float32 [2048, 3200], P('seq', 'dp')
Inputs may be any that keep to these rules, and one draw needn't show every extreme that they name: `image_units`: each row sums to 128 and its largest entry is 32.
All inputs are finite; a program needn't handle non-finite values.
Results may differ from a plain program's by a relative error of at most 0.015.
Values may be sent and summed in bfloat16 or wider, within the bound.
No kernel may reach another device: no remote copies, remote signals or barrier semaphores. Data moves between devices by JAX's collectives and lax.ppermute only.
A program may use at most 128 MiB of HBM per device.

v0:
```python
import math

import jax
import jax.numpy as jnp
from jax import lax
from jax.sharding import PartitionSpec as P

HEAD_DIM = 128


def image_tables(units, length):
    sizes = units * 16
    bounds = jnp.cumsum(sizes)
    places = jnp.arange(length, dtype=jnp.int32)
    owners = jnp.sum((places[:, None] >= bounds[None, :]).astype(jnp.int32), axis=1)
    openings = jnp.sum(jnp.where(bounds[None, :] <= places[:, None], sizes[None, :], 0), axis=1)
    return (owners, openings)


def rounded(value):
    return lax.optimization_barrier(value.astype(jnp.bfloat16)).astype(jnp.float32)


def attend_back(query_head, key_head, value_head, output_head, grad_head, owners):
    length, columns = query_head.shape
    head_count = columns // HEAD_DIM
    block_rows = min(length, 512)
    scaling = 1.0 / math.sqrt(HEAD_DIM)
    split_shape = (length, head_count, HEAD_DIM)
    query_split = query_head.reshape(split_shape)
    key_split = key_head.reshape(split_shape)
    value_split = value_head.reshape(split_shape)
    output_split = output_head.reshape(split_shape)
    grad_split = grad_head.reshape(split_shape)

    def one_block(counter, running):
        query_acc, key_acc, value_acc = running
        first_row = (counter * block_rows).astype(jnp.int32)
        query_rows = lax.dynamic_slice_in_dim(query_split, first_row, block_rows, 0)
        out_rows = lax.dynamic_slice_in_dim(output_split, first_row, block_rows, 0)
        grad_rows = lax.dynamic_slice_in_dim(grad_split, first_row, block_rows, 0)
        same_image = (
            lax.dynamic_slice_in_dim(owners, first_row, block_rows, 0)[:, None] == owners[None, :]
        )
        scores = (
            jnp.einsum("qhd,khd->hqk", query_rows, key_split, preferred_element_type=jnp.float32)
            * scaling
        )
        scores = jnp.where(same_image[None], scores, jnp.float32(-1e30))
        largest = jnp.max(scores, axis=2, keepdims=True)
        log_total = largest + jnp.log(jnp.sum(jnp.exp(scores - largest), axis=2, keepdims=True))
        weights = jnp.exp(scores - log_total)
        weights_low = weights.astype(jnp.bfloat16)
        row_delta = jnp.sum(grad_rows.astype(jnp.float32) * out_rows.astype(jnp.float32), axis=2).T
        weight_grads = jnp.einsum(
            "qhd,khd->hqk", grad_rows, value_split, preferred_element_type=jnp.float32
        )
        score_grads = (weights * (weight_grads - row_delta[:, :, None])).astype(jnp.bfloat16)
        query_part = (
            jnp.einsum("hqk,khd->qhd", score_grads, key_split, preferred_element_type=jnp.float32)
            * scaling
        )
        key_part = (
            jnp.einsum("hqk,qhd->khd", score_grads, query_rows, preferred_element_type=jnp.float32)
            * scaling
        )
        value_part = jnp.einsum(
            "hqk,qhd->khd", weights_low, grad_rows, preferred_element_type=jnp.float32
        )
        query_acc = lax.dynamic_update_slice_in_dim(query_acc, query_part, first_row, 0)
        key_acc = key_acc + key_part
        value_acc = value_acc + value_part
        return (query_acc, key_acc, value_acc)

    empty_acc = jnp.zeros(split_shape, jnp.float32)
    results = lax.fori_loop(0, length // block_rows, one_block, (empty_acc, empty_acc, empty_acc))
    return tuple((item.reshape(length, columns).astype(jnp.bfloat16) for item in results))


def on_device(queries, keys_in, values_in, saved_out, out_grad, out_weight, image_units):
    local_rows = queries.shape[1]
    all_columns = queries.shape[2]
    pack_len = local_rows * lax.axis_size("seq")
    query_local = queries.reshape(local_rows, all_columns)
    key_local = keys_in.reshape(local_rows, all_columns)
    value_local = values_in.reshape(local_rows, all_columns)
    output_local = saved_out.reshape(local_rows, all_columns)
    grad_local = out_grad.reshape(local_rows, out_grad.shape[2])
    owners, openings = image_tables(image_units[0], pack_len)
    head_local = lax.dot_general(
        grad_local,
        lax.all_gather(out_weight, "seq", axis=0, tiled=True),
        (((1,), (1,)), ((), ())),
        preferred_element_type=jnp.float32,
    ).astype(jnp.bfloat16)
    query_head, key_head, value_head, output_head, grad_head = (
        lax.all_to_all(query_local, "seq", split_axis=1, concat_axis=0, tiled=True),
        lax.all_to_all(key_local, "seq", split_axis=1, concat_axis=0, tiled=True),
        lax.all_to_all(value_local, "seq", split_axis=1, concat_axis=0, tiled=True),
        lax.all_to_all(output_local, "seq", split_axis=1, concat_axis=0, tiled=True),
        lax.all_to_all(head_local, "seq", split_axis=1, concat_axis=0, tiled=True),
    )
    partial_grad = lax.psum_scatter(
        rounded(jnp.dot(output_local.T, grad_local, preferred_element_type=jnp.float32)).astype(
            jnp.bfloat16
        ),
        "seq",
        scatter_dimension=0,
        tiled=True,
    ).astype(jnp.float32)
    query_back, key_back, value_back = attend_back(
        query_head, key_head, value_head, output_head, grad_head, owners
    )
    query_rows, key_rows, value_rows = (
        lax.all_to_all(query_back, "seq", split_axis=0, concat_axis=1, tiled=True),
        lax.all_to_all(key_back, "seq", split_axis=0, concat_axis=1, tiled=True),
        lax.all_to_all(value_back, "seq", split_axis=0, concat_axis=1, tiled=True),
    )
    weight_grad = lax.psum_scatter(partial_grad, "dp", scatter_dimension=1, tiled=True) * (
        1.0 / math.sqrt(pack_len * lax.axis_size("dp"))
    )
    out_shape = (1, local_rows, all_columns)
    return (
        query_rows.reshape(out_shape),
        key_rows.reshape(out_shape),
        value_rows.reshape(out_shape),
        weight_grad,
    )


def solution(mesh):
    placed = (
        P("dp", "seq", None),
        P("dp", "seq", None),
        P("dp", "seq", None),
        P("dp", "seq", None),
        P("dp", "seq", None),
        P("seq", None),
        P("dp", None),
    )
    return jax.shard_map(
        on_device,
        mesh=mesh,
        in_specs=placed,
        out_specs=(
            P("dp", "seq", None),
            P("dp", "seq", None),
            P("dp", "seq", None),
            P("seq", "dp"),
        ),
        check_vma=False,
    )
```

profile of v0, /device:TPU:2, one launch (start us, length us, event | category | flops | bytes accessed | tf_op | source)
XLA Modules:
  0.0 335.1 jit_solution(12656931550392240611)
XLA Ops:
  8.3 9.3 %convolution_convert_fusion = bf16[2048,3200]{1,0:T(8,128)(2,1)} fusion(bf16[1,128,3200]{2,1,0:T(8,128)(2,1)S(1)} %copy-done, bf16[1,128,2048]{2,1,0:T(8,128)(2,1)} %param.12), kind=kOutput, calls=%fused_computation.31 | convolution fusion | flops 1684275200 | bytes 14450688 | tf_op jit(solution)/shard_map/dot_general | solution.py:104
  19.7 7.5 %all-to-all-start.3 = ((bf16[128,16,128]{0,2,1:T(8,128)(2,1)}), bf16[128,16,128]{0,2,1:T(8,128)(2,1)S(1)}, u32[]{:S(2)}, u32[]{:S(2)}) async-start(bf16[128,16,128]{0,2,1:T(8,128)(2,1)} %bitcast.11), calls=%async_computation.3 | async-start | bytes 1048576 | tf_op jit(solution)/shard_map/all_to_all | solution.py:99
  28.2 14.3 %all-to-all-done.3 = bf16[128,16,128]{0,2,1:T(8,128)(2,1)S(1)} async-done(((bf16[128,16,128]{0,2,1:T(8,128)(2,1)}), bf16[128,16,128]{0,2,1:T(8,128)(2,1)S(1)}, u32[]{:S(2)}, u32[]{:S(2)}) %all-to-all-start.3) | async-done | bytes 524320 | tf_op jit(solution)/shard_map/all_to_all | solution.py:99
  42.4 5.9 %all-to-all-start.4 = ((bf16[128,16,128]{0,2,1:T(8,128)(2,1)}), bf16[128,16,128]{0,2,1:T(8,128)(2,1)S(1)}, u32[]{:S(2)}, u32[]{:S(2)}) async-start(bf16[128,16,128]{0,2,1:T(8,128)(2,1)} %bitcast.14), calls=%async_computation.4 | async-start | bytes 1048576 | tf_op jit(solution)/shard_map/all_to_all | solution.py:100
  49.3 7.2 %all-to-all-done.4 = bf16[128,16,128]{0,2,1:T(8,128)(2,1)S(1)} async-done(((bf16[128,16,128]{0,2,1:T(8,128)(2,1)}), bf16[128,16,128]{0,2,1:T(8,128)(2,1)S(1)}, u32[]{:S(2)}, u32[]{:S(2)}) %all-to-all-start.4) | async-done | bytes 524320 | tf_op jit(solution)/shard_map/all_to_all | solution.py:100
  56.5 5.7 %all-to-all-start = ((bf16[128,16,128]{0,2,1:T(8,128)(2,1)}), bf16[128,16,128]{0,2,1:T(8,128)(2,1)S(1)}, u32[]{:S(2)}, u32[]{:S(2)}) async-start(bf16[128,16,128]{0,2,1:T(8,128)(2,1)} %bitcast.2), calls=%async_computation | async-start | bytes 1048576 | tf_op jit(solution)/shard_map/all_to_all | solution.py:97
  63.2 13.3 %all-to-all-done = bf16[128,16,128]{0,2,1:T(8,128)(2,1)S(1)} async-done(((bf16[128,16,128]{0,2,1:T(8,128)(2,1)}), bf16[128,16,128]{0,2,1:T(8,128)(2,1)S(1)}, u32[]{:S(2)}, u32[]{:S(2)}) %all-to-all-start) | async-done | bytes 524320 | tf_op jit(solution)/shard_map/all_to_all | solution.py:97
  76.5 6.1 %all-to-all-start.1 = ((bf16[128,16,128]{0,2,1:T(8,128)(2,1)}), bf16[128,16,128]{0,2,1:T(8,128)(2,1)S(1)}, u32[]{:S(2)}, u32[]{:S(2)}) async-start(bf16[128,16,128]{0,2,1:T(8,128)(2,1)} %bitcast.5), calls=%async_computation.1 | async-start | bytes 1048576 | tf_op jit(solution)/shard_map/all_to_all | solution.py:98
  82.7 44.7 %all-gather.2.cloned.1.call-done = bf16[2048,3200]{1,0:T(8,128)(2,1)} async-done(((bf16[128,3200]{1,0:T(8,128)(2,1)}), bf16[2048,3200]{1,0:T(8,128)(2,1)}) %all-gather.2.cloned.1.call-update) | async-done | bytes 13107216 | tf_op jit(solution)/shard_map/all_gather | solution.py:92
  127.3 9.0 %fusion.23 = bf16[16,16,8,128]{3,2,1,0:T(8,128)(2,1)S(1)} fusion(bf16[2048,3200]{1,0:T(8,128)(2,1)} %all-gather.2.cloned.1.call-done, bf16[1,128,3200]{2,1,0:T(8,128)(2,1)S(1)} %copy-done), kind=kOutput, calls=%fused_computation.33 | convolution fusion | flops 1677983744 | bytes 14450688 | tf_op jit(solution)/shard_map/dot_general | solution.py:90
  138.1 5.8 %all-to-all-start.2 = ((bf16[128,16,128]{2,0,1:T(8,128)(2,1)}), bf16[128,16,128]{2,0,1:T(8,128)(2,1)}, u32[]{:S(2)}, u32[]{:S(2)}) async-start(bf16[128,16,128]{2,0,1:T(8,128)(2,1)} %bitcast.90), calls=%async_computation.2 | async-start | bytes 1048576 | tf_op jit(solution)/shard_map/all_to_all | solution.py:101
  145.5 2.1 copy.76
  151.7 7.7 %all-to-all-done.2 = bf16[128,16,128]{2,0,1:T(8,128)(2,1)} async-done(((bf16[128,16,128]{2,0,1:T(8,128)(2,1)}), bf16[128,16,128]{2,0,1:T(8,128)(2,1)}, u32[]{:S(2)}, u32[]{:S(2)}) %all-to-all-start.2) | async-done | bytes 524320 | tf_op jit(solution)/shard_map/all_to_all | solution.py:101
  160.2 57.9 %while.18 = (s32[]{:T(128)}, bf16[2048,1,128]{2,0,1:T(8,128)(2,1)}, f32[2048,1,128]{0,2,1:T(8,128)S(1)}, f32[2048,1,128]{0,2,1:T(8,128)S(1)}, s32[2048]{0:T(1024...) while((s32[]{:T(128)}, bf16[2048,1,128]{2,0,1:T(8,128)(2,1)}, ...), condition=%wide.region_6.7_spmd.clone, body=%wide.region_2.6_spmd.clone.sunk | while | flops 1356397568 | bytes 65571112 | solution.py:76
  164.9 3.9 %fusion.54 = f32[2048,1,128]{0,2,1:T(8,128)S(1)} fusion(f32[512,2048]{1,0:T(8,128)} %copy-done.1, f32[512]{0:T(512)S(1)} %log_add_fusion.2, f32[2048,1,128]{0,2,1:T(8,128)S(1)} %get-tuple-element.339, pred[]{:T(512)S(6)} %compare.3, bf16[2048,1,128]{2,0,1:T(8,128)(2,1)} %get-tuple-element.357, s32[]{:T(128)S(6)} %select_n.24), kind=kOutput, calls=%fused_computation.8.clone.1 | convolution fusion | flops 271056896 | bytes 6424581 | tf_op jit(solution)/shard_map/while/body/eval_jaxpr/hqk,qhd->khd/dot_general | solution.py:67
  179.6 3.7 %fusion.54 = f32[2048,1,128]{0,2,1:T(8,128)S(1)} fusion(f32[512,2048]{1,0:T(8,128)} %copy-done.1, f32[512]{0:T(512)S(1)} %log_add_fusion.2, f32[2048,1,128]{0,2,1:T(8,128)S(1)} %get-tuple-element.339, pred[]{:T(512)S(6)} %compare.3, bf16[2048,1,128]{2,0,1:T(8,128)(2,1)} %get-tuple-element.357, s32[]{:T(128)S(6)} %select_n.24), kind=kOutput, calls=%fused_computation.8.clone.1 | convolution fusion | flops 271056896 | bytes 6424581 | tf_op jit(solution)/shard_map/while/body/eval_jaxpr/hqk,qhd->khd/dot_general | solution.py:67
  194.2 3.7 %fusion.54 = f32[2048,1,128]{0,2,1:T(8,128)S(1)} fusion(f32[512,2048]{1,0:T(8,128)} %copy-done.1, f32[512]{0:T(512)S(1)} %log_add_fusion.2, f32[2048,1,128]{0,2,1:T(8,128)S(1)} %get-tuple-element.339, pred[]{:T(512)S(6)} %compare.3, bf16[2048,1,128]{2,0,1:T(8,128)(2,1)} %get-tuple-element.357, s32[]{:T(128)S(6)} %select_n.24), kind=kOutput, calls=%fused_computation.8.clone.1 | convolution fusion | flops 271056896 | bytes 6424581 | tf_op jit(solution)/shard_map/while/body/eval_jaxpr/hqk,qhd->khd/dot_general | solution.py:67
  208.7 3.5 %fusion.54 = f32[2048,1,128]{0,2,1:T(8,128)S(1)} fusion(f32[512,2048]{1,0:T(8,128)} %copy-done.1, f32[512]{0:T(512)S(1)} %log_add_fusion.2, f32[2048,1,128]{0,2,1:T(8,128)S(1)} %get-tuple-element.339, pred[]{:T(512)S(6)} %compare.3, bf16[2048,1,128]{2,0,1:T(8,128)(2,1)} %get-tuple-element.357, s32[]{:T(128)S(6)} %select_n.24), kind=kOutput, calls=%fused_computation.8.clone.1 | convolution fusion | flops 271056896 | bytes 6424581 | tf_op jit(solution)/shard_map/while/body/eval_jaxpr/hqk,qhd->khd/dot_general | solution.py:67
  219.2 5.9 %all-to-all-start.6 = ((bf16[16,128,128]{2,1,0:T(8,128)(2,1)}), bf16[16,128,128]{2,1,0:T(8,128)(2,1)S(1)}, u32[]{:S(2)}, u32[]{:S(2)}) async-start(bf16[16,128,128]{2,1,0:T(8,128)(2,1)} %bitcast.20), calls=%async_computation.6 | async-start | bytes 1048576 | tf_op jit(solution)/shard_map/all_to_all | solution.py:116
  225.4 14.1 %all-to-all-done.6 = bf16[16,128,128]{2,1,0:T(8,128)(2,1)S(1)} async-done(((bf16[16,128,128]{2,1,0:T(8,128)(2,1)}), bf16[16,128,128]{2,1,0:T(8,128)(2,1)S(1)}, u32[]{:S(2)}, u32[]{:S(2)}) %all-to-all-start.6) | async-done | bytes 524320 | tf_op jit(solution)/shard_map/all_to_all | solution.py:116
  239.5 14.3 %all_to_all.119 = bf16[16,128,128]{2,1,0:T(8,128)(2,1)S(1)} all-to-all(bf16[16,128,128]{2,1,0:T(8,128)(2,1)S(1)} %bitcast.123), channel_id=1, replica_groups=mesh['dp'=16,'seq'=16] {'seq'}, dimensions={0} | all-to-all | bytes 1048576 | tf_op jit(solution)/shard_map/all_to_all | solution.py:117
  253.8 5.7 %all-to-all-start.5 = ((bf16[16,128,128]{2,1,0:T(8,128)(2,1)}), bf16[16,128,128]{2,1,0:T(8,128)(2,1)S(1)}, u32[]{:S(2)}, u32[]{:S(2)}) async-start(bf16[16,128,128]{2,1,0:T(8,128)(2,1)} %bitcast.17), calls=%async_computation.5 | async-start | bytes 1048576 | tf_op jit(solution)/shard_map/all_to_all | solution.py:115
  263.3 4.0 %all-to-all-done.5 = bf16[16,128,128]{2,1,0:T(8,128)(2,1)S(1)} async-done(((bf16[16,128,128]{2,1,0:T(8,128)(2,1)}), bf16[16,128,128]{2,1,0:T(8,128)(2,1)S(1)}, u32[]{:S(2)}, u32[]{:S(2)}) %all-to-all-start.5) | async-done | bytes 524320 | tf_op jit(solution)/shard_map/all_to_all | solution.py:115
  268.7 58.7 %all-reduce.2 = f32[128,3200]{1,0:T(8,128)S(1)} all-reduce(bf16[128,3200]{1,0:T(8,128)(2,1)} %reduce-scatter.3.cloned.1.call-done), channel_id=3, replica_groups=mesh['dp'=16,'seq'=16] {'dp'}, use_global_device_ids=true, to_apply=%region_8.9.clone | all-reduce | flops 409600 | bytes 2457600
  (111 shorter events, 64.0 us)
Async XLA Ops:
  7.2 120.1 %all-gather.2.cloned.1.call-start = ((), (), s32[]{:S(2)}) async-start(), calls=%async_computation.9 | async-start | bytes 13926400 | tf_op jit(solution)/shard_map/all_gather | solution.py:92
  7.9 260.8 %reduce-scatter.3.cloned.1.call-start = ((), (), s32[]{:S(2)}) async-start(), calls=%async_computation.10 | async-start | bytes 13926400 | tf_op jit(solution)/shard_map/reduce_scatter | solution.py:103
  17.7 9.5 %copy-start.4 = (bf16[1,128,2048]{2,1,0:T(8,128)(2,1)S(1)}, bf16[1,128,2048]{2,1,0:T(8,128)(2,1)}, u32[]{:S(2)}) copy-start(bf16[1,128,2048]{2,1,0:T(8,128)(2,1)} %param.12) | copy-start | bytes 1572868
  18.7 29.6 %copy-start.10 = (bf16[1,128,2048]{2,1,0:T(8,128)(2,1)S(1)}, bf16[1,128,2048]{2,1,0:T(8,128)(2,1)}, u32[]{:S(2)}) copy-start(bf16[1,128,2048]{2,1,0:T(8,128)(2,1)} %param.9) | copy-start | bytes 1572868
  18.7 43.5 %copy-start.11 = (bf16[1,128,2048]{2,1,0:T(8,128)(2,1)S(1)}, bf16[1,128,2048]{2,1,0:T(8,128)(2,1)}, u32[]{:S(2)}) copy-start(bf16[1,128,2048]{2,1,0:T(8,128)(2,1)} %param.10) | copy-start | bytes 1572868
  19.7 22.7 %all-to-all-start.3 = ((bf16[128,16,128]{0,2,1:T(8,128)(2,1)}), bf16[128,16,128]{0,2,1:T(8,128)(2,1)S(1)}, u32[]{:S(2)}, u32[]{:S(2)}) async-start(bf16[128,16,128]{0,2,1:T(8,128)(2,1)} %bitcast.11), calls=%async_computation.3 | async-start | bytes 1048576 | tf_op jit(solution)/shard_map/all_to_all | solution.py:99
  42.4 93.9 %copy-start.5 = (bf16[128,16,128]{0,2,1:T(8,128)(2,1)}, bf16[128,16,128]{0,2,1:T(8,128)(2,1)S(1)}, u32[]{:S(2)}) copy-start(bf16[128,16,128]{0,2,1:T(8,128)(2,1)S(1)} %all-to-all-done.3) | copy-start | bytes 1572868
  42.4 14.0 %all-to-all-start.4 = ((bf16[128,16,128]{0,2,1:T(8,128)(2,1)}), bf16[128,16,128]{0,2,1:T(8,128)(2,1)S(1)}, u32[]{:S(2)}, u32[]{:S(2)}) async-start(bf16[128,16,128]{0,2,1:T(8,128)(2,1)} %bitcast.14), calls=%async_computation.4 | async-start | bytes 1048576 | tf_op jit(solution)/shard_map/all_to_all | solution.py:100
  56.5 79.8 %copy-start.6 = (bf16[128,16,128]{0,2,1:T(8,128)(2,1)}, bf16[128,16,128]{0,2,1:T(8,128)(2,1)S(1)}, u32[]{:S(2)}) copy-start(bf16[128,16,128]{0,2,1:T(8,128)(2,1)S(1)} %all-to-all-done.4) | copy-start | bytes 1572868
  56.5 20.0 %all-to-all-start = ((bf16[128,16,128]{0,2,1:T(8,128)(2,1)}), bf16[128,16,128]{0,2,1:T(8,128)(2,1)S(1)}, u32[]{:S(2)}, u32[]{:S(2)}) async-start(bf16[128,16,128]{0,2,1:T(8,128)(2,1)} %bitcast.2), calls=%async_computation | async-start | bytes 1048576 | tf_op jit(solution)/shard_map/all_to_all | solution.py:97
  76.5 59.8 %copy-start.7 = (bf16[128,16,128]{0,2,1:T(8,128)(2,1)}, bf16[128,16,128]{0,2,1:T(8,128)(2,1)S(1)}, u32[]{:S(2)}) copy-start(bf16[128,16,128]{0,2,1:T(8,128)(2,1)S(1)} %all-to-all-done) | copy-start | bytes 1572868
  76.5 60.8 %all-to-all-start.1 = ((bf16[128,16,128]{0,2,1:T(8,128)(2,1)}), bf16[128,16,128]{0,2,1:T(8,128)(2,1)S(1)}, u32[]{:S(2)}, u32[]{:S(2)}) async-start(bf16[128,16,128]{0,2,1:T(8,128)(2,1)} %bitcast.5), calls=%async_computation.1 | async-start | bytes 1048576 | tf_op jit(solution)/shard_map/all_to_all | solution.py:98
  82.6 61.2 %copy-start.12 = (s32[1,8]{1,0:T(1,128)S(1)}, s32[1,8]{1,0:T(1,128)}, u32[]{:S(2)}) copy-start(s32[1,8]{1,0:T(1,128)} %param.15) | copy-start | bytes 100
  138.1 21.2 %all-to-all-start.2 = ((bf16[128,16,128]{2,0,1:T(8,128)(2,1)}), bf16[128,16,128]{2,0,1:T(8,128)(2,1)}, u32[]{:S(2)}, u32[]{:S(2)}) async-start(bf16[128,16,128]{2,0,1:T(8,128)(2,1)} %bitcast.90), calls=%async_computation.2 | async-start | bytes 1048576 | tf_op jit(solution)/shard_map/all_to_all | solution.py:101
  164.9 5.0 %copy-start.2 = (f32[512,2048]{1,0:T(8,128)S(1)}, f32[512,2048]{1,0:T(8,128)}, u32[]{:S(2)}) copy-start(f32[512,2048]{1,0:T(8,128)} %copy-done.1) | copy-start | bytes 12582916 | tf_op jit(solution)/shard_map/while
  170.0 3.5 %copy-start.3 = (bf16[2048,1,128]{2,0,1:T(8,128)(2,1)S(1)}, bf16[2048,1,128]{2,0,1:T(8,128)(2,1)}, u32[]{:S(2)}) copy-start(bf16[2048,1,128]{2,0,1:T(8,128)(2,1)} %get-tuple-element.356) | copy-start | bytes 1572868 | tf_op jit(solution)/shard_map/while
  179.6 4.9 %copy-start.2 = (f32[512,2048]{1,0:T(8,128)S(1)}, f32[512,2048]{1,0:T(8,128)}, u32[]{:S(2)}) copy-start(f32[512,2048]{1,0:T(8,128)} %copy-done.1) | copy-start | bytes 12582916 | tf_op jit(solution)/shard_map/while
  184.5 3.5 %copy-start.3 = (bf16[2048,1,128]{2,0,1:T(8,128)(2,1)S(1)}, bf16[2048,1,128]{2,0,1:T(8,128)(2,1)}, u32[]{:S(2)}) copy-start(bf16[2048,1,128]{2,0,1:T(8,128)(2,1)} %get-tuple-element.356) | copy-start | bytes 1572868 | tf_op jit(solution)/shard_map/while
  194.1 4.9 %copy-start.2 = (f32[512,2048]{1,0:T(8,128)S(1)}, f32[512,2048]{1,0:T(8,128)}, u32[]{:S(2)}) copy-start(f32[512,2048]{1,0:T(8,128)} %copy-done.1) | copy-start | bytes 12582916 | tf_op jit(solution)/shard_map/while
  199.0 3.5 %copy-start.3 = (bf16[2048,1,128]{2,0,1:T(8,128)(2,1)S(1)}, bf16[2048,1,128]{2,0,1:T(8,128)(2,1)}, u32[]{:S(2)}) copy-start(bf16[2048,1,128]{2,0,1:T(8,128)(2,1)} %get-tuple-element.356) | copy-start | bytes 1572868 | tf_op jit(solution)/shard_map/while
  208.7 4.6 %copy-start.2 = (f32[512,2048]{1,0:T(8,128)S(1)}, f32[512,2048]{1,0:T(8,128)}, u32[]{:S(2)}) copy-start(f32[512,2048]{1,0:T(8,128)} %copy-done.1) | copy-start | bytes 12582916 | tf_op jit(solution)/shard_map/while
  218.1 41.4 %copy-start.13 = (u32[256]{0:T(256)S(1)}, u32[256]{0:T(256)}, u32[]{:S(2)}) copy-start(u32[256]{0:T(256)} %constant.73) | copy-start | bytes 3076
  219.2 20.4 %all-to-all-start.6 = ((bf16[16,128,128]{2,1,0:T(8,128)(2,1)}), bf16[16,128,128]{2,1,0:T(8,128)(2,1)S(1)}, u32[]{:S(2)}, u32[]{:S(2)}) async-start(bf16[16,128,128]{2,1,0:T(8,128)(2,1)} %bitcast.20), calls=%async_computation.6 | async-start | bytes 1048576 | tf_op jit(solution)/shard_map/all_to_all | solution.py:116
  253.8 13.6 %all-to-all-start.5 = ((bf16[16,128,128]{2,1,0:T(8,128)(2,1)}), bf16[16,128,128]{2,1,0:T(8,128)(2,1)S(1)}, u32[]{:S(2)}, u32[]{:S(2)}) async-start(bf16[16,128,128]{2,1,0:T(8,128)(2,1)} %bitcast.17), calls=%async_computation.5 | async-start | bytes 1048576 | tf_op jit(solution)/shard_map/all_to_all | solution.py:115
  (8 other events, 14.2 us)
Sparse Core Ops, SparseCore 0:
  10.5 116.7 all-gather.1
  131.0 110.9 reduce-scatter.2
where the time goes:
time: 338 us; the launch traced here: 335 us
  waiting for transfers between devices  106 us (31%)
  blocking collectives  73 us (22%)
  matrix products  60.6 us (18%)
  starting transfers between devices  42.6 us (13%)
  local copies, waits for them, and re-layouts  30.1 us (9%)
  between operations  14.9 us (4%)
  other arithmetic  7.86 us (2%)
    unnamed x1, blocking collectives  58.7 us
    all_gather x1, waiting for transfers between devices, on_device(): lax.all_gather(out_weight, 'seq', axis=0, tiled=True)  44.7 us
    dot_general x4, matrix products, one_block(): jnp.einsum('hqk,qhd->khd', weights_low, grad_rows, preferred_element_type...  14.8 us
    all_to_all x1, blocking collectives, on_device(): lax.all_to_all(value_back, 'seq', split_axis=0, concat_axis=1, tiled=True)  14.3 us
    all_to_all x1, waiting for transfers between devices, on_device(): lax.all_to_all(value_local, 'seq', split_axis=1, concat_axis=0, tiled=True)  14.3 us
    all_to_all x1, waiting for transfers between devices, on_device(): lax.all_to_all(key_back, 'seq', split_axis=0, concat_axis=1, tiled=True)  14.1 us
    all_to_all x1, waiting for transfers between devices, on_device(): lax.all_to_all(query_local, 'seq', split_axis=1, concat_axis=0, tiled=True)  13.3 us
    unnamed x31, local copies, waits for them, and re-layouts  10.6 us
  transfers between devices with their start and end apart: 9, of which 7 were waited for; matrix products, arithmetic and copies ran while one was open for 26% of the time, Pallas kernels for 0%

commit v1 on v0

v1 whole, which is shorter than its diff:
```python
import math

import jax
import jax.numpy as jnp
from jax import lax
from jax.experimental import pallas as pl
from jax.experimental.pallas import tpu as pltpu
from jax.sharding import PartitionSpec as P

HEAD = 128
PACK = 2048
TOK = 128
MODEL = 3200
IMG = 512
SEGS = 8
NEG = -1e30
BF = jnp.bfloat16
F32 = jnp.float32
XS = [[(4 * x + y, 4 * ((x + k) % 4) + y) for x in range(4) for y in range(4)] for k in range(4)]
YS = [[(4 * x + y, 4 * x + (y + k) % 4) for x in range(4) for y in range(4)] for k in range(4)]
YGROUPS = [[4 * x + y for y in range(4)] for x in range(4)]
CORES = [(i, i ^ 1) for i in range(16)]
ZGROUPS = [[2 * z + c for z in range(8)] for c in range(2)]


def nt(a, b):
    return lax.dot_general(a, b, (((1,), (1,)), ((), ())), preferred_element_type=F32)


def nn(a, b):
    return lax.dot_general(a, b, (((1,), (0,)), ((), ())), preferred_element_type=F32)


def tn(a, b):
    return lax.dot_general(a, b, (((0,), (0,)), ((), ())), preferred_element_type=F32)


def attention_kernel(xi, units, qkv, h0, h1, h2, h3, out, qs, ks, vs, hs, ds_, gq, gk, gv):
    for i in range(16):
        rows = pl.ds(i * TOK, TOK)
        qs[rows, :] = qkv[i, 0]
        ks[rows, :] = qkv[i, 1]
        vs[rows, :] = qkv[i, 2]
    tail = pl.ds(PACK, IMG)
    for ref in (qs, ks, vs, hs):
        ref[tail, :] = jnp.zeros((IMG, HEAD), BF)
    ds_[pl.ds(16, 8), :] = jnp.zeros((8, HEAD), F32)
    for k, h in enumerate((h0, h1, h2, h3)):
        block = lax.rem(xi[0] + k, 4)
        hs[pl.ds(pl.multiple_of(block * IMG, IMG), IMG), :] = h[pl.ds(0, IMG), :]
        parts = h[pl.ds(IMG, 16), :].astype(F32)
        ds_[pl.ds(block * 4, 4), :] = parts[0:4] + parts[4:8] + parts[8:12]
    scaling = 1.0 / math.sqrt(HEAD)
    to_two = scaling * math.log2(math.e)

    def image(start, size, width, step):
        kw = ks[pl.ds(start, width), :]
        vw = vs[pl.ds(start, width), :]
        row = lax.broadcasted_iota(jnp.int32, (width, 1), 0)
        bias = jnp.where(row < size, 0.0, NEG).astype(F32)
        first = lax.div(start, TOK)
        shift = start - first * TOK
        gk_sum = gv_sum = None
        for b in range(width // step):
            here = pl.ds(pl.multiple_of(start + b * step, 16), step)
            qb = qs[here, :]
            hb = hs[here, :]
            lane = lax.broadcasted_iota(jnp.int32, (1, step), 1) + b * step
            pieces = []
            for n in range(step // TOK):
                line = first + b * (step // TOK) + n
                two = jnp.concatenate([ds_[pl.ds(line, 1), :], ds_[pl.ds(line + 1, 1), :]], axis=1)
                pieces.append(pltpu.roll(two, 2 * TOK - shift, 1)[:, :TOK])
            delta = pieces[0] if len(pieces) == 1 else jnp.concatenate(pieces, axis=1)
            s = nt(kw, qb) * to_two + bias
            top = jnp.max(s, axis=0, keepdims=True)
            e = jnp.exp2(s - top)
            norm = jnp.where(lane < size, 1.0 / jnp.sum(e, axis=0, keepdims=True), 0.0)
            p = e * norm
            dp = nt(vw, hb)
            dsc = (p * (dp - delta)).astype(BF)
            pk = nn(dsc, qb)
            pv = nn(p.astype(BF), hb)
            gk_sum = pk if gk_sum is None else gk_sum + pk
            gv_sum = pv if gv_sum is None else gv_sum + pv
            gq[here, :] = (tn(dsc, kw) * scaling).astype(BF)
        gk[pl.ds(start, width), :] = (gk_sum * scaling).astype(BF)
        gv[pl.ds(start, width), :] = gv_sum.astype(BF)

    def one(j, start):
        size = units[j] * 16
        start = pl.multiple_of(start, 16)
        for width, step in ((128, 128), (256, 256), (384, 384), (512, 256)):
            pl.when((size > width - 128) & (size <= width))(lambda width=width, step=step: image(start, size, width, step))
        return start + size

    lax.fori_loop(0, SEGS, one, jnp.int32(0))
    for i in range(16):
        rows = pl.ds(i * TOK, TOK)
        out[i, 0] = gq[rows, :]
        out[i, 1] = gk[rows, :]
        out[i, 2] = gv[rows, :]


def attention(xi, units, qkv, hs):
    vm = pl.BlockSpec(memory_space=pltpu.VMEM)
    sm = pl.BlockSpec(memory_space=pltpu.SMEM)
    return pl.pallas_call(
        attention_kernel,
        out_shape=jax.ShapeDtypeStruct((16, 3, TOK, HEAD), BF),
        in_specs=[sm, sm] + [vm] * 5,
        out_specs=vm,
        scratch_shapes=[pltpu.VMEM((PACK + IMG, HEAD), BF)] * 4 + [pltpu.VMEM((24, HEAD), F32)] + [pltpu.VMEM((PACK + IMG, HEAD), BF)] * 3,
        compiler_params=pltpu.CompilerParams(vmem_limit_bytes=40 * 1024 * 1024),
        cost_estimate=pl.CostEstimate(flops=2 * 5 * 128 * 900000, bytes_accessed=4 * 1024 * 1024, transcendentals=900000),
        name="attention",
    )(xi, units, qkv, *hs)


def pack_kernel(q, k, v, out):
    for i in range(16):
        cols = pl.ds(i * HEAD, HEAD)
        out[i, 0] = q[:, cols]
        out[i, 1] = k[:, cols]
        out[i, 2] = v[:, cols]


def pack(q, k, v):
    vm = pl.BlockSpec(memory_space=pltpu.VMEM)
    return pl.pallas_call(
        pack_kernel,
        out_shape=jax.ShapeDtypeStruct((16, 3, TOK, HEAD), BF),
        in_specs=[vm] * 3,
        out_specs=vm,
        cost_estimate=pl.CostEstimate(flops=0, bytes_accessed=3 * 1024 * 1024, transcendentals=0),
        name="pack",
    )(q, k, v)


def unpack_kernel(grads, q, k, v):
    for i in range(16):
        cols = pl.ds(i * HEAD, HEAD)
        q[:, cols] = grads[i, 0]
        k[:, cols] = grads[i, 1]
        v[:, cols] = grads[i, 2]


def unpack(grads):
    vm = pl.BlockSpec(memory_space=pltpu.VMEM)
    return pl.pallas_call(
        unpack_kernel,
        out_shape=[jax.ShapeDtypeStruct((TOK, 16 * HEAD), BF)] * 3,
        in_specs=[vm],
        out_specs=[vm] * 3,
        cost_estimate=pl.CostEstimate(flops=0, bytes_accessed=3 * 1024 * 1024, transcendentals=0),
        name="unpack",
    )(grads)


def three_terms(value):
    high = value.astype(BF)
    rest = value - high.astype(F32)
    middle = rest.astype(BF)
    return jnp.concatenate([high, middle, (rest - middle.astype(F32)).astype(BF), jnp.zeros_like(high)], axis=0)


def on_device(queries, keys_in, values_in, saved_out, out_grad, out_weight, image_units):
    seq = lax.axis_index("seq")
    dp = lax.axis_index("dp")
    x, y, core = seq // 4, seq % 4, dp % 2
    g = out_grad[0]

    o_sent = saved_out[0].reshape(TOK, 4, 4, HEAD).transpose(2, 0, 1, 3).reshape(4, TOK, 4 * HEAD)
    o_rows = lax.all_to_all(o_sent, "seq", split_axis=0, concat_axis=0, tiled=True, axis_index_groups=YGROUPS)

    g_back = lax.ppermute(g, "seq", YS[1])
    g_next = lax.ppermute(g, "seq", YS[3])
    w_parts = [out_weight] + [lax.ppermute(out_weight, "seq", XS[k]) for k in (1, 2, 3)]
    g_far = jnp.concatenate([lax.ppermute(g_back[:64], "seq", YS[1]), lax.ppermute(g_next[64:], "seq", YS[3])], axis=0)
    g_rows = lax.dynamic_slice_in_dim(
        jnp.concatenate([g, g_next, g_far, g_back, g, g_next, g_far], axis=0), lax.rem(4 - y, 4) * TOK, 4 * TOK, 0
    )
    w_rows = jnp.concatenate(w_parts, axis=0)
    head = nt(g_rows, w_rows).astype(BF)
    o_flat = o_rows.reshape(4 * TOK, 4, HEAD)

    h_parts = []
    for k in range(4):
        hk = head[:, k * HEAD : (k + 1) * HEAD]
        ok = lax.dynamic_index_in_dim(o_flat, lax.rem(x + 4 - k, 4), 1, keepdims=False)
        delta = jnp.sum(hk.astype(F32) * ok.astype(F32), axis=1).reshape(4, TOK)
        hk = jnp.concatenate([hk, three_terms(delta)], axis=0)
        h_parts.append(lax.ppermute(hk, "seq", XS[4 - k]) if k else hk)

    qkv = lax.all_to_all(
        pack(queries[0], keys_in[0], values_in[0]), "seq", split_axis=0, concat_axis=0, tiled=True
    )
    grads = attention(x.astype(jnp.int32)[None], image_units[0], qkv, h_parts)
    back = lax.all_to_all(grads, "seq", split_axis=0, concat_axis=0, tiled=True)
    query_grad, key_grad, value_grad = unpack(back)

    term = tn(g_rows, o_rows.reshape(4 * TOK, 4 * HEAD)).astype(BF).reshape(8, 2, 200, 4 * HEAD)
    mine = lax.dynamic_index_in_dim(term, core, 1, keepdims=False)
    other = lax.ppermute(lax.dynamic_index_in_dim(term, 1 - core, 1, keepdims=False), "dp", CORES)
    both = (mine.astype(F32) + other.astype(F32)).astype(BF).reshape(1600, 4 * HEAD)
    summed = lax.psum_scatter(both, "dp", scatter_dimension=0, tiled=True, axis_index_groups=ZGROUPS)
    blocks = summed.astype(F32).reshape(200, 4, HEAD)
    weight = lax.dynamic_index_in_dim(blocks, x, 1, keepdims=False)
    for k in (1, 2, 3):
        weight = weight + lax.ppermute(
            lax.dynamic_index_in_dim(blocks, lax.rem(x + k, 4), 1, keepdims=False), "seq", XS[k]
        )
    weight_grad = weight.T * (1.0 / math.sqrt(PACK * 16))
    return query_grad[None], key_grad[None], value_grad[None], weight_grad


def solution(mesh):
    rows = P("dp", "seq", None)
    return jax.shard_map(
        on_device,
        mesh=mesh,
        in_specs=(rows, rows, rows, rows, rows, P("seq", None), P("dp", None)),
        out_specs=(rows, rows, rows, P("seq", "dp")),
        check_vma=False,
    )
```

time: 338 us -> 177 us (0.52)
  blocking collectives: 73 us -> 0 us
  matrix products: 60.6 us -> 8.63 us
  waiting for transfers between devices: 106 us -> 76 us
  Pallas kernels: 0 us -> 13.7 us
  local copies, waits for them, and re-layouts: 30.1 us -> 21 us
  starting transfers between devices: 42.6 us -> 35.6 us
  other arithmetic: 7.86 us -> 4.18 us
    unnamed x1 -> x0, blocking collectives: 58.7 us -> none
    dot_general x22 -> x2, matrix products: 60.6 us -> 8.63 us  [the longest x1 4.81 us: nt(): lax.dot_general(a, b, (((1,), (1,)), ((), ())), preferred_element_type=F32)]
    all_gather x1 -> x0, waiting for transfers between devices: 44.7 us -> none  [on_device(): lax.all_gather(out_weight, 'seq', axis=0, tiled=True)]
    ppermute x0 -> x14, waiting for transfers between devices: none -> 42.4 us  [the longest x3 27.9 us: on_device(): lax.ppermute(out_weight, 'seq', XS[k])]
    all_to_all x7 -> x3, waiting for transfers between devices: 60.5 us -> 18.8 us  [the longest x1 18 us: on_device(): lax.all_to_all(o_sent, 'seq', split_axis=0, concat_axis=0, tiled=True, ax...]
    all_to_all x7 -> x3, starting transfers between devices: 42.6 us -> 15.4 us  [the longest x1 5.88 us: on_device(): back = lax.all_to_all(grads, 'seq', split_axis=0, concat_axis=0, tiled=True)]
    ppermute x0 -> x14, starting transfers between devices: none -> 20 us  [the longest x3 4.88 us: on_device(): lax.ppermute(lax.dynamic_index_in_dim(blocks, lax.rem(x + k, 4), 1, keepd...]
    reduce_scatter x1, waiting for transfers between devices: 0.01 us -> 14.8 us  [on_device(): lax.psum_scatter(both, 'dp', scatter_dimension=0, tiled=True, axis_index_...]
  transfers between devices with their start and end apart: 9 -> 18, of which waited for: 7 -> 10; matrix products, arithmetic and copies ran while one was open for 26% -> 11% of each run, Pallas kernels for 0% -> 8%
where the time goes in v1:
time: 177 us; the launch traced here: 173 us
  waiting for transfers between devices  76 us (43%)
  starting transfers between devices  35.6 us (20%)
  local copies, waits for them, and re-layouts  21 us (12%)
  between operations  14.3 us (8%)
  Pallas kernels  13.7 us (8%)
  matrix products  8.63 us (5%)
  other arithmetic  4.18 us (2%)
    ppermute x3, waiting for transfers between devices, on_device(): lax.ppermute(out_weight, 'seq', XS[k])  27.9 us
    all_to_all x1, waiting for transfers between devices, on_device(): lax.all_to_all(o_sent, 'seq', split_axis=0, concat_axis=0, tiled=True, ax...  18 us
    reduce_scatter x1, waiting for transfers between devices, on_device(): lax.psum_scatter(both, 'dp', scatter_dimension=0, tiled=True, axis_index_...  14.8 us
    unnamed x19, local copies, waits for them, and re-layouts  13.7 us
    ppermute x3, waiting for transfers between devices, on_device(): h_parts.append(lax.ppermute(hk, 'seq', XS[4 - k]) if k else hk)  8.87 us
    pallas_call x1, Pallas kernels, attention(): pl.pallas_call(attention_kernel, out_shape=jax.ShapeDtypeStruct((16, 3, T...  7.89 us
    all_to_all x1, starting transfers between devices, on_device(): back = lax.all_to_all(grads, 'seq', split_axis=0, concat_axis=0, tiled=True)  5.88 us
    ppermute x1, waiting for transfers between devices, on_device(): lax.ppermute(g_back[:64], 'seq', YS[1])  5.54 us
  transfers between devices with their start and end apart: 18, of which 10 were waited for; matrix products, arithmetic and copies ran while one was open for 11% of the time, Pallas kernels for 8%

profile of v1, /device:TPU:2, one launch (start us, length us, event | category | flops | bytes accessed | tf_op | source)
XLA Modules:
  0.0 173.4 jit_solution(12783788201233632979)
XLA Ops:
  7.2 3.1 %collective-permute-start = (bf16[128,3200]{1,0:T(8,128)(2,1)}, bf16[128,3200]{1,0:T(8,128)(2,1)S(1)}, u32[]{:S(2)}, u32[]{:S(2)}) collective-permute-start(bf16[128,3200]{1,0:T(8,128)(2,1)} %bitcast.104), channel_id=1, source_target_pairs={{0,3},{1,0},{2,1},{3,2},{4,7},{5,4},{6,5},{7,6},{8,11},{9,8},{10,9... | collective-permute-start | bytes 2457608 | tf_op jit(solution)/shard_map/ppermute | solution.py:177
  12.4 4.5 %all-to-all-start.1 = ((bf16[4,128,512]{1,2,0:T(8,128)(2,1)}), bf16[4,128,512]{1,2,0:T(8,128)(2,1)S(1)}, u32[]{:S(2)}, u32[]{:S(2)}) async-start(bf16[4,128,512]{1,2,0:T(8,128)(2,1)} %bitcast.8), calls=%async_computation.1 | async-start | bytes 1048576 | tf_op jit(solution)/shard_map/all_to_all | solution.py:174
  16.9 2.1 %constant_dynamic-update-slice_fusion.8 = bf16[896,3200]{1,0:T(8,128)(2,1)} fusion(bf16[1,128,3200]{2,1,0:T(8,128)(2,1)} %param.11), kind=kLoop, calls=%fused_computation.36 | loop fusion | bytes 1638400
  19.0 18.0 %all-to-all-done.1 = bf16[4,128,512]{1,2,0:T(8,128)(2,1)S(1)} async-done(((bf16[4,128,512]{1,2,0:T(8,128)(2,1)}), bf16[4,128,512]{1,2,0:T(8,128)(2,1)S(1)}, u32[]{:S(2)}, u32[]{:S(2)}) %all-to-all-start.1) | async-done | bytes 524320 | tf_op jit(solution)/shard_map/all_to_all | solution.py:174
  38.4 3.3 %collective-permute-start.3 = (bf16[64,3200]{1,0:T(8,128)(2,1)S(1)}, bf16[64,3200]{1,0:T(8,128)(2,1)S(1)}, u32[]{:S(2)}, u32[]{:S(2)}) collective-permute-start(bf16[64,3200]{1,0:T(8,128)(2,1)S(1)} %slice.25), channel_id=1, source_target_pairs={{0,3},{1,0},{2,1},{3,2},{4,7},{5,4},{6,5},{7,6},{8,11},{9,8},{10,9... | collective-permute-start | bytes 1228808 | tf_op jit(solution)/shard_map/ppermute | solution.py:179
  42.7 5.5 %collective-permute-done.2 = bf16[64,3200]{1,0:T(8,128)(2,1)S(1)} collective-permute-done((bf16[64,3200]{1,0:T(8,128)(2,1)S(1)}, bf16[64,3200]{1,0:T(8,128)(2,1)S(1)}, u32[]{:S(2)}, u32[]{:S(2)}) %collective-permute-start.2) | collective-permute-done | bytes 409632 | tf_op jit(solution)/shard_map/ppermute | solution.py:179
  49.9 2.1 %constant_dynamic-update-slice_fusion.4 = bf16[896,3200]{1,0:T(8,128)(2,1)} fusion(bf16[896,3200]{1,0:T(8,128)(2,1)} %constant_dynamic-update-slice_fusion.5, bf16[128,3200]{1,0:T(8,128)(2,1)} %collective-permute-done.1), kind=kLoop, calls=%fused_computation.32 | loop fusion | bytes 1638400
  55.5 3.8 %convolution_convert_fusion = bf16[3200,512]{1,0:T(8,128)(2,1)S(1)} fusion(bf16[512,512]{1,0:T(8,128)(2,1)S(1)} %bitcast.108, bf16[896,3200]{1,0:T(8,128)(2,1)} %constant_dynamic-update-slice_fusion, s32[]{:T(128)S(6)} %select_n.47), kind=kOutput, calls=%fused_computation | convolution fusion | flops 1679360000 | bytes 7077892 | tf_op jit(solution)/shard_map/dot_general | solution.py:35
  64.9 2.2 %collective-permute-start.6 = (bf16[128,3200]{1,0:T(8,128)(2,1)}, bf16[128,3200]{1,0:T(8,128)(2,1)}, u32[]{:S(2)}, u32[]{:S(2)}) collective-permute-start(bf16[128,3200]{1,0:T(8,128)(2,1)} %param.12), channel_id=1, source_target_pairs={{0,12},{1,13},{2,14},{3,15},{4,0},{5,1},{6,2},{7,3},{8,4},{9,5},{1... | collective-permute-start | bytes 2457608 | tf_op jit(solution)/shard_map/ppermute | solution.py:178
  67.1 2.8 %pack.1 = bf16[16,3,128,128]{3,2,1,0:T(8,128)(2,1)} custom-call(bf16[128,2048]{1,0:T(8,128)(2,1)} %bitcast.110, bf16[128,2048]{1,0:T(8,128)(2,1)} %bitcast.111, bf16[128,2048]{1,0:T(8,128)(2,1)} %bitcast.112), custom_call_target="tpu_custom_call" | custom-call | bytes 3145728 | tf_op jit(solution)/shard_map/pack/pallas_call | solution.py:130
  69.9 5.0 %all-to-all-start = ((bf16[16,3,128,128]{3,2,1,0:T(8,128)(2,1)}), bf16[16,3,128,128]{3,2,1,0:T(8,128)(2,1)S(1)}, u32[]{:S(2)}, u32[]{:S(2)}) async-start(bf16[16,3,128,128]{3,2,1,0:T(8,128)(2,1)} %pack.1), calls=%async_computation | async-start | bytes 3145728 | tf_op jit(solution)/shard_map/all_to_all | solution.py:195
  76.4 7.2 %collective-permute-done.4 = bf16[128,3200]{1,0:T(8,128)(2,1)} collective-permute-done((bf16[128,3200]{1,0:T(8,128)(2,1)}, bf16[128,3200]{1,0:T(8,128)(2,1)}, u32[]{:S(2)}, u32[]{:S(2)}) %collective-permute-start.4) | collective-permute-done | bytes 819232 | tf_op jit(solution)/shard_map/ppermute | solution.py:178
  83.7 3.1 %collective-permute-done.5 = bf16[128,3200]{1,0:T(8,128)(2,1)} collective-permute-done((bf16[128,3200]{1,0:T(8,128)(2,1)}, bf16[128,3200]{1,0:T(8,128)(2,1)}, u32[]{:S(2)}, u32[]{:S(2)}) %collective-permute-start.5) | collective-permute-done | bytes 819232 | tf_op jit(solution)/shard_map/ppermute | solution.py:178
  86.8 17.6 %collective-permute-done.6 = bf16[128,3200]{1,0:T(8,128)(2,1)} collective-permute-done((bf16[128,3200]{1,0:T(8,128)(2,1)}, bf16[128,3200]{1,0:T(8,128)(2,1)}, u32[]{:S(2)}, u32[]{:S(2)}) %collective-permute-start.6) | collective-permute-done | bytes 819232 | tf_op jit(solution)/shard_map/ppermute | solution.py:178
  104.4 4.8 %fusion.11 = bf16[512,512]{1,0:T(8,128)(2,1)S(1)} fusion(bf16[128,3200]{1,0:T(8,128)(2,1)} %collective-permute-done.6, bf16[128,3200]{1,0:T(8,128)(2,1)} %collective-permute-done.5, bf16[128,3200]{1,0:T(8,128)(2,1)} %collective-permute-done.4, bf16[128,3200]{1,0:T(8,128)(2,1)} %param.12, bf16[896,3200]{1,0:T(8,128)(2,1)} %constant_dynamic-update-slice_fusion, ...), kind=kOutput, calls=%fused_computation.14 | convolution fusion | flops 1691090944 | bytes 7077892 | tf_op jit(solution)/shard_map/dot_general | solution.py:27
  109.6 3.1 %fusion.8 = bf16[8,200,512]{2,1,0:T(8,128)(2,1)} fusion(bf16[8,200,512]{2,1,0:T(8,128)(2,1)} %collective-permute-done.10, bf16[8,2,200,512]{3,2,1,0:T(8,128)(2,1)S(1)} %bitcast.107, s32[]{:T(128)S(6)} %select_n.53), kind=kLoop, calls=%fused_computation.10 | loop fusion | flops 3276800 | bytes 4915204 | tf_op jit(solution)/shard_map/convert_element_type | solution.py:205
  115.0 2.1 %collective-permute-start.7 = (bf16[528,128]{1,0:T(8,128)(2,1)S(1)}, bf16[528,128]{1,0:T(8,128)(2,1)S(1)}, u32[]{:S(2)}, u32[]{:S(2)}) collective-permute-start(bf16[528,128]{1,0:T(8,128)(2,1)S(1)} %concatenate.23), channel_id=1, source_target_pairs={{0,12},{1,13},{2,14},{3,15},{4,0},{5,1},{6,2},{7,3},{8,4},{9,5},{1... | collective-permute-start | bytes 405512 | tf_op jit(solution)/shard_map/ppermute | solution.py:193
  117.2 6.2 %collective-permute-done.9.h3 = bf16[528,128]{1,0:T(8,128)(2,1)S(1)} collective-permute-done((bf16[528,128]{1,0:T(8,128)(2,1)S(1)}, bf16[528,128]{1,0:T(8,128)(2,1)S(1)}, u32[]{:S(2)}, u32[]{:S(2)}) %collective-permute-start.9) | collective-permute-done | bytes 135200 | tf_op jit(solution)/shard_map/ppermute | solution.py:193
  123.4 1.8 %collective-permute-done.8.h2 = bf16[528,128]{1,0:T(8,128)(2,1)S(1)} collective-permute-done((bf16[528,128]{1,0:T(8,128)(2,1)S(1)}, bf16[528,128]{1,0:T(8,128)(2,1)S(1)}, u32[]{:S(2)}, u32[]{:S(2)}) %collective-permute-start.8) | collective-permute-done | bytes 135200 | tf_op jit(solution)/shard_map/ppermute | solution.py:193
  126.0 7.9 %attention.1 = bf16[16,3,128,128]{3,2,1,0:T(8,128)(2,1)} custom-call(s32[1]{0:T(128)} %bitcast.xi, s32[8]{0:T(128)S(1)} %bitcast.102, bf16[16,3,128,128]{3,2,1,0:T(8,128)(2,1)S(1)} %all-to-all-done.qkv, bf16[528,128]{1,0:T(8,128)(2,1)S(1)} %concatenate.22.h0, bf16[528,128]{1,0:T(8,128)(2,1)S(1)} %collective-permute-done.7.h1, ...), custom_call_target="tpu_custom_call" | custom-call | flops 1152000000 | bytes 4194304 | tf_op jit(solution)/shard_map/attention/pallas_call | solution.py:108
  133.9 5.9 %all-to-all-start.2 = ((bf16[16,3,128,128]{3,2,1,0:T(8,128)(2,1)}), bf16[16,3,128,128]{3,2,1,0:T(8,128)(2,1)S(1)}, u32[]{:S(2)}, u32[]{:S(2)}) async-start(bf16[16,3,128,128]{3,2,1,0:T(8,128)(2,1)} %attention.1), calls=%async_computation.2 | async-start | bytes 3145728 | tf_op jit(solution)/shard_map/all_to_all | solution.py:199
  139.8 14.8 %reduce-scatter.2.cloned.1.call-done = bf16[200,512]{1,0:T(8,128)(2,1)} async-done(((bf16[1600,512]{1,0:T(8,128)(2,1)}), bf16[200,512]{1,0:T(8,128)(2,1)}) %reduce-scatter.2.cloned.1.call-update) | async-done | bytes 204816 | tf_op jit(solution)/shard_map/reduce_scatter | solution.py:206
  158.7 2.2 %collective-permute-start.13 = (f32[200,128]{1,0:T(8,128)S(1)}, f32[200,128]{1,0:T(8,128)S(1)}, u32[]{:S(2)}, u32[]{:S(2)}) collective-permute-start(f32[200,128]{1,0:T(8,128)S(1)} %bitcast.114), channel_id=1, source_target_pairs={{0,12},{1,13},{2,14},{3,15},{4,0},{5,1},{6,2},{7,3},{8,4},{9,5},{1... | collective-permute-start | bytes 307208 | tf_op jit(solution)/shard_map/ppermute | solution.py:210
  162.9 3.0 %unpack.1 = (bf16[128,2048]{1,0:T(8,128)(2,1)}, bf16[128,2048]{1,0:T(8,128)(2,1)}, bf16[128,2048]{1,0:T(8,128)(2,1)}) custom-call(bf16[16,3,128,128]{3,2,1,0:T(8,128)(2,1)} %copy-done.1), custom_call_target="tpu_custom_call" | custom-call | bytes 3145728 | tf_op jit(solution)/shard_map/unpack/pallas_call | solution.py:150
  (64 shorter events, 27.0 us)
Async XLA Ops:
  7.2 31.2 %collective-permute-start = (bf16[128,3200]{1,0:T(8,128)(2,1)}, bf16[128,3200]{1,0:T(8,128)(2,1)S(1)}, u32[]{:S(2)}, u32[]{:S(2)}) collective-permute-start(bf16[128,3200]{1,0:T(8,128)(2,1)} %bitcast.104), channel_id=1, source_target_pairs={{0,3},{1,0},{2,1},{3,2},{4,7},{5,4},{6,5},{7,6},{8,11},{9,8},{10,9... | collective-permute-start | bytes 2457608 | tf_op jit(solution)/shard_map/ppermute | solution.py:177
  10.3 27.0 %collective-permute-start.1 = (bf16[128,3200]{1,0:T(8,128)(2,1)}, bf16[128,3200]{1,0:T(8,128)(2,1)}, u32[]{:S(2)}, u32[]{:S(2)}) collective-permute-start(bf16[128,3200]{1,0:T(8,128)(2,1)} %bitcast.105), channel_id=1, source_target_pairs={{0,1},{1,2},{2,3},{3,0},{4,5},{5,6},{6,7},{7,4},{8,9},{9,10},{10,1... | collective-permute-start | bytes 2457608 | tf_op jit(solution)/shard_map/ppermute | solution.py:176
  11.6 40.4 %copy-start.2 = (bf16[1,128,3200]{2,1,0:T(8,128)(2,1)S(1)}, bf16[1,128,3200]{2,1,0:T(8,128)(2,1)}, u32[]{:S(2)}) copy-start(bf16[1,128,3200]{2,1,0:T(8,128)(2,1)} %param.11) | copy-start | bytes 2457604
  12.4 24.6 %all-to-all-start.1 = ((bf16[4,128,512]{1,2,0:T(8,128)(2,1)}), bf16[4,128,512]{1,2,0:T(8,128)(2,1)S(1)}, u32[]{:S(2)}, u32[]{:S(2)}) async-start(bf16[4,128,512]{1,2,0:T(8,128)(2,1)} %bitcast.8), calls=%async_computation.1 | async-start | bytes 1048576 | tf_op jit(solution)/shard_map/all_to_all | solution.py:174
  38.3 10.0 %collective-permute-start.2 = (bf16[64,3200]{1,0:T(8,128)(2,1)S(1)}, bf16[64,3200]{1,0:T(8,128)(2,1)S(1)}, u32[]{:S(2)}, u32[]{:S(2)}) collective-permute-start(bf16[64,3200]{1,0:T(8,128)(2,1)S(1)} %slice.24), channel_id=1, source_target_pairs={{0,1},{1,2},{2,3},{3,0},{4,5},{5,6},{6,7},{7,4},{8,9},{9,10},{10,1... | collective-permute-start | bytes 1228808 | tf_op jit(solution)/shard_map/ppermute | solution.py:179
  38.4 10.7 %collective-permute-start.3 = (bf16[64,3200]{1,0:T(8,128)(2,1)S(1)}, bf16[64,3200]{1,0:T(8,128)(2,1)S(1)}, u32[]{:S(2)}, u32[]{:S(2)}) collective-permute-start(bf16[64,3200]{1,0:T(8,128)(2,1)S(1)} %slice.25), channel_id=1, source_target_pairs={{0,3},{1,0},{2,1},{3,2},{4,7},{5,4},{6,5},{7,6},{8,11},{9,8},{10,9... | collective-permute-start | bytes 1228808 | tf_op jit(solution)/shard_map/ppermute | solution.py:179
  59.3 1.7 copy-start.3
  62.3 47.3 %collective-permute-start.10 = (bf16[8,200,512]{2,1,0:T(8,128)(2,1)}, bf16[8,200,512]{2,1,0:T(8,128)(2,1)}, u32[]{:S(2)}, u32[]{:S(2)}) collective-permute-start(bf16[8,200,512]{2,1,0:T(8,128)(2,1)} %dynamic-slice_bitcast_fusion), channel_id=1, source_target_pairs={{0,16},{16,0},{32,48},{48,32},{64,80},{80,64},{96,112},{112,96},{1... | collective-permute-start | bytes 4915208 | tf_op jit(solution)/shard_map/ppermute | solution.py:204
  62.3 21.4 %collective-permute-start.4 = (bf16[128,3200]{1,0:T(8,128)(2,1)}, bf16[128,3200]{1,0:T(8,128)(2,1)}, u32[]{:S(2)}, u32[]{:S(2)}) collective-permute-start(bf16[128,3200]{1,0:T(8,128)(2,1)} %param.12), channel_id=1, source_target_pairs={{0,4},{1,5},{2,6},{3,7},{4,8},{5,9},{6,10},{7,11},{8,12},{9,13},{1... | collective-permute-start | bytes 2457608 | tf_op jit(solution)/shard_map/ppermute | solution.py:178
  63.8 22.9 %collective-permute-start.5 = (bf16[128,3200]{1,0:T(8,128)(2,1)}, bf16[128,3200]{1,0:T(8,128)(2,1)}, u32[]{:S(2)}, u32[]{:S(2)}) collective-permute-start(bf16[128,3200]{1,0:T(8,128)(2,1)} %param.12), channel_id=1, source_target_pairs={{0,8},{1,9},{2,10},{3,11},{4,12},{5,13},{6,14},{7,15},{8,0},{9,1},... | collective-permute-start | bytes 2457608 | tf_op jit(solution)/shard_map/ppermute | solution.py:178
  64.9 39.4 %collective-permute-start.6 = (bf16[128,3200]{1,0:T(8,128)(2,1)}, bf16[128,3200]{1,0:T(8,128)(2,1)}, u32[]{:S(2)}, u32[]{:S(2)}) collective-permute-start(bf16[128,3200]{1,0:T(8,128)(2,1)} %param.12), channel_id=1, source_target_pairs={{0,12},{1,13},{2,14},{3,15},{4,0},{5,1},{6,2},{7,3},{8,4},{9,5},{1... | collective-permute-start | bytes 2457608 | tf_op jit(solution)/shard_map/ppermute | solution.py:178
  69.9 56.1 %all-to-all-start = ((bf16[16,3,128,128]{3,2,1,0:T(8,128)(2,1)}), bf16[16,3,128,128]{3,2,1,0:T(8,128)(2,1)S(1)}, u32[]{:S(2)}, u32[]{:S(2)}) async-start(bf16[16,3,128,128]{3,2,1,0:T(8,128)(2,1)} %pack.1), calls=%async_computation | async-start | bytes 3145728 | tf_op jit(solution)/shard_map/all_to_all | solution.py:195
  74.9 79.7 %reduce-scatter.2.cloned.1.call-start = ((), (), s32[]{:S(2)}) async-start(), calls=%async_computation.4 | async-start | bytes 1843200 | tf_op jit(solution)/shard_map/reduce_scatter | solution.py:206
  76.4 33.2 %copy-start.4 = (bf16[3200,512]{1,0:T(8,128)(2,1)S(1)}, bf16[3200,512]{1,0:T(8,128)(2,1)}, u32[]{:S(2)}) copy-start(bf16[3200,512]{1,0:T(8,128)(2,1)} %copy-done.3) | copy-start | bytes 9830404
  109.2 16.8 %copy-start = (s32[1,8]{1,0:T(1,128)S(1)}, s32[1,8]{1,0:T(1,128)}, u32[]{:S(2)}) copy-start(s32[1,8]{1,0:T(1,128)} %param.13) | copy-start | bytes 100
  112.9 10.4 %collective-permute-start.9 = (bf16[528,128]{1,0:T(8,128)(2,1)S(1)}, bf16[528,128]{1,0:T(8,128)(2,1)S(1)}, u32[]{:S(2)}, u32[]{:S(2)}) collective-permute-start(bf16[528,128]{1,0:T(8,128)(2,1)S(1)} %concatenate.25), channel_id=1, source_target_pairs={{0,4},{1,5},{2,6},{3,7},{4,8},{5,9},{6,10},{7,11},{8,12},{9,13},{1... | collective-permute-start | bytes 405512 | tf_op jit(solution)/shard_map/ppermute | solution.py:193
  113.6 11.6 %collective-permute-start.8 = (bf16[528,128]{1,0:T(8,128)(2,1)S(1)}, bf16[528,128]{1,0:T(8,128)(2,1)S(1)}, u32[]{:S(2)}, u32[]{:S(2)}) collective-permute-start(bf16[528,128]{1,0:T(8,128)(2,1)S(1)} %concatenate.24), channel_id=1, source_target_pairs={{0,8},{1,9},{2,10},{3,11},{4,12},{5,13},{6,14},{7,15},{8,0},{9,1},... | collective-permute-start | bytes 405512 | tf_op jit(solution)/shard_map/ppermute | solution.py:193
  115.0 11.1 %collective-permute-start.7 = (bf16[528,128]{1,0:T(8,128)(2,1)S(1)}, bf16[528,128]{1,0:T(8,128)(2,1)S(1)}, u32[]{:S(2)}, u32[]{:S(2)}) collective-permute-start(bf16[528,128]{1,0:T(8,128)(2,1)S(1)} %concatenate.23), channel_id=1, source_target_pairs={{0,12},{1,13},{2,14},{3,15},{4,0},{5,1},{6,2},{7,3},{8,4},{9,5},{1... | collective-permute-start | bytes 405512 | tf_op jit(solution)/shard_map/ppermute | solution.py:193
  133.9 27.8 %all-to-all-start.2 = ((bf16[16,3,128,128]{3,2,1,0:T(8,128)(2,1)}), bf16[16,3,128,128]{3,2,1,0:T(8,128)(2,1)S(1)}, u32[]{:S(2)}, u32[]{:S(2)}) async-start(bf16[16,3,128,128]{3,2,1,0:T(8,128)(2,1)} %attention.1), calls=%async_computation.2 | async-start | bytes 3145728 | tf_op jit(solution)/shard_map/all_to_all | solution.py:199
  156.0 9.8 %collective-permute-start.11 = (f32[200,128]{1,0:T(8,128)S(1)}, f32[200,128]{1,0:T(8,128)S(1)}, u32[]{:S(2)}, u32[]{:S(2)}) collective-permute-start(f32[200,128]{1,0:T(8,128)S(1)} %bitcast.116), channel_id=1, source_target_pairs={{0,4},{1,5},{2,6},{3,7},{4,8},{5,9},{6,10},{7,11},{8,12},{9,13},{1... | collective-permute-start | bytes 307208 | tf_op jit(solution)/shard_map/ppermute | solution.py:210
  157.6 8.3 %collective-permute-start.12 = (f32[200,128]{1,0:T(8,128)S(1)}, f32[200,128]{1,0:T(8,128)S(1)}, u32[]{:S(2)}, u32[]{:S(2)}) collective-permute-start(f32[200,128]{1,0:T(8,128)S(1)} %bitcast.115), channel_id=1, source_target_pairs={{0,8},{1,9},{2,10},{3,11},{4,12},{5,13},{6,14},{7,15},{8,0},{9,1},... | collective-permute-start | bytes 307208 | tf_op jit(solution)/shard_map/ppermute | solution.py:210
  158.7 7.2 %collective-permute-start.13 = (f32[200,128]{1,0:T(8,128)S(1)}, f32[200,128]{1,0:T(8,128)S(1)}, u32[]{:S(2)}, u32[]{:S(2)}) collective-permute-start(f32[200,128]{1,0:T(8,128)S(1)} %bitcast.114), channel_id=1, source_target_pairs={{0,12},{1,13},{2,14},{3,15},{4,0},{5,1},{6,2},{7,3},{8,4},{9,5},{1... | collective-permute-start | bytes 307208 | tf_op jit(solution)/shard_map/ppermute | solution.py:210
  161.7 1.2 copy-start.1
Sparse Core Ops, SparseCore 0:
  112.8 41.6 reduce-scatter.1

commit v2 on v1

--- a/solution.py
+++ b/solution.py
@@ -20,7 +20,14 @@
 YS = [[(4 * x + y, 4 * x + (y + k) % 4) for x in range(4) for y in range(4)] for k in range(4)]
 YGROUPS = [[4 * x + y for y in range(4)] for x in range(4)]
 CORES = [(i, i ^ 1) for i in range(16)]
-ZGROUPS = [[2 * z + c for z in range(8)] for c in range(2)]
+ZS = [[(2 * z + c, 2 * (z ^ b) + c) for z in range(8) for c in range(2)] for b in (1, 2, 4)]
+BOTH = [
+    (16 * d + 4 * x + y, 16 * d + 4 * ((x + (1, 3)[d % 2]) % 4) + y)
+    for d in range(16)
+    for x in range(4)
+    for y in range(4)
+]
+CHUNK = 640
 
 
 def nt(a, b):
@@ -112,7 +119,7 @@
         out_specs=vm,
         scratch_shapes=[pltpu.VMEM((PACK + IMG, HEAD), BF)] * 4 + [pltpu.VMEM((24, HEAD), F32)] + [pltpu.VMEM((PACK + IMG, HEAD), BF)] * 3,
         compiler_params=pltpu.CompilerParams(vmem_limit_bytes=40 * 1024 * 1024),
-        cost_estimate=pl.CostEstimate(flops=2 * 5 * 128 * 900000, bytes_accessed=4 * 1024 * 1024, transcendentals=900000),
+        cost_estimate=pl.CostEstimate(flops=10350000000, bytes_accessed=32400000, transcendentals=0),
         name="attention",
     )(xi, units, qkv, *hs)
 
@@ -132,7 +139,7 @@
         out_shape=jax.ShapeDtypeStruct((16, 3, TOK, HEAD), BF),
         in_specs=[vm] * 3,
         out_specs=vm,
-        cost_estimate=pl.CostEstimate(flops=0, bytes_accessed=3 * 1024 * 1024, transcendentals=0),
+        cost_estimate=pl.CostEstimate(flops=1, bytes_accessed=1, transcendentals=0),
         name="pack",
     )(q, k, v)
 
@@ -152,7 +159,7 @@
         out_shape=[jax.ShapeDtypeStruct((TOK, 16 * HEAD), BF)] * 3,
         in_specs=[vm],
         out_specs=[vm] * 3,
-        cost_estimate=pl.CostEstimate(flops=0, bytes_accessed=3 * 1024 * 1024, transcendentals=0),
+        cost_estimate=pl.CostEstimate(flops=1, bytes_accessed=1, transcendentals=0),
         name="unpack",
     )(grads)
 
@@ -164,53 +171,243 @@
     return jnp.concatenate([high, middle, (rest - middle.astype(F32)).astype(BF), jnp.zeros_like(high)], axis=0)
 
 
+def pack_out_kernel(o, out):
+    for y in range(4):
+        for x in range(4):
+            out[y, :, pl.ds(x * HEAD, HEAD)] = o[:, pl.ds((4 * x + y) * HEAD, HEAD)]
+
+
+def pack_out(o):
+    vm = pl.BlockSpec(memory_space=pltpu.VMEM)
+    return pl.pallas_call(
+        pack_out_kernel,
+        out_shape=jax.ShapeDtypeStruct((4, TOK, 4 * HEAD), BF),
+        in_specs=[vm],
+        out_specs=vm,
+        cost_estimate=pl.CostEstimate(flops=1, bytes_accessed=1, transcendentals=0),
+        name="pack_out",
+    )(o)
+
+
+def chunk_copies(pieces, whole, sems, c):
+    cols = pl.ds(c * CHUNK, CHUNK)
+    copies = []
+    for n, (ref, row) in enumerate(pieces):
+        rows = ref.shape[0]
+        copies.append(
+            pltpu.make_async_copy(
+                ref.at[:, cols], whole.at[pl.ds(pl.multiple_of(row, 64), rows), cols], sems.at[c, n]
+            )
+        )
+    return copies
+
+
+def grad_pieces(y, g, back, ahead, fa, fb):
+    far = lax.rem(y + 2, 4) * TOK
+    return [(g, y * TOK), (back, lax.rem(y + 3, 4) * TOK), (ahead, lax.rem(y + 1, 4) * TOK), (fa, far), (fb, far + 64)]
+
+
+def head_kernel(at, *refs):
+    g, (w, wa, wb, wc, wd, o), hs, (gs, ws, acc, gsem, wsem) = refs[:5], refs[5:11], refs[11:15], refs[15:]
+    x, y, core = at[0], at[1], at[2]
+    g_pieces = grad_pieces(y, *g)
+    near = lax.select(core == 0, 1, 3)
+    w_pieces = [
+        (w, 0),
+        (wa, near * TOK),
+        (wb, (4 - near) * TOK),
+        (wc, 2 * TOK + 64 * core),
+        (wd, 2 * TOK + 64 * (1 - core)),
+    ]
+    copies = [chunk_copies(w_pieces, ws, wsem, c) + chunk_copies(g_pieces, gs, gsem, c) for c in range(MODEL // CHUNK)]
+    for group in copies:
+        for copy in group:
+            copy.start()
+    for c, group in enumerate(copies):
+        for copy in group:
+            copy.wait()
+        cols = pl.ds(c * CHUNK, CHUNK)
+        part = nt(gs[:, cols], ws[:, cols])
+        if c == 0:
+            acc[...] = part
+        else:
+            acc[...] += part
+    for k in range(4):
+        own = pl.ds(pl.multiple_of(lax.rem(x + 4 - k, 4) * HEAD, HEAD), HEAD)
+        lines = []
+        for j in range(4):
+            rows = pl.ds(j * TOK, TOK)
+            h = acc[rows, pl.ds(k * HEAD, HEAD)].astype(BF)
+            hs[k][rows, :] = h
+            product = h.astype(F32) * o[j, :, own].astype(F32)
+            lines.append(jnp.sum(product.T, axis=0, keepdims=True))
+        hs[k][pl.ds(4 * TOK, 16), :] = three_terms(jnp.concatenate(lines, axis=0))
+
+
+def head_blocks(at, g, w, o):
+    vm = pl.BlockSpec(memory_space=pltpu.VMEM)
+    sm = pl.BlockSpec(memory_space=pltpu.SMEM)
+    hbm = pl.BlockSpec(memory_space=pl.ANY)
+    return pl.pallas_call(
+        head_kernel,
+        out_shape=[jax.ShapeDtypeStruct((4 * TOK + 16, HEAD), BF)] * 4,
+        in_specs=[sm] + [hbm] * 10 + [vm],
+        out_specs=[vm] * 4,
+        scratch_shapes=[
+            pltpu.VMEM((4 * TOK, MODEL), BF),
+            pltpu.VMEM((4 * HEAD, MODEL), BF),
+            pltpu.VMEM((4 * TOK, 4 * HEAD), F32),
+            pltpu.SemaphoreType.DMA((MODEL // CHUNK, 5)),
+            pltpu.SemaphoreType.DMA((MODEL // CHUNK, 5)),
+        ],
+        compiler_params=pltpu.CompilerParams(vmem_limit_bytes=40 * 1024 * 1024),
+        cost_estimate=pl.CostEstimate(flops=1, bytes_accessed=1, transcendentals=0),
+        name="head_blocks",
+    )(at, *g, *w, o)
+
+
+def term_kernel(at, *refs):
+    g, (o, mine, *other, gs, acc, gsem) = refs[:5], refs[5:]
+    y, core = at[1], at[2]
+    g_pieces = grad_pieces(y, *g)
+    copies = [chunk_copies(g_pieces, gs, gsem, c) for c in range(MODEL // CHUNK)]
+    for group in copies:
+        for copy in group:
+            copy.start()
+    outs = o[...].reshape(4 * TOK, 4 * HEAD)
+    for c, group in enumerate(copies):
+        for copy in group:
+            copy.wait()
+        acc[pl.ds(c * CHUNK, CHUNK), :] = tn(gs[:, pl.ds(c * CHUNK, CHUNK)], outs)
+    for z in range(8):
+        mine[z] = acc[pl.ds(pl.multiple_of(400 * z + 200 * core, 8), 200), :].astype(BF)
+        other[z // 2][z % 2] = acc[pl.ds(pl.multiple_of(400 * z + 200 - 200 * core, 8), 200), :].astype(BF)
+
+
+def weight_term(at, g, o):
+    vm = pl.BlockSpec(memory_space=pltpu.VMEM)
+    sm = pl.BlockSpec(memory_space=pltpu.SMEM)
+    hbm = pl.BlockSpec(memory_space=pl.ANY)
+    return pl.pallas_call(
+        term_kernel,
+        out_shape=[jax.ShapeDtypeStruct((n, 200, 4 * HEAD), BF) for n in (8, 2, 2, 2, 2)],
+        in_specs=[sm] + [hbm] * 5 + [vm],
+        out_specs=[vm] * 5,
+        scratch_shapes=[
+            pltpu.VMEM((4 * TOK, MODEL), BF),
+            pltpu.VMEM((MODEL, 4 * HEAD), F32),
+            pltpu.SemaphoreType.DMA((MODEL // CHUNK, 5)),
+        ],
+        compiler_params=pltpu.CompilerParams(vmem_limit_bytes=40 * 1024 * 1024),
+        cost_estimate=pl.CostEstimate(flops=1, bytes_accessed=1, transcendentals=0),
+        name="weight_term",
+    )(at, *g, o)
+
+
+def pair_kernel(at, mine, *refs):
+    other, outs = refs[:4], refs[4:]
+    for k in range(4):
+        cols = pl.ds(pl.multiple_of(lax.rem(at[0] + k, 4) * HEAD, HEAD), HEAD)
+        for z in range(8):
+            outs[k][z] = (mine[z, :, cols].astype(F32) + other[z // 2][z % 2, :, cols].astype(F32)).astype(BF)
+
+
+def pair_sum(at, mine, *other):
+    vm = pl.BlockSpec(memory_space=pltpu.VMEM)
+    sm = pl.BlockSpec(memory_space=pltpu.SMEM)
+    return pl.pallas_call(
+        pair_kernel,
+        out_shape=[jax.ShapeDtypeStruct((8, 200, HEAD), BF)] * 4,
+        in_specs=[sm] + [vm] * 5,
+        out_specs=[vm] * 4,
+        cost_estimate=pl.CostEstimate(flops=1, bytes_accessed=1, transcendentals=0),
+        name="pair_sum",
+    )(at, mine, *other)
+
+
+def row_kernel(at, a, b, c, d, kept, sent):
+    bit = lax.rem(at[3], 2)
+    for i in range(4):
+        own, away = 2 * i + bit, 2 * i + 1 - bit
+        kept[i] = a[own].astype(F32) + b[own].astype(F32) + c[own].astype(F32) + d[own].astype(F32)
+        sent[i] = (a[away].astype(F32) + b[away].astype(F32) + c[away].astype(F32) + d[away].astype(F32)).astype(BF)
+
+
+def half_kernel(shift, at, held, got, kept, sent):
+    bit = lax.rem(lax.div(at[3], shift), 2)
+    for i in range(held.shape[0] // 2):
+        own, away = 2 * i + bit, 2 * i + 1 - bit
+        kept[i] = held[own] + got[own].astype(F32)
+        sent[i] = (held[away] + got[away].astype(F32)).astype(BF)
+
+
+def halved(at, parts, shift, count):
+    vm = pl.BlockSpec(memory_space=pltpu.VMEM)
+    sm = pl.BlockSpec(memory_space=pltpu.SMEM)
+    body = row_kernel if shift == 1 else lambda *refs: half_kernel(shift, *refs)
+    return pl.pallas_call(
+        body,
+        out_shape=[jax.ShapeDtypeStruct((count, 200, HEAD), F32), jax.ShapeDtypeStruct((count, 200, HEAD), BF)],
+        in_specs=[sm] + [vm] * len(parts),
+        out_specs=[vm] * 2,
+        cost_estimate=pl.CostEstimate(flops=2300000000, bytes_accessed=7200000, transcendentals=0),
+        name=f"halved_{shift}",
+    )(at, *parts)
+
+
+def last_kernel(held, got, out):
+    out[...] = (held[0] + got[0].astype(F32)).T * (1.0 / math.sqrt(PACK * 16))
+
+
+def last_sum(held, got):
+    vm = pl.BlockSpec(memory_space=pltpu.VMEM)
+    return pl.pallas_call(
+        last_kernel,
+        out_shape=jax.ShapeDtypeStruct((HEAD, 200), F32),
+        in_specs=[vm] * 2,
+        out_specs=vm,
+        cost_estimate=pl.CostEstimate(flops=2300000000, bytes_accessed=7200000, transcendentals=0),
+        name="last_sum",
+    )(held, got)
+
+
 def on_device(queries, keys_in, values_in, saved_out, out_grad, out_weight, image_units):
-    seq = lax.axis_index("seq")
-    dp = lax.axis_index("dp")
-    x, y, core = seq // 4, seq % 4, dp % 2
+    seq = lax.axis_index("seq").astype(jnp.int32)
+    dp = lax.axis_index("dp").astype(jnp.int32)
+    core = lax.rem(dp, 2)
+    at = jnp.stack([lax.div(seq, 4), lax.rem(seq, 4), core, lax.div(dp, 2)])
+    after = lax.optimization_barrier
+    move = lax.ppermute
+
     g = out_grad[0]
-
-    o_sent = saved_out[0].reshape(TOK, 4, 4, HEAD).transpose(2, 0, 1, 3).reshape(4, TOK, 4 * HEAD)
-    o_rows = lax.all_to_all(o_sent, "seq", split_axis=0, concat_axis=0, tiled=True, axis_index_groups=YGROUPS)
-
-    g_back = lax.ppermute(g, "seq", YS[1])
-    g_next = lax.ppermute(g, "seq", YS[3])
-    w_parts = [out_weight] + [lax.ppermute(out_weight, "seq", XS[k]) for k in (1, 2, 3)]
-    g_far = jnp.concatenate([lax.ppermute(g_back[:64], "seq", YS[1]), lax.ppermute(g_next[64:], "seq", YS[3])], axis=0)
-    g_rows = lax.dynamic_slice_in_dim(
-        jnp.concatenate([g, g_next, g_far, g_back, g, g_next, g_far], axis=0), lax.rem(4 - y, 4) * TOK, 4 * TOK, 0
+    back, ahead = move(g, "seq", YS[1]), move(g, "seq", YS[3])
+    wa = move(out_weight, ("dp", "seq"), BOTH)
+    wc = move(lax.dynamic_slice_in_dim(out_weight, 64 * core, 64, 0), "seq", XS[2])
+    o_rows = lax.all_to_all(
+        pack_out(saved_out[0]), "seq", split_axis=0, concat_axis=0, tiled=True, axis_index_groups=YGROUPS
     )
-    w_rows = jnp.concatenate(w_parts, axis=0)
-    head = nt(g_rows, w_rows).astype(BF)
-    o_flat = o_rows.reshape(4 * TOK, 4, HEAD)
-
-    h_parts = []
-    for k in range(4):
-        hk = head[:, k * HEAD : (k + 1) * HEAD]
-        ok = lax.dynamic_index_in_dim(o_flat, lax.rem(x + 4 - k, 4), 1, keepdims=False)
-        delta = jnp.sum(hk.astype(F32) * ok.astype(F32), axis=1).reshape(4, TOK)
-        hk = jnp.concatenate([hk, three_terms(delta)], axis=0)
-        h_parts.append(lax.ppermute(hk, "seq", XS[4 - k]) if k else hk)
-
-    qkv = lax.all_to_all(
-        pack(queries[0], keys_in[0], values_in[0]), "seq", split_axis=0, concat_axis=0, tiled=True
-    )
-    grads = attention(x.astype(jnp.int32)[None], image_units[0], qkv, h_parts)
-    back = lax.all_to_all(grads, "seq", split_axis=0, concat_axis=0, tiled=True)
-    query_grad, key_grad, value_grad = unpack(back)
-
-    term = tn(g_rows, o_rows.reshape(4 * TOK, 4 * HEAD)).astype(BF).reshape(8, 2, 200, 4 * HEAD)
-    mine = lax.dynamic_index_in_dim(term, core, 1, keepdims=False)
-    other = lax.ppermute(lax.dynamic_index_in_dim(term, 1 - core, 1, keepdims=False), "dp", CORES)
-    both = (mine.astype(F32) + other.astype(F32)).astype(BF).reshape(1600, 4 * HEAD)
-    summed = lax.psum_scatter(both, "dp", scatter_dimension=0, tiled=True, axis_index_groups=ZGROUPS)
-    blocks = summed.astype(F32).reshape(200, 4, HEAD)
-    weight = lax.dynamic_index_in_dim(blocks, x, 1, keepdims=False)
-    for k in (1, 2, 3):
-        weight = weight + lax.ppermute(
-            lax.dynamic_index_in_dim(blocks, lax.rem(x + k, 4), 1, keepdims=False), "seq", XS[k]
-        )
-    weight_grad = weight.T * (1.0 / math.sqrt(PACK * 16))
+    back, ahead, wa, wc, o_rows = after((back, ahead, wa, wc, o_rows))
+    fa, fb = move(back[:64], "seq", YS[1]), move(ahead[64:], "seq", YS[3])
+    wb, wd = move(wa, "dp", CORES), move(wc, "dp", CORES)
+    g_pieces = (g, back, ahead, fa, fb)
+    heads = head_blocks(at, g_pieces, (out_weight, wa, wb, wc, wd), o_rows)
+    local, o_later = after((heads[0], o_rows))
+    heads = [local] + [move(heads[k], "seq", XS[4 - k]) for k in (1, 2, 3)]
+
+    packed, _, _, _, _ = after((pack(queries[0], keys_in[0], values_in[0]), fa, fb, wb, wd))
+    qkv = lax.all_to_all(packed, "seq", split_axis=0, concat_axis=0, tiled=True)
+    mine, *other = weight_term(at, g_pieces, o_later)
+    pairs = pair_sum(at, mine, *[move(part, "dp", CORES) for part in other])
+    qkv, *pairs = after((qkv, *pairs))
+    grads = attention(at, image_units[0], qkv, heads)
+    sent = lax.all_to_all(grads, "seq", split_axis=0, concat_axis=0, tiled=True)
+    query_grad, key_grad, value_grad = unpack(sent)
+
+    parts = [pairs[0]] + [move(pairs[k], "seq", XS[k]) for k in (1, 2, 3)]
+    held, away = halved(at, parts, 1, 4)
+    held, away = halved(at, [held, move(away, "dp", ZS[0])], 2, 2)
+    held, away = halved(at, [held, move(away, "dp", ZS[1])], 4, 1)
+    weight_grad = last_sum(held, move(away, "dp", ZS[2]))
     return query_grad[None], key_grad[None], value_grad[None], weight_grad
 
 

time: 177 us -> 137 us (0.77)
  waiting for transfers between devices: 76 us -> 23.2 us
  Pallas kernels: 13.7 us -> 38.6 us
  blocking collectives: 0 us -> 20.3 us
  between operations: 14.3 us -> 0.79 us
  local copies, waits for them, and re-layouts: 21 us -> 11.3 us
  matrix products: 8.63 us -> 0 us
  starting transfers between devices: 35.6 us -> 40.4 us
  other arithmetic: 4.18 us -> 0.08 us
    pallas_call x0 -> x8, Pallas kernels: none -> 23.4 us  [the longest x3 5.89 us: halved(): pl.pallas_call(body, out_shape=[jax.ShapeDtypeStruct((count, 200, HEAD),...]
    all_to_all x0 -> x1, blocking collectives: none -> 20.3 us  [on_device(): lax.all_to_all(pack_out(saved_out[0]), 'seq', split_axis=0, concat_axis=0...]
    ppermute x14 -> x21, waiting for transfers between devices: 42.4 us -> 23.2 us  [the longest x2 8.58 us: on_device(): fa, fb = (move(back[:64], 'seq', YS[1]), move(ahead[64:], 'seq', YS[3]))]
    all_to_all x3 -> x2, waiting for transfers between devices: 18.8 us -> 0.01 us  [the longest x1 0.01 us: on_device(): qkv = lax.all_to_all(packed, 'seq', split_axis=0, concat_axis=0, tiled=True)]
    reduce_scatter x1 -> x0, waiting for transfers between devices: 14.8 us -> none  [on_device(): lax.psum_scatter(both, 'dp', scatter_dimension=0, tiled=True, axis_index_...]
    ppermute x14 -> x21, starting transfers between devices: 20 us -> 29.4 us  [the longest x1 6.12 us: on_device(): weight_grad = last_sum(held, move(away, 'dp', ZS[2]))]
    dot_general x2 -> x0, matrix products: 8.63 us -> none  [the longest x1 4.81 us: nt(): lax.dot_general(a, b, (((1,), (1,)), ((), ())), preferred_element_type=F32)]
    unnamed x19 -> x35, local copies, waits for them, and re-layouts: 13.7 us -> 8.73 us
  transfers between devices with their start and end apart: 18 -> 23, of which waited for: 10 -> 7; matrix products, arithmetic and copies ran while one was open for 11% -> 3% of each run, Pallas kernels for 8% -> 26%
where the time goes in v2:
time: 137 us; the launch traced here: 135 us
  starting transfers between devices  40.4 us (29%)
  Pallas kernels  38.6 us (28%)
  waiting for transfers between devices  23.2 us (17%)
  blocking collectives  20.3 us (15%)
  local copies, waits for them, and re-layouts  11.3 us (8%)
    all_to_all x1, blocking collectives, on_device(): lax.all_to_all(pack_out(saved_out[0]), 'seq', split_axis=0, concat_axis=0...  20.3 us
    pallas_call x1, Pallas kernels, attention(): pl.pallas_call(attention_kernel, out_shape=jax.ShapeDtypeStruct((16, 3, T...  9.48 us
    unnamed x35, local copies, waits for them, and re-layouts  8.73 us
    ppermute x2, waiting for transfers between devices, on_device(): fa, fb = (move(back[:64], 'seq', YS[1]), move(ahead[64:], 'seq', YS[3]))  8.58 us
    ppermute x1, starting transfers between devices, on_device(): weight_grad = last_sum(held, move(away, 'dp', ZS[2]))  6.12 us
    pallas_call x3, Pallas kernels, halved(): pl.pallas_call(body, out_shape=[jax.ShapeDtypeStruct((count, 200, HEAD),...  5.89 us
    all_to_all x1, starting transfers between devices, on_device(): sent = lax.all_to_all(grads, 'seq', split_axis=0, concat_axis=0, tiled=True)  5.86 us
    pallas_call x1, Pallas kernels, head_blocks(): pl.pallas_call(head_kernel, out_shape=[jax.ShapeDtypeStruct((4 * TOK + 16...  5.72 us
  transfers between devices with their start and end apart: 23, of which 7 were waited for; matrix products, arithmetic and copies ran while one was open for 3% of the time, Pallas kernels for 26%

profile of v2, /device:TPU:2, one launch (start us, length us, event | category | flops | bytes accessed | tf_op | source)
XLA Modules:
  0.0 134.7 jit_solution(13821096677151155583)
XLA Ops:
  0.6 3.1 %collective-permute-start.1 = (bf16[128,3200]{1,0:T(8,128)(2,1)}, bf16[128,3200]{1,0:T(8,128)(2,1)S(1)}, u32[]{:S(2)}, u32[]{:S(2)}) collective-permute-start(bf16[128,3200]{1,0:T(8,128)(2,1)} %bitcast.13), channel_id=1, source_target_pairs={{0,3},{1,0},{2,1},{3,2},{4,7},{5,4},{6,5},{7,6},{8,11},{9,8},{10,9... | collective-permute-start | bytes 2457608 | tf_op jit(solution)/shard_map/ppermute | solution.py:383
  6.3 1.9 %collective-permute-start.3 = (bf16[64,3200]{1,0:T(8,128)(2,1)S(1)}, bf16[64,3200]{1,0:T(8,128)(2,1)}, u32[]{:S(2)}, u32[]{:S(2)}) collective-permute-start(bf16[64,3200]{1,0:T(8,128)(2,1)S(1)} %constant_dynamic-slice_fusion), channel_id=1, source_target_pairs={{0,8},{1,9},{2,10},{3,11},{4,12},{5,13},{6,14},{7,15},{8,0},{9,1},... | collective-permute-start | bytes 1228808 | tf_op jit(solution)/shard_map/ppermute | solution.py:385
  8.2 1.9 %pack_out.1 = bf16[4,128,512]{2,1,0:T(8,128)(2,1)} custom-call(bf16[128,2048]{1,0:T(8,128)(2,1)} %bitcast.18), custom_call_target="tpu_custom_call" | custom-call | flops 1 | bytes 1 | tf_op jit(solution)/shard_map/pack_out/pallas_call | solution.py:182
  10.2 20.3 %all_to_all.15.refs_10_.refs_5_ = bf16[4,128,512]{2,1,0:T(8,128)(2,1)S(1)} all-to-all(bf16[4,128,512]{2,1,0:T(8,128)(2,1)} %pack_out.1), channel_id=1, replica_groups={{0,1,2,3},{4,5,6,7},{8,9,10,11},{12,13,14,15},{16,17,18,19},{20,21,22,2..., dimensions={0} | all-to-all | bytes 1048576 | tf_op jit(solution)/shard_map/all_to_all | solution.py:386
  34.2 2.8 %pack.1 = bf16[16,3,128,128]{3,2,1,0:T(8,128)(2,1)} custom-call(bf16[128,2048]{1,0:T(8,128)(2,1)} %bitcast.19, bf16[128,2048]{1,0:T(8,128)(2,1)} %bitcast.20, bf16[128,2048]{1,0:T(8,128)(2,1)} %bitcast.21), custom_call_target="tpu_custom_call" | custom-call | flops 1 | bytes 1 | tf_op jit(solution)/shard_map/pack/pallas_call | solution.py:137
  37.0 7.3 %collective-permute-done.5.refs_4_ = bf16[64,3200]{1,0:T(8,128)(2,1)S(1)} collective-permute-done((bf16[64,3200]{1,0:T(8,128)(2,1)}, bf16[64,3200]{1,0:T(8,128)(2,1)S(1)}, u32[]{:S(2)}, u32[]{:S(2)}) %collective-permute-start.5) | collective-permute-done | bytes 409632 | tf_op jit(solution)/shard_map/ppermute | solution.py:390
  45.6 5.1 %all-to-all-start.1 = ((bf16[16,3,128,128]{3,2,1,0:T(8,128)(2,1)}), bf16[16,3,128,128]{3,2,1,0:T(8,128)(2,1)}, u32[]{:S(2)}, u32[]{:S(2)}) async-start(bf16[16,3,128,128]{3,2,1,0:T(8,128)(2,1)} %pack.1), calls=%async_computation.1 | async-start | bytes 3145728 | tf_op jit(solution)/shard_map/all_to_all | solution.py:398
  51.9 5.7 %head_blocks.1 = (bf16[528,128]{1,0:T(8,128)(2,1)S(1)}, bf16[528,128]{1,0:T(8,128)(2,1)}, bf16[528,128]{1,0:T(8,128)(2,1)}, bf16[528,128]{1,0:T(8,128)(2,1)}) custom-call(s32[4]{0:T(128)S(1)} %pad_add_fusion.at.xi.refs_0_, bf16[128,3200]{1,0:T(8,128)(2,1)S(1)} %bitcast.15, bf16[128,3200]{1,0:T(8,128)(2,1)S(1)} %collective-permute-done.refs_1_, ...), custom_call_target="tpu_custom_call" | custom-call | flops 1 | bytes 1 | tf_op jit(solution)/shard_map/head_blocks/pallas_call | solution.py:251
  57.7 4.7 %weight_term.1 = (bf16[8,200,512]{2,1,0:T(8,128)(2,1)S(1)}, bf16[2,200,512]{2,1,0:T(8,128)(2,1)S(1)}, bf16[2,200,512]{2,1,0:T(8,128)(2,1)S(1)}, bf16[2,200,512]{2,1,0:T(8,128)(2,1)S(1)}, bf16[2,200,512]{2,1,0:T(8,128)(2,1)S(1)}) custom-call(s32[4]{0:T(128)S(1)} %pad_add_fusion.at.xi.refs_0_, bf16[128,3200]{1,0:T(8,128)(2,1)S(1)} %bitcast.16, ...), custom_call_target="tpu_custom_call" | custom-call | flops 1 | bytes 1 | tf_op jit(solution)/shard_map/weight_term/pallas_call | solution.py:291
  65.3 2.2 %collective-permute-start.13 = (bf16[528,128]{1,0:T(8,128)(2,1)}, bf16[528,128]{1,0:T(8,128)(2,1)S(1)}, u32[]{:S(2)}, u32[]{:S(2)}) collective-permute-start(bf16[528,128]{1,0:T(8,128)(2,1)} %get-tuple-element.59), channel_id=1, source_target_pairs={{0,8},{1,9},{2,10},{3,11},{4,12},{5,13},{6,14},{7,15},{8,0},{9,1},... | collective-permute-start | bytes 405512 | tf_op jit(solution)/shard_map/ppermute | solution.py:395
  70.2 3.5 %pair_sum.1 = (bf16[8,200,128]{2,1,0:T(8,128)(2,1)}, bf16[8,200,128]{2,1,0:T(8,128)(2,1)}, bf16[8,200,128]{2,1,0:T(8,128)(2,1)}, bf16[8,200,128]{2,1,0:T(8,128)(2,1)}) custom-call(s32[4]{0:T(128)} %copy-done.3, bf16[8,200,512]{2,1,0:T(8,128)(2,1)} %copy-done.2, bf16[2,200,512]{2,1,0:T(8,128)(2,1)} %copy-done.7, bf16[2,200,512]{2,1,0:T(8,128)(2,1)} %copy-done.8, ...), custom_call_target="tpu_custom_call" | custom-call | flops 1 | bytes 1 | tf_op jit(solution)/shard_map/pair_sum/pallas_call | solution.py:318
  73.8 2.6 %collective-permute-start.16 = (bf16[8,200,128]{2,1,0:T(8,128)(2,1)}, bf16[8,200,128]{2,1,0:T(8,128)(2,1)S(1)}, u32[]{:S(2)}, u32[]{:S(2)}) collective-permute-start(bf16[8,200,128]{2,1,0:T(8,128)(2,1)} %get-tuple-element.66), channel_id=1, source_target_pairs={{0,8},{1,9},{2,10},{3,11},{4,12},{5,13},{6,14},{7,15},{8,0},{9,1},... | collective-permute-start | bytes 1228808 | tf_op jit(solution)/shard_map/ppermute | solution.py:406
  78.0 9.5 %attention.1 = bf16[16,3,128,128]{3,2,1,0:T(8,128)(2,1)} custom-call(s32[4]{0:T(128)S(1)} %copy-done.4, s32[8]{0:T(128)S(1)} %bitcast.17, bf16[16,3,128,128]{3,2,1,0:T(8,128)(2,1)} %all-to-all-done.1.qkv, bf16[528,128]{1,0:T(8,128)(2,1)S(1)} %get-tuple-element.57.h0, bf16[528,128]{1,0:T(8,128)(2,1)S(1)} %collective-permute-done.12.h1, ...), custom_call_target="tpu_custom_call" | custom-call | flops 10350000128 | bytes 32400000 | tf_op jit(solution)/shard_map/attention/pallas_call | solution.py:115
  87.4 5.9 %all-to-all-start.2 = ((bf16[16,3,128,128]{3,2,1,0:T(8,128)(2,1)}), bf16[16,3,128,128]{3,2,1,0:T(8,128)(2,1)S(1)}, u32[]{:S(2)}, u32[]{:S(2)}) async-start(bf16[16,3,128,128]{3,2,1,0:T(8,128)(2,1)} %attention.1), calls=%async_computation.2 | async-start | bytes 3145728 | tf_op jit(solution)/shard_map/all_to_all | solution.py:403
  93.3 1.8 %collective-permute-done.17.d = bf16[8,200,128]{2,1,0:T(8,128)(2,1)S(1)} collective-permute-done((bf16[8,200,128]{2,1,0:T(8,128)(2,1)}, bf16[8,200,128]{2,1,0:T(8,128)(2,1)S(1)}, u32[]{:S(2)}, u32[]{:S(2)}) %collective-permute-start.17) | collective-permute-done | bytes 409632 | tf_op jit(solution)/shard_map/ppermute | solution.py:406
  95.9 2.4 %halved_1.1 = (f32[4,200,128]{2,1,0:T(8,128)}, bf16[4,200,128]{2,1,0:T(8,128)(2,1)}) custom-call(s32[4]{0:T(128)} %copy-done.3, bf16[8,200,128]{2,1,0:T(8,128)(2,1)} %get-tuple-element.64.a, bf16[8,200,128]{2,1,0:T(8,128)(2,1)} %copy-done.11, bf16[8,200,128]{2,1,0:T(8,128)(2,1)} %copy-done.12, bf16[8,200,128]{2,1,0:T(8,128)(2,1)} %copy-done.13), custom_call_target="tpu_custom_call" | custom-call | flops 2300000000 | bytes 7200000 | tf_op jit(solution)/shard_map/halved_1/pallas_call | solution.py:348
  98.3 1.9 %collective-permute-start.18 = (bf16[4,200,128]{2,1,0:T(8,128)(2,1)}, bf16[4,200,128]{2,1,0:T(8,128)(2,1)S(1)}, u32[]{:S(2)}, u32[]{:S(2)}) collective-permute-start(bf16[4,200,128]{2,1,0:T(8,128)(2,1)} %get-tuple-element.69), channel_id=1, source_target_pairs={{0,32},{16,48},{32,0},{48,16},{64,96},{80,112},{96,64},{112,80},{1... | collective-permute-start | bytes 614408 | tf_op jit(solution)/shard_map/ppermute | solution.py:408
  100.2 5.3 %collective-permute-done.18.refs_2_ = bf16[4,200,128]{2,1,0:T(8,128)(2,1)S(1)} collective-permute-done((bf16[4,200,128]{2,1,0:T(8,128)(2,1)}, bf16[4,200,128]{2,1,0:T(8,128)(2,1)S(1)}, u32[]{:S(2)}, u32[]{:S(2)}) %collective-permute-start.18) | collective-permute-done | bytes 204832 | tf_op jit(solution)/shard_map/ppermute | solution.py:408
  106.2 1.8 %halved_2.1 = (f32[2,200,128]{2,1,0:T(8,128)}, bf16[2,200,128]{2,1,0:T(8,128)(2,1)}) custom-call(s32[4]{0:T(128)} %copy-done.3, f32[4,200,128]{2,1,0:T(8,128)} %get-tuple-element.68.refs_1_, bf16[4,200,128]{2,1,0:T(8,128)(2,1)} %copy-done.14), custom_call_target="tpu_custom_call" | custom-call | flops 2300000000 | bytes 7200000 | tf_op jit(solution)/shard_map/halved_2/pallas_call | solution.py:348
  108.0 3.3 %collective-permute-start.19 = (bf16[2,200,128]{2,1,0:T(8,128)(2,1)}, bf16[2,200,128]{2,1,0:T(8,128)(2,1)S(1)}, u32[]{:S(2)}, u32[]{:S(2)}) collective-permute-start(bf16[2,200,128]{2,1,0:T(8,128)(2,1)} %get-tuple-element.71), channel_id=1, source_target_pairs={{0,64},{16,80},{32,96},{48,112},{64,0},{80,16},{96,32},{112,48},{1... | collective-permute-start | bytes 307208 | tf_op jit(solution)/shard_map/ppermute | solution.py:409
  111.3 4.6 %collective-permute-done.19.refs_2_ = bf16[2,200,128]{2,1,0:T(8,128)(2,1)S(1)} collective-permute-done((bf16[2,200,128]{2,1,0:T(8,128)(2,1)}, bf16[2,200,128]{2,1,0:T(8,128)(2,1)S(1)}, u32[]{:S(2)}, u32[]{:S(2)}) %collective-permute-start.19) | collective-permute-done | bytes 102432 | tf_op jit(solution)/shard_map/ppermute | solution.py:409
  118.2 6.1 %collective-permute-start.20 = (bf16[1,200,128]{2,1,0:T(8,128)(2,1)}, bf16[1,200,128]{2,1,0:T(8,128)(2,1)S(1)}, u32[]{:S(2)}, u32[]{:S(2)}) collective-permute-start(bf16[1,200,128]{2,1,0:T(8,128)(2,1)} %get-tuple-element.73), channel_id=1, source_target_pairs={{0,128},{16,144},{32,160},{48,176},{64,192},{80,208},{96,224},{112... | collective-permute-start | bytes 153608 | tf_op jit(solution)/shard_map/ppermute | solution.py:410
  124.3 2.3 %collective-permute-done.20.got = bf16[1,200,128]{2,1,0:T(8,128)(2,1)S(1)} collective-permute-done((bf16[1,200,128]{2,1,0:T(8,128)(2,1)}, bf16[1,200,128]{2,1,0:T(8,128)(2,1)S(1)}, u32[]{:S(2)}, u32[]{:S(2)}) %collective-permute-start.20) | collective-permute-done | bytes 51232 | tf_op jit(solution)/shard_map/ppermute | solution.py:410
  131.7 3.0 %unpack.1 = (bf16[128,2048]{1,0:T(8,128)(2,1)}, bf16[128,2048]{1,0:T(8,128)(2,1)}, bf16[128,2048]{1,0:T(8,128)(2,1)}) custom-call(bf16[16,3,128,128]{3,2,1,0:T(8,128)(2,1)} %copy-done.6), custom_call_target="tpu_custom_call" | custom-call | flops 1 | bytes 1 | tf_op jit(solution)/shard_map/unpack/pallas_call | solution.py:157
  (73 shorter events, 24.9 us)
Async XLA Ops:
  0.6 29.8 %collective-permute-start.1 = (bf16[128,3200]{1,0:T(8,128)(2,1)}, bf16[128,3200]{1,0:T(8,128)(2,1)S(1)}, u32[]{:S(2)}, u32[]{:S(2)}) collective-permute-start(bf16[128,3200]{1,0:T(8,128)(2,1)} %bitcast.13), channel_id=1, source_target_pairs={{0,3},{1,0},{2,1},{3,2},{4,7},{5,4},{6,5},{7,6},{8,11},{9,8},{10,9... | collective-permute-start | bytes 2457608 | tf_op jit(solution)/shard_map/ppermute | solution.py:383
  3.7 26.8 %collective-permute-start = (bf16[128,3200]{1,0:T(8,128)(2,1)}, bf16[128,3200]{1,0:T(8,128)(2,1)S(1)}, u32[]{:S(2)}, u32[]{:S(2)}) collective-permute-start(bf16[128,3200]{1,0:T(8,128)(2,1)} %bitcast.14), channel_id=1, source_target_pairs={{0,1},{1,2},{2,3},{3,0},{4,5},{5,6},{6,7},{7,4},{8,9},{9,10},{10,1... | collective-permute-start | bytes 2457608 | tf_op jit(solution)/shard_map/ppermute | solution.py:383
  3.7 26.8 %collective-permute-start.2 = (bf16[128,3200]{1,0:T(8,128)(2,1)}, bf16[128,3200]{1,0:T(8,128)(2,1)}, u32[]{:S(2)}, u32[]{:S(2)}) collective-permute-start(bf16[128,3200]{1,0:T(8,128)(2,1)} %refs_5_.1), channel_id=1, source_target_pairs={{0,4},{1,5},{2,6},{3,7},{4,8},{5,9},{6,10},{7,11},{8,12},{9,13},{1... | collective-permute-start | bytes 2457608 | tf_op jit(solution)/shard_map/ppermute | solution.py:384
  6.3 24.2 %collective-permute-start.3 = (bf16[64,3200]{1,0:T(8,128)(2,1)S(1)}, bf16[64,3200]{1,0:T(8,128)(2,1)}, u32[]{:S(2)}, u32[]{:S(2)}) collective-permute-start(bf16[64,3200]{1,0:T(8,128)(2,1)S(1)} %constant_dynamic-slice_fusion), channel_id=1, source_target_pairs={{0,8},{1,9},{2,10},{3,11},{4,12},{5,13},{6,14},{7,15},{8,0},{9,1},... | collective-permute-start | bytes 1228808 | tf_op jit(solution)/shard_map/ppermute | solution.py:385
  30.5 15.1 %collective-permute-start.6 = (bf16[128,3200]{1,0:T(8,128)(2,1)}, bf16[128,3200]{1,0:T(8,128)(2,1)}, u32[]{:S(2)}, u32[]{:S(2)}) collective-permute-start(bf16[128,3200]{1,0:T(8,128)(2,1)} %collective-permute-done.2.refs_6_), channel_id=1, source_target_pairs={{0,16},{16,0},{32,48},{48,32},{64,80},{80,64},{96,112},{112,96},{1... | collective-permute-start | bytes 2457608 | tf_op jit(solution)/shard_map/ppermute | solution.py:391
  32.1 12.1 %collective-permute-start.5 = (bf16[64,3200]{1,0:T(8,128)(2,1)}, bf16[64,3200]{1,0:T(8,128)(2,1)S(1)}, u32[]{:S(2)}, u32[]{:S(2)}) collective-permute-start(bf16[64,3200]{1,0:T(8,128)(2,1)} %slice.7), channel_id=1, source_target_pairs={{0,3},{1,0},{2,1},{3,2},{4,7},{5,4},{6,5},{7,6},{8,11},{9,8},{10,9... | collective-permute-start | bytes 1228808 | tf_op jit(solution)/shard_map/ppermute | solution.py:390
  32.4 13.1 %collective-permute-start.4 = (bf16[64,3200]{1,0:T(8,128)(2,1)}, bf16[64,3200]{1,0:T(8,128)(2,1)}, u32[]{:S(2)}, u32[]{:S(2)}) collective-permute-start(bf16[64,3200]{1,0:T(8,128)(2,1)} %slice.6), channel_id=1, source_target_pairs={{0,1},{1,2},{2,3},{3,0},{4,5},{5,6},{6,7},{7,4},{8,9},{9,10},{10,1... | collective-permute-start | bytes 1228808 | tf_op jit(solution)/shard_map/ppermute | solution.py:390
  34.2 11.4 %collective-permute-start.7 = (bf16[64,3200]{1,0:T(8,128)(2,1)}, bf16[64,3200]{1,0:T(8,128)(2,1)}, u32[]{:S(2)}, u32[]{:S(2)}) collective-permute-start(bf16[64,3200]{1,0:T(8,128)(2,1)} %collective-permute-done.3.refs_8_), channel_id=1, source_target_pairs={{0,16},{16,0},{32,48},{48,32},{64,80},{80,64},{96,112},{112,96},{1... | collective-permute-start | bytes 1228808 | tf_op jit(solution)/shard_map/ppermute | solution.py:391
  37.0 13.8 %copy-start = (bf16[1,128,3200]{2,1,0:T(8,128)(2,1)S(1)}, bf16[1,128,3200]{2,1,0:T(8,128)(2,1)}, u32[]{:S(2)}) copy-start(bf16[1,128,3200]{2,1,0:T(8,128)(2,1)} %param.11) | copy-start | bytes 2457604
  45.6 28.1 %all-to-all-start.1 = ((bf16[16,3,128,128]{3,2,1,0:T(8,128)(2,1)}), bf16[16,3,128,128]{3,2,1,0:T(8,128)(2,1)}, u32[]{:S(2)}, u32[]{:S(2)}) async-start(bf16[16,3,128,128]{3,2,1,0:T(8,128)(2,1)} %pack.1), calls=%async_computation.1 | async-start | bytes 3145728 | tf_op jit(solution)/shard_map/all_to_all | solution.py:398
  63.6 1.7 %collective-permute-start.8 = (bf16[2,200,512]{2,1,0:T(8,128)(2,1)S(1)}, bf16[2,200,512]{2,1,0:T(8,128)(2,1)S(1)}, u32[]{:S(2)}, u32[]{:S(2)}) collective-permute-start(bf16[2,200,512]{2,1,0:T(8,128)(2,1)S(1)} %get-tuple-element.48), channel_id=1, source_target_pairs={{0,16},{16,0},{32,48},{48,32},{64,80},{80,64},{96,112},{112,96},{1... | collective-permute-start | bytes 1228808 | tf_op jit(solution)/shard_map/ppermute | solution.py:400
  63.6 4.0 %collective-permute-start.9 = (bf16[2,200,512]{2,1,0:T(8,128)(2,1)S(1)}, bf16[2,200,512]{2,1,0:T(8,128)(2,1)S(1)}, u32[]{:S(2)}, u32[]{:S(2)}) collective-permute-start(bf16[2,200,512]{2,1,0:T(8,128)(2,1)S(1)} %get-tuple-element.49), channel_id=1, source_target_pairs={{0,16},{16,0},{32,48},{48,32},{64,80},{80,64},{96,112},{112,96},{1... | collective-permute-start | bytes 1228808 | tf_op jit(solution)/shard_map/ppermute | solution.py:400
  64.1 5.2 %collective-permute-start.10 = (bf16[2,200,512]{2,1,0:T(8,128)(2,1)S(1)}, bf16[2,200,512]{2,1,0:T(8,128)(2,1)S(1)}, u32[]{:S(2)}, u32[]{:S(2)}) collective-permute-start(bf16[2,200,512]{2,1,0:T(8,128)(2,1)S(1)} %get-tuple-element.50), channel_id=1, source_target_pairs={{0,16},{16,0},{32,48},{48,32},{64,80},{80,64},{96,112},{112,96},{1... | collective-permute-start | bytes 1228808 | tf_op jit(solution)/shard_map/ppermute | solution.py:400
  64.1 5.2 %collective-permute-start.11 = (bf16[2,200,512]{2,1,0:T(8,128)(2,1)S(1)}, bf16[2,200,512]{2,1,0:T(8,128)(2,1)S(1)}, u32[]{:S(2)}, u32[]{:S(2)}) collective-permute-start(bf16[2,200,512]{2,1,0:T(8,128)(2,1)S(1)} %get-tuple-element.51), channel_id=1, source_target_pairs={{0,16},{16,0},{32,48},{48,32},{64,80},{80,64},{96,112},{112,96},{1... | collective-permute-start | bytes 1228808 | tf_op jit(solution)/shard_map/ppermute | solution.py:400
  64.6 11.8 %collective-permute-start.12 = (bf16[528,128]{1,0:T(8,128)(2,1)}, bf16[528,128]{1,0:T(8,128)(2,1)S(1)}, u32[]{:S(2)}, u32[]{:S(2)}) collective-permute-start(bf16[528,128]{1,0:T(8,128)(2,1)} %get-tuple-element.58), channel_id=1, source_target_pairs={{0,12},{1,13},{2,14},{3,15},{4,0},{5,1},{6,2},{7,3},{8,4},{9,5},{1... | collective-permute-start | bytes 405512 | tf_op jit(solution)/shard_map/ppermute | solution.py:395
  65.3 12.6 %collective-permute-start.13 = (bf16[528,128]{1,0:T(8,128)(2,1)}, bf16[528,128]{1,0:T(8,128)(2,1)S(1)}, u32[]{:S(2)}, u32[]{:S(2)}) collective-permute-start(bf16[528,128]{1,0:T(8,128)(2,1)} %get-tuple-element.59), channel_id=1, source_target_pairs={{0,8},{1,9},{2,10},{3,11},{4,12},{5,13},{6,14},{7,15},{8,0},{9,1},... | collective-permute-start | bytes 405512 | tf_op jit(solution)/shard_map/ppermute | solution.py:395
  67.6 10.4 %collective-permute-start.14 = (bf16[528,128]{1,0:T(8,128)(2,1)}, bf16[528,128]{1,0:T(8,128)(2,1)S(1)}, u32[]{:S(2)}, u32[]{:S(2)}) collective-permute-start(bf16[528,128]{1,0:T(8,128)(2,1)} %get-tuple-element.60), channel_id=1, source_target_pairs={{0,4},{1,5},{2,6},{3,7},{4,8},{5,9},{6,10},{7,11},{8,12},{9,13},{1... | collective-permute-start | bytes 405512 | tf_op jit(solution)/shard_map/ppermute | solution.py:395
  73.7 19.6 %collective-permute-start.15 = (bf16[8,200,128]{2,1,0:T(8,128)(2,1)}, bf16[8,200,128]{2,1,0:T(8,128)(2,1)S(1)}, u32[]{:S(2)}, u32[]{:S(2)}) collective-permute-start(bf16[8,200,128]{2,1,0:T(8,128)(2,1)} %get-tuple-element.65), channel_id=1, source_target_pairs={{0,4},{1,5},{2,6},{3,7},{4,8},{5,9},{6,10},{7,11},{8,12},{9,13},{1... | collective-permute-start | bytes 1228808 | tf_op jit(solution)/shard_map/ppermute | solution.py:406
  73.8 19.5 %collective-permute-start.16 = (bf16[8,200,128]{2,1,0:T(8,128)(2,1)}, bf16[8,200,128]{2,1,0:T(8,128)(2,1)S(1)}, u32[]{:S(2)}, u32[]{:S(2)}) collective-permute-start(bf16[8,200,128]{2,1,0:T(8,128)(2,1)} %get-tuple-element.66), channel_id=1, source_target_pairs={{0,8},{1,9},{2,10},{3,11},{4,12},{5,13},{6,14},{7,15},{8,0},{9,1},... | collective-permute-start | bytes 1228808 | tf_op jit(solution)/shard_map/ppermute | solution.py:406
  76.4 18.7 %collective-permute-start.17 = (bf16[8,200,128]{2,1,0:T(8,128)(2,1)}, bf16[8,200,128]{2,1,0:T(8,128)(2,1)S(1)}, u32[]{:S(2)}, u32[]{:S(2)}) collective-permute-start(bf16[8,200,128]{2,1,0:T(8,128)(2,1)} %get-tuple-element.67), channel_id=1, source_target_pairs={{0,12},{1,13},{2,14},{3,15},{4,0},{5,1},{6,2},{7,3},{8,4},{9,5},{1... | collective-permute-start | bytes 1228808 | tf_op jit(solution)/shard_map/ppermute | solution.py:406
  87.4 43.1 %all-to-all-start.2 = ((bf16[16,3,128,128]{3,2,1,0:T(8,128)(2,1)}), bf16[16,3,128,128]{3,2,1,0:T(8,128)(2,1)S(1)}, u32[]{:S(2)}, u32[]{:S(2)}) async-start(bf16[16,3,128,128]{3,2,1,0:T(8,128)(2,1)} %attention.1), calls=%async_computation.2 | async-start | bytes 3145728 | tf_op jit(solution)/shard_map/all_to_all | solution.py:403
  98.3 7.2 %collective-permute-start.18 = (bf16[4,200,128]{2,1,0:T(8,128)(2,1)}, bf16[4,200,128]{2,1,0:T(8,128)(2,1)S(1)}, u32[]{:S(2)}, u32[]{:S(2)}) collective-permute-start(bf16[4,200,128]{2,1,0:T(8,128)(2,1)} %get-tuple-element.69), channel_id=1, source_target_pairs={{0,32},{16,48},{32,0},{48,16},{64,96},{80,112},{96,64},{112,80},{1... | collective-permute-start | bytes 614408 | tf_op jit(solution)/shard_map/ppermute | solution.py:408
  108.0 7.9 %collective-permute-start.19 = (bf16[2,200,128]{2,1,0:T(8,128)(2,1)}, bf16[2,200,128]{2,1,0:T(8,128)(2,1)S(1)}, u32[]{:S(2)}, u32[]{:S(2)}) collective-permute-start(bf16[2,200,128]{2,1,0:T(8,128)(2,1)} %get-tuple-element.71), channel_id=1, source_target_pairs={{0,64},{16,80},{32,96},{48,112},{64,0},{80,16},{96,32},{112,48},{1... | collective-permute-start | bytes 307208 | tf_op jit(solution)/shard_map/ppermute | solution.py:409
  118.2 8.4 %collective-permute-start.20 = (bf16[1,200,128]{2,1,0:T(8,128)(2,1)}, bf16[1,200,128]{2,1,0:T(8,128)(2,1)S(1)}, u32[]{:S(2)}, u32[]{:S(2)}) collective-permute-start(bf16[1,200,128]{2,1,0:T(8,128)(2,1)} %get-tuple-element.73), channel_id=1, source_target_pairs={{0,128},{16,144},{32,160},{48,176},{64,192},{80,208},{96,224},{112... | collective-permute-start | bytes 153608 | tf_op jit(solution)/shard_map/ppermute | solution.py:410
  (16 other events, 38.5 us)

commit v3 on v2

--- a/solution.py
+++ b/solution.py
@@ -20,7 +20,8 @@
 YS = [[(4 * x + y, 4 * x + (y + k) % 4) for x in range(4) for y in range(4)] for k in range(4)]
 YGROUPS = [[4 * x + y for y in range(4)] for x in range(4)]
 CORES = [(i, i ^ 1) for i in range(16)]
-ZS = [[(2 * z + c, 2 * (z ^ b) + c) for z in range(8) for c in range(2)] for b in (1, 2, 4)]
+ZNEAR = [(2 * z + c, 2 * (z ^ 1) + c) for z in range(8) for c in range(2)]
+ZFAR = [[(2 * z + c, 2 * ((z + 2 * k) % 8) + c) for z in range(8) for c in range(2)] for k in range(4)]
 BOTH = [
     (16 * d + 4 * x + y, 16 * d + 4 * ((x + (1, 3)[d % 2]) % 4) + y)
     for d in range(16)
@@ -97,7 +98,7 @@
     def one(j, start):
         size = units[j] * 16
         start = pl.multiple_of(start, 16)
-        for width, step in ((128, 128), (256, 256), (384, 384), (512, 256)):
+        for width, step in ((128, 128), (256, 256), (384, 384), (512, 512)):
             pl.when((size > width - 128) & (size <= width))(lambda width=width, step=step: image(start, size, width, step))
         return start + size
 
@@ -118,7 +119,7 @@
         in_specs=[sm, sm] + [vm] * 5,
         out_specs=vm,
         scratch_shapes=[pltpu.VMEM((PACK + IMG, HEAD), BF)] * 4 + [pltpu.VMEM((24, HEAD), F32)] + [pltpu.VMEM((PACK + IMG, HEAD), BF)] * 3,
-        compiler_params=pltpu.CompilerParams(vmem_limit_bytes=40 * 1024 * 1024),
+        compiler_params=pltpu.CompilerParams(vmem_limit_bytes=60 * 1024 * 1024),
         cost_estimate=pl.CostEstimate(flops=10350000000, bytes_accessed=32400000, transcendentals=0),
         name="attention",
     )(xi, units, qkv, *hs)
@@ -139,7 +140,7 @@
         out_shape=jax.ShapeDtypeStruct((16, 3, TOK, HEAD), BF),
         in_specs=[vm] * 3,
         out_specs=vm,
-        cost_estimate=pl.CostEstimate(flops=1, bytes_accessed=1, transcendentals=0),
+        cost_estimate=pl.CostEstimate(flops=1150000, bytes_accessed=3600, transcendentals=0),
         name="pack",
     )(q, k, v)
 
@@ -153,12 +154,14 @@
 
 
 def unpack(grads):
-    vm = pl.BlockSpec(memory_space=pltpu.VMEM)
+    rows = TOK // 2
     return pl.pallas_call(
         unpack_kernel,
+        grid=(2,),
         out_shape=[jax.ShapeDtypeStruct((TOK, 16 * HEAD), BF)] * 3,
-        in_specs=[vm],
-        out_specs=[vm] * 3,
+        in_specs=[pl.BlockSpec((16, 3, rows, HEAD), lambda i: (0, 0, i, 0))],
+        out_specs=[pl.BlockSpec((rows, 16 * HEAD), lambda i: (i, 0))] * 3,
+        compiler_params=pltpu.CompilerParams(vmem_limit_bytes=60 * 1024 * 1024),
         cost_estimate=pl.CostEstimate(flops=1, bytes_accessed=1, transcendentals=0),
         name="unpack",
     )(grads)
@@ -260,8 +263,8 @@
             pltpu.SemaphoreType.DMA((MODEL // CHUNK, 5)),
             pltpu.SemaphoreType.DMA((MODEL // CHUNK, 5)),
         ],
-        compiler_params=pltpu.CompilerParams(vmem_limit_bytes=40 * 1024 * 1024),
-        cost_estimate=pl.CostEstimate(flops=1, bytes_accessed=1, transcendentals=0),
+        compiler_params=pltpu.CompilerParams(vmem_limit_bytes=60 * 1024 * 1024),
+        cost_estimate=pl.CostEstimate(flops=3450000000, bytes_accessed=10800000, transcendentals=0),
         name="head_blocks",
     )(at, *g, *w, o)
 
@@ -298,8 +301,8 @@
             pltpu.VMEM((MODEL, 4 * HEAD), F32),
             pltpu.SemaphoreType.DMA((MODEL // CHUNK, 5)),
         ],
-        compiler_params=pltpu.CompilerParams(vmem_limit_bytes=40 * 1024 * 1024),
-        cost_estimate=pl.CostEstimate(flops=1, bytes_accessed=1, transcendentals=0),
+        compiler_params=pltpu.CompilerParams(vmem_limit_bytes=60 * 1024 * 1024),
+        cost_estimate=pl.CostEstimate(flops=6900000000, bytes_accessed=21600000, transcendentals=0),
         name="weight_term",
     )(at, *g, o)
 
@@ -325,57 +328,11 @@
     )(at, mine, *other)
 
 
-def row_kernel(at, a, b, c, d, kept, sent):
-    bit = lax.rem(at[3], 2)
-    for i in range(4):
-        own, away = 2 * i + bit, 2 * i + 1 - bit
-        kept[i] = a[own].astype(F32) + b[own].astype(F32) + c[own].astype(F32) + d[own].astype(F32)
-        sent[i] = (a[away].astype(F32) + b[away].astype(F32) + c[away].astype(F32) + d[away].astype(F32)).astype(BF)
-
-
-def half_kernel(shift, at, held, got, kept, sent):
-    bit = lax.rem(lax.div(at[3], shift), 2)
-    for i in range(held.shape[0] // 2):
-        own, away = 2 * i + bit, 2 * i + 1 - bit
-        kept[i] = held[own] + got[own].astype(F32)
-        sent[i] = (held[away] + got[away].astype(F32)).astype(BF)
-
-
-def halved(at, parts, shift, count):
-    vm = pl.BlockSpec(memory_space=pltpu.VMEM)
-    sm = pl.BlockSpec(memory_space=pltpu.SMEM)
-    body = row_kernel if shift == 1 else lambda *refs: half_kernel(shift, *refs)
-    return pl.pallas_call(
-        body,
-        out_shape=[jax.ShapeDtypeStruct((count, 200, HEAD), F32), jax.ShapeDtypeStruct((count, 200, HEAD), BF)],
-        in_specs=[sm] + [vm] * len(parts),
-        out_specs=[vm] * 2,
-        cost_estimate=pl.CostEstimate(flops=2300000000, bytes_accessed=7200000, transcendentals=0),
-        name=f"halved_{shift}",
-    )(at, *parts)
-
-
-def last_kernel(held, got, out):
-    out[...] = (held[0] + got[0].astype(F32)).T * (1.0 / math.sqrt(PACK * 16))
-
-
-def last_sum(held, got):
-    vm = pl.BlockSpec(memory_space=pltpu.VMEM)
-    return pl.pallas_call(
-        last_kernel,
-        out_shape=jax.ShapeDtypeStruct((HEAD, 200), F32),
-        in_specs=[vm] * 2,
-        out_specs=vm,
-        cost_estimate=pl.CostEstimate(flops=2300000000, bytes_accessed=7200000, transcendentals=0),
-        name="last_sum",
-    )(held, got)
-
-
 def on_device(queries, keys_in, values_in, saved_out, out_grad, out_weight, image_units):
     seq = lax.axis_index("seq").astype(jnp.int32)
     dp = lax.axis_index("dp").astype(jnp.int32)
-    core = lax.rem(dp, 2)
-    at = jnp.stack([lax.div(seq, 4), lax.rem(seq, 4), core, lax.div(dp, 2)])
+    core, z = lax.rem(dp, 2), lax.div(dp, 2)
+    at = jnp.stack([lax.div(seq, 4), lax.rem(seq, 4), core, z])
     after = lax.optimization_barrier
     move = lax.ppermute
 
@@ -387,27 +344,35 @@
         pack_out(saved_out[0]), "seq", split_axis=0, concat_axis=0, tiled=True, axis_index_groups=YGROUPS
     )
     back, ahead, wa, wc, o_rows = after((back, ahead, wa, wc, o_rows))
-    fa, fb = move(back[:64], "seq", YS[1]), move(ahead[64:], "seq", YS[3])
+    q, fa, fb = after((queries[0], back[:64], ahead[64:]))
+    fa, fb = move(fa, "seq", YS[1]), move(fb, "seq", YS[3])
     wb, wd = move(wa, "dp", CORES), move(wc, "dp", CORES)
+    qkv = lax.all_to_all(pack(q, keys_in[0], values_in[0]), "seq", split_axis=0, concat_axis=0, tiled=True)
     g_pieces = (g, back, ahead, fa, fb)
-    heads = head_blocks(at, g_pieces, (out_weight, wa, wb, wc, wd), o_rows)
-    local, o_later = after((heads[0], o_rows))
-    heads = [local] + [move(heads[k], "seq", XS[4 - k]) for k in (1, 2, 3)]
-
-    packed, _, _, _, _ = after((pack(queries[0], keys_in[0], values_in[0]), fa, fb, wb, wd))
-    qkv = lax.all_to_all(packed, "seq", split_axis=0, concat_axis=0, tiled=True)
-    mine, *other = weight_term(at, g_pieces, o_later)
+
+    mine, *other = weight_term(at, g_pieces, o_rows)
+    mine, at_later = after((mine, at))
+    heads = head_blocks(at_later, g_pieces, (out_weight, wa, wb, wc, wd), o_rows)
+    heads = [heads[0]] + [move(heads[k], "seq", XS[4 - k]) for k in (1, 2, 3)]
+
     pairs = pair_sum(at, mine, *[move(part, "dp", CORES) for part in other])
     qkv, *pairs = after((qkv, *pairs))
     grads = attention(at, image_units[0], qkv, heads)
     sent = lax.all_to_all(grads, "seq", split_axis=0, concat_axis=0, tiled=True)
     query_grad, key_grad, value_grad = unpack(sent)
 
-    parts = [pairs[0]] + [move(pairs[k], "seq", XS[k]) for k in (1, 2, 3)]
-    held, away = halved(at, parts, 1, 4)
-    held, away = halved(at, [held, move(away, "dp", ZS[0])], 2, 2)
-    held, away = halved(at, [held, move(away, "dp", ZS[1])], 4, 1)
-    weight_grad = last_sum(held, move(away, "dp", ZS[2]))
+    total = pairs[0].astype(F32)
+    for k in (1, 2, 3):
+        total = total + move(pairs[k], "seq", XS[k]).astype(F32)
+    total = total.reshape(4, 2, 200, HEAD)
+    bit, quarter = lax.rem(z, 2), lax.div(z, 2)
+    away = lax.dynamic_index_in_dim(total, 1 - bit, 1, keepdims=False).astype(BF)
+    total = lax.dynamic_index_in_dim(total, bit, 1, keepdims=False) + move(away, "dp", ZNEAR).astype(F32)
+    last = lax.dynamic_index_in_dim(total, quarter, 0, keepdims=False)
+    for k in (1, 2, 3):
+        part = lax.dynamic_index_in_dim(total, lax.rem(quarter + k, 4), 0, keepdims=False).astype(BF)
+        last = last + move(part, "dp", ZFAR[k]).astype(F32)
+    weight_grad = last.T * (1.0 / math.sqrt(PACK * 16))
     return query_grad[None], key_grad[None], value_grad[None], weight_grad
 
 

time: 137 us -> 122 us (0.89)
  the two profiles are of different devices: /device:TPU:2 before, /device:TPU:26 now
where the time goes in v3:
time: 122 us; the launch traced here: 121 us
  starting transfers between devices  42.4 us (35%)
  Pallas kernels  32.7 us (27%)
  blocking collectives  19.5 us (16%)
  waiting for transfers between devices  17.1 us (14%)
  local copies, waits for them, and re-layouts  6.32 us (5%)
  other arithmetic  2.64 us (2%)
    all_to_all x1, blocking collectives, on_device(): lax.all_to_all(pack_out(saved_out[0]), 'seq', split_axis=0, concat_axis=0...  19.5 us
    ppermute x3, starting transfers between devices, on_device(): last = last + move(part, 'dp', ZFAR[k]).astype(F32)  11 us
    pallas_call x1, Pallas kernels, attention(): pl.pallas_call(attention_kernel, out_shape=jax.ShapeDtypeStruct((16, 3, T...  8.65 us
    all_to_all x1, starting transfers between devices, on_device(): lax.all_to_all(pack(q, keys_in[0], values_in[0]), 'seq', split_axis=0, co...  6.96 us
    pallas_call x1, Pallas kernels, weight_term(): pl.pallas_call(term_kernel, out_shape=[jax.ShapeDtypeStruct((n, 200, 4 *...  6.93 us
    pallas_call x1, Pallas kernels, head_blocks(): pl.pallas_call(head_kernel, out_shape=[jax.ShapeDtypeStruct((4 * TOK + 16...  6.51 us
    all_to_all x1, starting transfers between devices, on_device(): sent = lax.all_to_all(grads, 'seq', split_axis=0, concat_axis=0, tiled=True)  5.94 us
    ppermute x3, waiting for transfers between devices, on_device(): total = total + move(pairs[k], 'seq', XS[k]).astype(F32)  5.18 us
  transfers between devices with their start and end apart: 24, of which 5 were waited for; matrix products, arithmetic and copies ran while one was open for 3% of the time, Pallas kernels for 25%

profile of v3, /device:TPU:26, one launch (start us, length us, event | category | flops | bytes accessed | tf_op | source)
XLA Modules:
  0.0 121.5 jit_solution(13232628721139333278)
XLA Ops:
  0.9 1.8 %collective-permute-start.1 = (bf16[128,3200]{1,0:T(8,128)(2,1)}, bf16[128,3200]{1,0:T(8,128)(2,1)S(1)}, u32[]{:S(2)}, u32[]{:S(2)}) collective-permute-start(bf16[128,3200]{1,0:T(8,128)(2,1)} %bitcast.47), channel_id=1, source_target_pairs={{0,3},{1,0},{2,1},{3,2},{4,7},{5,4},{6,5},{7,6},{8,11},{9,8},{10,9... | collective-permute-start | bytes 2457608 | tf_op jit(solution)/shard_map/ppermute | solution.py:340
  2.7 1.5 %collective-permute-start.2 = (bf16[128,3200]{1,0:T(8,128)(2,1)}, bf16[128,3200]{1,0:T(8,128)(2,1)}, u32[]{:S(2)}, u32[]{:S(2)}) collective-permute-start(bf16[128,3200]{1,0:T(8,128)(2,1)} %refs_5_.1), channel_id=1, source_target_pairs={{0,4},{1,5},{2,6},{3,7},{4,8},{5,9},{6,10},{7,11},{8,12},{9,13},{1... | collective-permute-start | bytes 2457608 | tf_op jit(solution)/shard_map/ppermute | solution.py:341
  6.5 1.9 %pack_out.1 = bf16[4,128,512]{2,1,0:T(8,128)(2,1)} custom-call(bf16[128,2048]{1,0:T(8,128)(2,1)} %bitcast.42), custom_call_target="tpu_custom_call" | custom-call | flops 1 | bytes 1 | tf_op jit(solution)/shard_map/pack_out/pallas_call | solution.py:185
  8.4 19.5 %all_to_all.15.refs_5_.refs_10_ = bf16[4,128,512]{2,1,0:T(8,128)(2,1)} all-to-all(bf16[4,128,512]{2,1,0:T(8,128)(2,1)} %pack_out.1), channel_id=1, replica_groups={{0,1,2,3},{4,5,6,7},{8,9,10,11},{12,13,14,15},{16,17,18,19},{20,21,22,2..., dimensions={0} | all-to-all | bytes 1048576 | tf_op jit(solution)/shard_map/all_to_all | solution.py:343
  28.8 1.4 %collective-permute-start.4 = (bf16[64,3200]{1,0:T(8,128)(2,1)S(1)}, bf16[64,3200]{1,0:T(8,128)(2,1)}, u32[]{:S(2)}, u32[]{:S(2)}) collective-permute-start(bf16[64,3200]{1,0:T(8,128)(2,1)S(1)} %slice.6), channel_id=1, source_target_pairs={{0,1},{1,2},{2,3},{3,0},{4,5},{5,6},{6,7},{7,4},{8,9},{9,10},{10,1... | collective-permute-start | bytes 1228808 | tf_op jit(solution)/shard_map/ppermute | solution.py:348
  30.9 2.8 %pack.1 = bf16[16,3,128,128]{3,2,1,0:T(8,128)(2,1)} custom-call(bf16[128,2048]{1,0:T(8,128)(2,1)} %bitcast.43, bf16[128,2048]{1,0:T(8,128)(2,1)} %bitcast.44, bf16[128,2048]{1,0:T(8,128)(2,1)} %bitcast.45), custom_call_target="tpu_custom_call" | custom-call | flops 1150000 | bytes 3600 | tf_op jit(solution)/shard_map/pack/pallas_call | solution.py:138
  33.7 7.0 %all-to-all-start.1 = ((bf16[16,3,128,128]{3,2,1,0:T(8,128)(2,1)}), bf16[16,3,128,128]{3,2,1,0:T(8,128)(2,1)S(1)}, u32[]{:S(2)}, u32[]{:S(2)}) async-start(bf16[16,3,128,128]{3,2,1,0:T(8,128)(2,1)} %pack.1), calls=%async_computation.1 | async-start | bytes 3145728 | tf_op jit(solution)/shard_map/all_to_all | solution.py:350
  41.7 4.3 %collective-permute-done.5.refs_4_ = bf16[64,3200]{1,0:T(8,128)(2,1)} collective-permute-done((bf16[64,3200]{1,0:T(8,128)(2,1)S(1)}, bf16[64,3200]{1,0:T(8,128)(2,1)}, u32[]{:S(2)}, u32[]{:S(2)}) %collective-permute-start.5) | collective-permute-done | bytes 409632 | tf_op jit(solution)/shard_map/ppermute | solution.py:348
  46.1 6.9 %weight_term.1 = (bf16[8,200,512]{2,1,0:T(8,128)(2,1)}, bf16[2,200,512]{2,1,0:T(8,128)(2,1)}, bf16[2,200,512]{2,1,0:T(8,128)(2,1)}, bf16[2,200,512]{2,1,0:T(8,128)(2,1)}, bf16[2,200,512]{2,1,0:T(8,128)(2,1)}) custom-call(s32[4]{0:T(128)} %pad_add_fusion.at.xi, bf16[128,3200]{1,0:T(8,128)(2,1)} %bitcast.48, bf16[128,3200]{1,0:T(8,128)(2,1)} %copy-done.8, ...), custom_call_target="tpu_custom_call" | custom-call | flops 6899999744 | bytes 21600000 | tf_op jit(solution)/shard_map/weight_term/pallas_call | solution.py:294
  54.5 6.5 %head_blocks.1 = (bf16[528,128]{1,0:T(8,128)(2,1)}, bf16[528,128]{1,0:T(8,128)(2,1)}, bf16[528,128]{1,0:T(8,128)(2,1)}, bf16[528,128]{1,0:T(8,128)(2,1)}) custom-call(s32[4]{0:T(128)} %pad_add_fusion.at.xi, bf16[128,3200]{1,0:T(8,128)(2,1)} %bitcast.49, bf16[128,3200]{1,0:T(8,128)(2,1)} %copy-done.8, bf16[128,3200]{1,0:T(8,128)(2,1)} %copy-done.9, ...), custom_call_target="tpu_custom_call" | custom-call | flops 3449999872 | bytes 10800000 | tf_op jit(solution)/shard_map/head_blocks/pallas_call | solution.py:254
  61.1 2.6 %collective-permute-start.13 = (bf16[528,128]{1,0:T(8,128)(2,1)}, bf16[528,128]{1,0:T(8,128)(2,1)S(1)}, u32[]{:S(2)}, u32[]{:S(2)}) collective-permute-start(bf16[528,128]{1,0:T(8,128)(2,1)} %get-tuple-element.57), channel_id=1, source_target_pairs={{0,8},{1,9},{2,10},{3,11},{4,12},{5,13},{6,14},{7,15},{8,0},{9,1},... | collective-permute-start | bytes 405512 | tf_op jit(solution)/shard_map/ppermute | solution.py:356
  63.7 2.5 %collective-permute-start.14 = (bf16[528,128]{1,0:T(8,128)(2,1)}, bf16[528,128]{1,0:T(8,128)(2,1)}, u32[]{:S(2)}, u32[]{:S(2)}) collective-permute-start(bf16[528,128]{1,0:T(8,128)(2,1)} %get-tuple-element.58), channel_id=1, source_target_pairs={{0,4},{1,5},{2,6},{3,7},{4,8},{5,9},{6,10},{7,11},{8,12},{9,13},{1... | collective-permute-start | bytes 405512 | tf_op jit(solution)/shard_map/ppermute | solution.py:356
  67.7 3.4 %pair_sum.1 = (bf16[8,200,128]{2,1,0:T(8,128)(2,1)}, bf16[8,200,128]{2,1,0:T(8,128)(2,1)}, bf16[8,200,128]{2,1,0:T(8,128)(2,1)}, bf16[8,200,128]{2,1,0:T(8,128)(2,1)}) custom-call(s32[4]{0:T(128)} %pad_add_fusion.at.xi, bf16[8,200,512]{2,1,0:T(8,128)(2,1)} %get-tuple-element.42.mine, bf16[2,200,512]{2,1,0:T(8,128)(2,1)} %copy-done.4, ...), custom_call_target="tpu_custom_call" | custom-call | flops 1 | bytes 1 | tf_op jit(solution)/shard_map/pair_sum/pallas_call | solution.py:321
  71.3 1.5 %collective-permute-start.16 = (bf16[8,200,128]{2,1,0:T(8,128)(2,1)}, bf16[8,200,128]{2,1,0:T(8,128)(2,1)S(1)}, u32[]{:S(2)}, u32[]{:S(2)}) collective-permute-start(bf16[8,200,128]{2,1,0:T(8,128)(2,1)} %get-tuple-element.64), channel_id=1, source_target_pairs={{0,8},{1,9},{2,10},{3,11},{4,12},{5,13},{6,14},{7,15},{8,0},{9,1},... | collective-permute-start | bytes 1228808 | tf_op jit(solution)/shard_map/ppermute | solution.py:366
  72.8 2.1 %collective-permute-start.17 = (bf16[8,200,128]{2,1,0:T(8,128)(2,1)}, bf16[8,200,128]{2,1,0:T(8,128)(2,1)}, u32[]{:S(2)}, u32[]{:S(2)}) collective-permute-start(bf16[8,200,128]{2,1,0:T(8,128)(2,1)} %get-tuple-element.65), channel_id=1, source_target_pairs={{0,12},{1,13},{2,14},{3,15},{4,0},{5,1},{6,2},{7,3},{8,4},{9,5},{1... | collective-permute-start | bytes 1228808 | tf_op jit(solution)/shard_map/ppermute | solution.py:366
  75.6 8.6 %attention.1 = bf16[16,3,128,128]{3,2,1,0:T(8,128)(2,1)} custom-call(s32[4]{0:T(128)} %pad_add_fusion.at.xi, s32[8]{0:T(128)} %bitcast.53, bf16[16,3,128,128]{3,2,1,0:T(8,128)(2,1)} %copy-done.1, bf16[528,128]{1,0:T(8,128)(2,1)} %get-tuple-element.55.h0, bf16[528,128]{1,0:T(8,128)(2,1)} %copy-done.12, bf16[528,128]{1,0:T(8,128)(2,1)} %copy-done.13, ...), custom_call_target="tpu_custom_call" | custom-call | flops 10350000128 | bytes 32400000 | tf_op jit(solution)/shard_map/attention/pallas_call | solution.py:116
  84.2 5.9 %all-to-all-start.2 = ((bf16[16,3,128,128]{3,2,1,0:T(8,128)(2,1)}), bf16[16,3,128,128]{3,2,1,0:T(8,128)(2,1)S(1)}, u32[]{:S(2)}, u32[]{:S(2)}) async-start(bf16[16,3,128,128]{3,2,1,0:T(8,128)(2,1)} %attention.1), calls=%async_computation.2 | async-start | bytes 3145728 | tf_op jit(solution)/shard_map/all_to_all | solution.py:361
  90.9 5.2 %collective-permute-done.17 = bf16[8,200,128]{2,1,0:T(8,128)(2,1)} collective-permute-done((bf16[8,200,128]{2,1,0:T(8,128)(2,1)}, bf16[8,200,128]{2,1,0:T(8,128)(2,1)}, u32[]{:S(2)}, u32[]{:S(2)}) %collective-permute-start.17) | collective-permute-done | bytes 409632 | tf_op jit(solution)/shard_map/ppermute | solution.py:366
  98.6 4.8 %collective-permute-done.18 = bf16[4,200,128]{2,1,0:T(8,128)(2,1)S(1)} collective-permute-done((bf16[4,200,128]{2,1,0:T(8,128)(2,1)S(1)}, bf16[4,200,128]{2,1,0:T(8,128)(2,1)S(1)}, u32[]{:S(2)}, u32[]{:S(2)}) %collective-permute-start.18) | collective-permute-done | bytes 204832 | tf_op jit(solution)/shard_map/ppermute | solution.py:370
  103.4 3.3 %collective-permute-start.19 = (bf16[200,128]{1,0:T(8,128)(2,1)S(1)}, bf16[200,128]{1,0:T(8,128)(2,1)S(1)}, u32[]{:S(2)}, u32[]{:S(2)}) collective-permute-start(bf16[200,128]{1,0:T(8,128)(2,1)S(1)} %get-tuple-element.66), channel_id=1, source_target_pairs={{0,64},{16,80},{32,96},{48,112},{64,128},{80,144},{96,160},{112,17... | collective-permute-start | bytes 153608 | tf_op jit(solution)/shard_map/ppermute | solution.py:374
  106.7 5.0 %collective-permute-start.20 = (bf16[200,128]{1,0:T(8,128)(2,1)S(1)}, bf16[200,128]{1,0:T(8,128)(2,1)S(1)}, u32[]{:S(2)}, u32[]{:S(2)}) collective-permute-start(bf16[200,128]{1,0:T(8,128)(2,1)S(1)} %get-tuple-element.68), channel_id=1, source_target_pairs={{0,128},{16,144},{32,160},{48,176},{64,192},{80,208},{96,224},{112... | collective-permute-start | bytes 153608 | tf_op jit(solution)/shard_map/ppermute | solution.py:374
  111.6 2.7 %collective-permute-start.21 = (bf16[200,128]{1,0:T(8,128)(2,1)S(1)}, bf16[200,128]{1,0:T(8,128)(2,1)S(1)}, u32[]{:S(2)}, u32[]{:S(2)}) collective-permute-start(bf16[200,128]{1,0:T(8,128)(2,1)S(1)} %get-tuple-element.67), channel_id=1, source_target_pairs={{0,192},{16,208},{32,224},{48,240},{64,0},{80,16},{96,32},{112,48}... | collective-permute-start | bytes 153608 | tf_op jit(solution)/shard_map/ppermute | solution.py:374
  114.8 2.4 %collective-permute-done.21 = bf16[200,128]{1,0:T(8,128)(2,1)S(1)} collective-permute-done((bf16[200,128]{1,0:T(8,128)(2,1)S(1)}, bf16[200,128]{1,0:T(8,128)(2,1)S(1)}, u32[]{:S(2)}, u32[]{:S(2)}) %collective-permute-start.21) | collective-permute-done | bytes 51232 | tf_op jit(solution)/shard_map/ppermute | solution.py:374
  119.0 2.5 %unpack.1 = (bf16[128,2048]{1,0:T(8,128)(2,1)}, bf16[128,2048]{1,0:T(8,128)(2,1)}, bf16[128,2048]{1,0:T(8,128)(2,1)}) custom-call(bf16[16,3,128,128]{3,2,1,0:T(8,128)(2,1)} %copy-done), custom_call_target="tpu_custom_call" | custom-call | flops 1 | bytes 1 | tf_op jit(solution)/shard_map/unpack/pallas_call | solution.py:158
  (69 shorter events, 14.6 us)
Async XLA Ops:
  0.6 27.3 %collective-permute-start = (bf16[128,3200]{1,0:T(8,128)(2,1)}, bf16[128,3200]{1,0:T(8,128)(2,1)S(1)}, u32[]{:S(2)}, u32[]{:S(2)}) collective-permute-start(bf16[128,3200]{1,0:T(8,128)(2,1)} %bitcast.46), channel_id=1, source_target_pairs={{0,1},{1,2},{2,3},{3,0},{4,5},{5,6},{6,7},{7,4},{8,9},{9,10},{10,1... | collective-permute-start | bytes 2457608 | tf_op jit(solution)/shard_map/ppermute | solution.py:340
  0.9 27.0 %collective-permute-start.1 = (bf16[128,3200]{1,0:T(8,128)(2,1)}, bf16[128,3200]{1,0:T(8,128)(2,1)S(1)}, u32[]{:S(2)}, u32[]{:S(2)}) collective-permute-start(bf16[128,3200]{1,0:T(8,128)(2,1)} %bitcast.47), channel_id=1, source_target_pairs={{0,3},{1,0},{2,1},{3,2},{4,7},{5,4},{6,5},{7,6},{8,11},{9,8},{10,9... | collective-permute-start | bytes 2457608 | tf_op jit(solution)/shard_map/ppermute | solution.py:340
  2.7 25.2 %collective-permute-start.2 = (bf16[128,3200]{1,0:T(8,128)(2,1)}, bf16[128,3200]{1,0:T(8,128)(2,1)}, u32[]{:S(2)}, u32[]{:S(2)}) collective-permute-start(bf16[128,3200]{1,0:T(8,128)(2,1)} %refs_5_.1), channel_id=1, source_target_pairs={{0,4},{1,5},{2,6},{3,7},{4,8},{5,9},{6,10},{7,11},{8,12},{9,13},{1... | collective-permute-start | bytes 2457608 | tf_op jit(solution)/shard_map/ppermute | solution.py:341
  5.3 22.6 %collective-permute-start.3 = (bf16[64,3200]{1,0:T(8,128)(2,1)S(1)}, bf16[64,3200]{1,0:T(8,128)(2,1)S(1)}, u32[]{:S(2)}, u32[]{:S(2)}) collective-permute-start(bf16[64,3200]{1,0:T(8,128)(2,1)S(1)} %constant_dynamic-slice_fusion), channel_id=1, source_target_pairs={{0,8},{1,9},{2,10},{3,11},{4,12},{5,13},{6,14},{7,15},{8,0},{9,1},... | collective-permute-start | bytes 1228808 | tf_op jit(solution)/shard_map/ppermute | solution.py:342
  28.8 13.0 %collective-permute-start.4 = (bf16[64,3200]{1,0:T(8,128)(2,1)S(1)}, bf16[64,3200]{1,0:T(8,128)(2,1)}, u32[]{:S(2)}, u32[]{:S(2)}) collective-permute-start(bf16[64,3200]{1,0:T(8,128)(2,1)S(1)} %slice.6), channel_id=1, source_target_pairs={{0,1},{1,2},{2,3},{3,0},{4,5},{5,6},{6,7},{7,4},{8,9},{9,10},{10,1... | collective-permute-start | bytes 1228808 | tf_op jit(solution)/shard_map/ppermute | solution.py:348
  30.2 15.9 %collective-permute-start.5 = (bf16[64,3200]{1,0:T(8,128)(2,1)S(1)}, bf16[64,3200]{1,0:T(8,128)(2,1)}, u32[]{:S(2)}, u32[]{:S(2)}) collective-permute-start(bf16[64,3200]{1,0:T(8,128)(2,1)S(1)} %slice.7), channel_id=1, source_target_pairs={{0,3},{1,0},{2,1},{3,2},{4,7},{5,4},{6,5},{7,6},{8,11},{9,8},{10,9... | collective-permute-start | bytes 1228808 | tf_op jit(solution)/shard_map/ppermute | solution.py:348
  33.7 37.5 %all-to-all-start.1 = ((bf16[16,3,128,128]{3,2,1,0:T(8,128)(2,1)}), bf16[16,3,128,128]{3,2,1,0:T(8,128)(2,1)S(1)}, u32[]{:S(2)}, u32[]{:S(2)}) async-start(bf16[16,3,128,128]{3,2,1,0:T(8,128)(2,1)} %pack.1), calls=%async_computation.1 | async-start | bytes 3145728 | tf_op jit(solution)/shard_map/all_to_all | solution.py:350
  40.6 13.5 %collective-permute-start.10 = (bf16[128,3200]{1,0:T(8,128)(2,1)}, bf16[128,3200]{1,0:T(8,128)(2,1)}, u32[]{:S(2)}, u32[]{:S(2)}) collective-permute-start(bf16[128,3200]{1,0:T(8,128)(2,1)} %collective-permute-done.2.refs_6_), channel_id=1, source_target_pairs={{0,16},{16,0},{32,48},{48,32},{64,80},{80,64},{96,112},{112,96},{1... | collective-permute-start | bytes 2457608 | tf_op jit(solution)/shard_map/ppermute | solution.py:349
  41.2 12.5 %collective-permute-start.11 = (bf16[64,3200]{1,0:T(8,128)(2,1)}, bf16[64,3200]{1,0:T(8,128)(2,1)S(1)}, u32[]{:S(2)}, u32[]{:S(2)}) collective-permute-start(bf16[64,3200]{1,0:T(8,128)(2,1)} %copy-done.10), channel_id=1, source_target_pairs={{0,16},{16,0},{32,48},{48,32},{64,80},{80,64},{96,112},{112,96},{1... | collective-permute-start | bytes 1228808 | tf_op jit(solution)/shard_map/ppermute | solution.py:349
  53.0 8.1 %collective-permute-start.6 = (bf16[2,200,512]{2,1,0:T(8,128)(2,1)}, bf16[2,200,512]{2,1,0:T(8,128)(2,1)S(1)}, u32[]{:S(2)}, u32[]{:S(2)}) collective-permute-start(bf16[2,200,512]{2,1,0:T(8,128)(2,1)} %get-tuple-element.43), channel_id=1, source_target_pairs={{0,16},{16,0},{32,48},{48,32},{64,80},{80,64},{96,112},{112,96},{1... | collective-permute-start | bytes 1228808 | tf_op jit(solution)/shard_map/ppermute | solution.py:358
  53.1 10.6 %collective-permute-start.7 = (bf16[2,200,512]{2,1,0:T(8,128)(2,1)}, bf16[2,200,512]{2,1,0:T(8,128)(2,1)S(1)}, u32[]{:S(2)}, u32[]{:S(2)}) collective-permute-start(bf16[2,200,512]{2,1,0:T(8,128)(2,1)} %get-tuple-element.44), channel_id=1, source_target_pairs={{0,16},{16,0},{32,48},{48,32},{64,80},{80,64},{96,112},{112,96},{1... | collective-permute-start | bytes 1228808 | tf_op jit(solution)/shard_map/ppermute | solution.py:358
  53.6 12.5 %collective-permute-start.8 = (bf16[2,200,512]{2,1,0:T(8,128)(2,1)}, bf16[2,200,512]{2,1,0:T(8,128)(2,1)S(1)}, u32[]{:S(2)}, u32[]{:S(2)}) collective-permute-start(bf16[2,200,512]{2,1,0:T(8,128)(2,1)} %get-tuple-element.45), channel_id=1, source_target_pairs={{0,16},{16,0},{32,48},{48,32},{64,80},{80,64},{96,112},{112,96},{1... | collective-permute-start | bytes 1228808 | tf_op jit(solution)/shard_map/ppermute | solution.py:358
  53.7 12.4 %collective-permute-start.9 = (bf16[2,200,512]{2,1,0:T(8,128)(2,1)}, bf16[2,200,512]{2,1,0:T(8,128)(2,1)S(1)}, u32[]{:S(2)}, u32[]{:S(2)}) collective-permute-start(bf16[2,200,512]{2,1,0:T(8,128)(2,1)} %get-tuple-element.46), channel_id=1, source_target_pairs={{0,16},{16,0},{32,48},{48,32},{64,80},{80,64},{96,112},{112,96},{1... | collective-permute-start | bytes 1228808 | tf_op jit(solution)/shard_map/ppermute | solution.py:358
  61.0 11.9 %collective-permute-start.12 = (bf16[528,128]{1,0:T(8,128)(2,1)}, bf16[528,128]{1,0:T(8,128)(2,1)S(1)}, u32[]{:S(2)}, u32[]{:S(2)}) collective-permute-start(bf16[528,128]{1,0:T(8,128)(2,1)} %get-tuple-element.56), channel_id=1, source_target_pairs={{0,12},{1,13},{2,14},{3,15},{4,0},{5,1},{6,2},{7,3},{8,4},{9,5},{1... | collective-permute-start | bytes 405512 | tf_op jit(solution)/shard_map/ppermute | solution.py:356
  61.1 13.8 %collective-permute-start.13 = (bf16[528,128]{1,0:T(8,128)(2,1)}, bf16[528,128]{1,0:T(8,128)(2,1)S(1)}, u32[]{:S(2)}, u32[]{:S(2)}) collective-permute-start(bf16[528,128]{1,0:T(8,128)(2,1)} %get-tuple-element.57), channel_id=1, source_target_pairs={{0,8},{1,9},{2,10},{3,11},{4,12},{5,13},{6,14},{7,15},{8,0},{9,1},... | collective-permute-start | bytes 405512 | tf_op jit(solution)/shard_map/ppermute | solution.py:356
  63.7 11.2 %collective-permute-start.14 = (bf16[528,128]{1,0:T(8,128)(2,1)}, bf16[528,128]{1,0:T(8,128)(2,1)}, u32[]{:S(2)}, u32[]{:S(2)}) collective-permute-start(bf16[528,128]{1,0:T(8,128)(2,1)} %get-tuple-element.58), channel_id=1, source_target_pairs={{0,4},{1,5},{2,6},{3,7},{4,8},{5,9},{6,10},{7,11},{8,12},{9,13},{1... | collective-permute-start | bytes 405512 | tf_op jit(solution)/shard_map/ppermute | solution.py:356
  71.1 19.0 %collective-permute-start.15 = (bf16[8,200,128]{2,1,0:T(8,128)(2,1)}, bf16[8,200,128]{2,1,0:T(8,128)(2,1)S(1)}, u32[]{:S(2)}, u32[]{:S(2)}) collective-permute-start(bf16[8,200,128]{2,1,0:T(8,128)(2,1)} %get-tuple-element.63), channel_id=1, source_target_pairs={{0,4},{1,5},{2,6},{3,7},{4,8},{5,9},{6,10},{7,11},{8,12},{9,13},{1... | collective-permute-start | bytes 1228808 | tf_op jit(solution)/shard_map/ppermute | solution.py:366
  71.3 18.8 %collective-permute-start.16 = (bf16[8,200,128]{2,1,0:T(8,128)(2,1)}, bf16[8,200,128]{2,1,0:T(8,128)(2,1)S(1)}, u32[]{:S(2)}, u32[]{:S(2)}) collective-permute-start(bf16[8,200,128]{2,1,0:T(8,128)(2,1)} %get-tuple-element.64), channel_id=1, source_target_pairs={{0,8},{1,9},{2,10},{3,11},{4,12},{5,13},{6,14},{7,15},{8,0},{9,1},... | collective-permute-start | bytes 1228808 | tf_op jit(solution)/shard_map/ppermute | solution.py:366
  72.8 23.3 %collective-permute-start.17 = (bf16[8,200,128]{2,1,0:T(8,128)(2,1)}, bf16[8,200,128]{2,1,0:T(8,128)(2,1)}, u32[]{:S(2)}, u32[]{:S(2)}) collective-permute-start(bf16[8,200,128]{2,1,0:T(8,128)(2,1)} %get-tuple-element.65), channel_id=1, source_target_pairs={{0,12},{1,13},{2,14},{3,15},{4,0},{5,1},{6,2},{7,3},{8,4},{9,5},{1... | collective-permute-start | bytes 1228808 | tf_op jit(solution)/shard_map/ppermute | solution.py:366
  84.2 33.6 %all-to-all-start.2 = ((bf16[16,3,128,128]{3,2,1,0:T(8,128)(2,1)}), bf16[16,3,128,128]{3,2,1,0:T(8,128)(2,1)S(1)}, u32[]{:S(2)}, u32[]{:S(2)}) async-start(bf16[16,3,128,128]{3,2,1,0:T(8,128)(2,1)} %attention.1), calls=%async_computation.2 | async-start | bytes 3145728 | tf_op jit(solution)/shard_map/all_to_all | solution.py:361
  97.5 5.8 %collective-permute-start.18 = (bf16[4,200,128]{2,1,0:T(8,128)(2,1)S(1)}, bf16[4,200,128]{2,1,0:T(8,128)(2,1)S(1)}, u32[]{:S(2)}, u32[]{:S(2)}) collective-permute-start(bf16[4,200,128]{2,1,0:T(8,128)(2,1)S(1)} %fusion), channel_id=1, source_target_pairs={{0,32},{16,48},{32,0},{48,16},{64,96},{80,112},{96,64},{112,80},{1... | collective-permute-start | bytes 614408 | tf_op jit(solution)/shard_map/ppermute | solution.py:370
  103.4 11.0 %collective-permute-start.19 = (bf16[200,128]{1,0:T(8,128)(2,1)S(1)}, bf16[200,128]{1,0:T(8,128)(2,1)S(1)}, u32[]{:S(2)}, u32[]{:S(2)}) collective-permute-start(bf16[200,128]{1,0:T(8,128)(2,1)S(1)} %get-tuple-element.66), channel_id=1, source_target_pairs={{0,64},{16,80},{32,96},{48,112},{64,128},{80,144},{96,160},{112,17... | collective-permute-start | bytes 153608 | tf_op jit(solution)/shard_map/ppermute | solution.py:374
  106.7 8.1 %collective-permute-start.20 = (bf16[200,128]{1,0:T(8,128)(2,1)S(1)}, bf16[200,128]{1,0:T(8,128)(2,1)S(1)}, u32[]{:S(2)}, u32[]{:S(2)}) collective-permute-start(bf16[200,128]{1,0:T(8,128)(2,1)S(1)} %get-tuple-element.68), channel_id=1, source_target_pairs={{0,128},{16,144},{32,160},{48,176},{64,192},{80,208},{96,224},{112... | collective-permute-start | bytes 153608 | tf_op jit(solution)/shard_map/ppermute | solution.py:374
  111.6 5.5 %collective-permute-start.21 = (bf16[200,128]{1,0:T(8,128)(2,1)S(1)}, bf16[200,128]{1,0:T(8,128)(2,1)S(1)}, u32[]{:S(2)}, u32[]{:S(2)}) collective-permute-start(bf16[200,128]{1,0:T(8,128)(2,1)S(1)} %get-tuple-element.67), channel_id=1, source_target_pairs={{0,192},{16,208},{32,224},{48,240},{64,0},{80,16},{96,32},{112,48}... | collective-permute-start | bytes 153608 | tf_op jit(solution)/shard_map/ppermute | solution.py:374
  (14 other events, 42.4 us)

commit v4 on v3

--- a/solution.py
+++ b/solution.py
@@ -161,7 +161,7 @@
         out_shape=[jax.ShapeDtypeStruct((TOK, 16 * HEAD), BF)] * 3,
         in_specs=[pl.BlockSpec((16, 3, rows, HEAD), lambda i: (0, 0, i, 0))],
         out_specs=[pl.BlockSpec((rows, 16 * HEAD), lambda i: (i, 0))] * 3,
-        compiler_params=pltpu.CompilerParams(vmem_limit_bytes=60 * 1024 * 1024),
+        compiler_params=pltpu.CompilerParams(vmem_limit_bytes=63 * 1024 * 1024),
         cost_estimate=pl.CostEstimate(flops=1, bytes_accessed=1, transcendentals=0),
         name="unpack",
     )(grads)
@@ -210,8 +210,9 @@
     return [(g, y * TOK), (back, lax.rem(y + 3, 4) * TOK), (ahead, lax.rem(y + 1, 4) * TOK), (fa, far), (fb, far + 64)]
 
 
-def head_kernel(at, *refs):
-    g, (w, wa, wb, wc, wd, o), hs, (gs, ws, acc, gsem, wsem) = refs[:5], refs[5:11], refs[11:15], refs[15:]
+def block_kernel(at, *refs):
+    g, (w, wa, wb, wc, wd, o), (mine, *other), hs = refs[:5], refs[5:11], refs[11:16], refs[16:20]
+    gs, ws, term, acc, gsem, wsem = refs[20:]
     x, y, core = at[0], at[1], at[2]
     g_pieces = grad_pieces(y, *g)
     near = lax.select(core == 0, 1, 3)
@@ -222,14 +223,19 @@
         (wc, 2 * TOK + 64 * core),
         (wd, 2 * TOK + 64 * (1 - core)),
     ]
-    copies = [chunk_copies(w_pieces, ws, wsem, c) + chunk_copies(g_pieces, gs, gsem, c) for c in range(MODEL // CHUNK)]
-    for group in copies:
-        for copy in group:
+    g_copies = [chunk_copies(g_pieces, gs, gsem, c) for c in range(MODEL // CHUNK)]
+    w_copies = [chunk_copies(w_pieces, ws, wsem, c) for c in range(MODEL // CHUNK)]
+    for pair in zip(g_copies, w_copies):
+        for copy in pair[0] + pair[1]:
             copy.start()
-    for c, group in enumerate(copies):
-        for copy in group:
+    outs = o[...].reshape(4 * TOK, 4 * HEAD)
+    for c in range(MODEL // CHUNK):
+        cols = pl.ds(c * CHUNK, CHUNK)
+        for copy in g_copies[c]:
             copy.wait()
-        cols = pl.ds(c * CHUNK, CHUNK)
+        term[cols, :] = tn(gs[:, cols], outs)
+        for copy in w_copies[c]:
+            copy.wait()
         part = nt(gs[:, cols], ws[:, cols])
         if c == 0:
             acc[...] = part
@@ -245,66 +251,33 @@
             product = h.astype(F32) * o[j, :, own].astype(F32)
             lines.append(jnp.sum(product.T, axis=0, keepdims=True))
         hs[k][pl.ds(4 * TOK, 16), :] = three_terms(jnp.concatenate(lines, axis=0))
-
-
-def head_blocks(at, g, w, o):
+    for z in range(8):
+        mine[z] = term[pl.ds(pl.multiple_of(400 * z + 200 * core, 8), 200), :].astype(BF)
+        other[z // 2][z % 2] = term[pl.ds(pl.multiple_of(400 * z + 200 - 200 * core, 8), 200), :].astype(BF)
+
+
+def blocks(at, g, w, o):
     vm = pl.BlockSpec(memory_space=pltpu.VMEM)
     sm = pl.BlockSpec(memory_space=pltpu.SMEM)
     hbm = pl.BlockSpec(memory_space=pl.ANY)
-    return pl.pallas_call(
-        head_kernel,
-        out_shape=[jax.ShapeDtypeStruct((4 * TOK + 16, HEAD), BF)] * 4,
+    sizes = [(n, 200, 4 * HEAD) for n in (8, 2, 2, 2, 2)] + [(4 * TOK + 16, HEAD)] * 4
+    return pl.pallas_call(
+        block_kernel,
+        out_shape=[jax.ShapeDtypeStruct(size, BF) for size in sizes],
         in_specs=[sm] + [hbm] * 10 + [vm],
-        out_specs=[vm] * 4,
+        out_specs=[vm] * 9,
         scratch_shapes=[
             pltpu.VMEM((4 * TOK, MODEL), BF),
             pltpu.VMEM((4 * HEAD, MODEL), BF),
+            pltpu.VMEM((MODEL, 4 * HEAD), F32),
             pltpu.VMEM((4 * TOK, 4 * HEAD), F32),
             pltpu.SemaphoreType.DMA((MODEL // CHUNK, 5)),
             pltpu.SemaphoreType.DMA((MODEL // CHUNK, 5)),
         ],
         compiler_params=pltpu.CompilerParams(vmem_limit_bytes=60 * 1024 * 1024),
-        cost_estimate=pl.CostEstimate(flops=3450000000, bytes_accessed=10800000, transcendentals=0),
-        name="head_blocks",
+        cost_estimate=pl.CostEstimate(flops=10350000000, bytes_accessed=32400000, transcendentals=0),
+        name="blocks",
     )(at, *g, *w, o)
-
-
-def term_kernel(at, *refs):
-    g, (o, mine, *other, gs, acc, gsem) = refs[:5], refs[5:]
-    y, core = at[1], at[2]
-    g_pieces = grad_pieces(y, *g)
-    copies = [chunk_copies(g_pieces, gs, gsem, c) for c in range(MODEL // CHUNK)]
-    for group in copies:
-        for copy in group:
-            copy.start()
-    outs = o[...].reshape(4 * TOK, 4 * HEAD)
-    for c, group in enumerate(copies):
-        for copy in group:
-            copy.wait()
-        acc[pl.ds(c * CHUNK, CHUNK), :] = tn(gs[:, pl.ds(c * CHUNK, CHUNK)], outs)
-    for z in range(8):
-        mine[z] = acc[pl.ds(pl.multiple_of(400 * z + 200 * core, 8), 200), :].astype(BF)
-        other[z // 2][z % 2] = acc[pl.ds(pl.multiple_of(400 * z + 200 - 200 * core, 8), 200), :].astype(BF)
-
-
-def weight_term(at, g, o):
-    vm = pl.BlockSpec(memory_space=pltpu.VMEM)
-    sm = pl.BlockSpec(memory_space=pltpu.SMEM)
-    hbm = pl.BlockSpec(memory_space=pl.ANY)
-    return pl.pallas_call(
-        term_kernel,
-        out_shape=[jax.ShapeDtypeStruct((n, 200, 4 * HEAD), BF) for n in (8, 2, 2, 2, 2)],
-        in_specs=[sm] + [hbm] * 5 + [vm],
-        out_specs=[vm] * 5,
-        scratch_shapes=[
-            pltpu.VMEM((4 * TOK, MODEL), BF),
-            pltpu.VMEM((MODEL, 4 * HEAD), F32),
-            pltpu.SemaphoreType.DMA((MODEL // CHUNK, 5)),
-        ],
-        compiler_params=pltpu.CompilerParams(vmem_limit_bytes=60 * 1024 * 1024),
-        cost_estimate=pl.CostEstimate(flops=6900000000, bytes_accessed=21600000, transcendentals=0),
-        name="weight_term",
-    )(at, *g, o)
 
 
 def pair_kernel(at, mine, *refs):
@@ -350,10 +323,8 @@
     qkv = lax.all_to_all(pack(q, keys_in[0], values_in[0]), "seq", split_axis=0, concat_axis=0, tiled=True)
     g_pieces = (g, back, ahead, fa, fb)
 
-    mine, *other = weight_term(at, g_pieces, o_rows)
-    mine, at_later = after((mine, at))
-    heads = head_blocks(at_later, g_pieces, (out_weight, wa, wb, wc, wd), o_rows)
-    heads = [heads[0]] + [move(heads[k], "seq", XS[4 - k]) for k in (1, 2, 3)]
+    mine, *other, h0, h1, h2, h3 = blocks(at, g_pieces, (out_weight, wa, wb, wc, wd), o_rows)
+    heads = [h0] + [move(h, "seq", XS[4 - k]) for k, h in ((1, h1), (2, h2), (3, h3))]
 
     pairs = pair_sum(at, mine, *[move(part, "dp", CORES) for part in other])
     qkv, *pairs = after((qkv, *pairs))

time: 122 us -> 113 us (0.926)
  the two profiles are of different devices: /device:TPU:26 before, /device:TPU:2 now
where the time goes in v4:
time: 113 us; the launch traced here: 112 us
  starting transfers between devices  45.5 us (40%)
  Pallas kernels  30.5 us (27%)
  blocking collectives  17.7 us (16%)
  waiting for transfers between devices  12.7 us (11%)
  local copies, waits for them, and re-layouts  3.44 us (3%)
  other arithmetic  1.51 us (1%)
    all_to_all x1, blocking collectives, on_device(): lax.all_to_all(pack_out(saved_out[0]), 'seq', split_axis=0, concat_axis=0...  17.7 us
    pallas_call x1, Pallas kernels, blocks(): pl.pallas_call(block_kernel, out_shape=[jax.ShapeDtypeStruct(size, BF) fo...  10.8 us
    ppermute x3, starting transfers between devices, on_device(): last = last + move(part, 'dp', ZFAR[k]).astype(F32)  10.7 us
    pallas_call x1, Pallas kernels, attention(): pl.pallas_call(attention_kernel, out_shape=jax.ShapeDtypeStruct((16, 3, T...  9.09 us
    all_to_all x1, starting transfers between devices, on_device(): sent = lax.all_to_all(grads, 'seq', split_axis=0, concat_axis=0, tiled=True)  6.05 us
    ppermute x1, waiting for transfers between devices, on_device(): move(away, 'dp', ZNEAR).astype(F32)  5.01 us
    ppermute x3, starting transfers between devices, on_device(): total = total + move(pairs[k], 'seq', XS[k]).astype(F32)  4.98 us
    all_to_all x1, starting transfers between devices, on_device(): lax.all_to_all(pack(q, keys_in[0], values_in[0]), 'seq', split_axis=0, co...  4.94 us
  transfers between devices with their start and end apart: 24, of which 7 were waited for; matrix products, arithmetic and copies ran while one was open for 2% of the time, Pallas kernels for 25%

profile of v4, /device:TPU:2, one launch (start us, length us, event | category | flops | bytes accessed | tf_op | source)
XLA Modules:
  0.0 112.2 jit_solution(534308276546462753)
XLA Ops:
  0.6 1.7 %collective-permute-start = (bf16[128,3200]{1,0:T(8,128)(2,1)}, bf16[128,3200]{1,0:T(8,128)(2,1)S(1)}, u32[]{:S(2)}, u32[]{:S(2)}) collective-permute-start(bf16[128,3200]{1,0:T(8,128)(2,1)} %bitcast.46), channel_id=1, source_target_pairs={{0,1},{1,2},{2,3},{3,0},{4,5},{5,6},{6,7},{7,4},{8,9},{9,10},{10,1... | collective-permute-start | bytes 2457608 | tf_op jit(solution)/shard_map/ppermute | solution.py:313
  2.3 1.7 %collective-permute-start.1 = (bf16[128,3200]{1,0:T(8,128)(2,1)}, bf16[128,3200]{1,0:T(8,128)(2,1)S(1)}, u32[]{:S(2)}, u32[]{:S(2)}) collective-permute-start(bf16[128,3200]{1,0:T(8,128)(2,1)} %bitcast.47), channel_id=1, source_target_pairs={{0,3},{1,0},{2,1},{3,2},{4,7},{5,4},{6,5},{7,6},{8,11},{9,8},{10,9... | collective-permute-start | bytes 2457608 | tf_op jit(solution)/shard_map/ppermute | solution.py:313
  6.5 2.9 %collective-permute-start.3 = (bf16[64,3200]{1,0:T(8,128)(2,1)S(1)}, bf16[64,3200]{1,0:T(8,128)(2,1)S(1)}, u32[]{:S(2)}, u32[]{:S(2)}) collective-permute-start(bf16[64,3200]{1,0:T(8,128)(2,1)S(1)} %constant_dynamic-slice_fusion), channel_id=1, source_target_pairs={{0,8},{1,9},{2,10},{3,11},{4,12},{5,13},{6,14},{7,15},{8,0},{9,1},... | collective-permute-start | bytes 1228808 | tf_op jit(solution)/shard_map/ppermute | solution.py:315
  9.4 1.9 %pack_out.1 = bf16[4,128,512]{2,1,0:T(8,128)(2,1)} custom-call(bf16[128,2048]{1,0:T(8,128)(2,1)} %bitcast.42), custom_call_target="tpu_custom_call" | custom-call | flops 1 | bytes 1 | tf_op jit(solution)/shard_map/pack_out/pallas_call | solution.py:185
  11.4 17.7 %all_to_all.15.refs_10_ = bf16[4,128,512]{2,1,0:T(8,128)(2,1)} all-to-all(bf16[4,128,512]{2,1,0:T(8,128)(2,1)} %pack_out.1), channel_id=1, replica_groups={{0,1,2,3},{4,5,6,7},{8,9,10,11},{12,13,14,15},{16,17,18,19},{20,21,22,2..., dimensions={0} | all-to-all | bytes 1048576 | tf_op jit(solution)/shard_map/all_to_all | solution.py:316
  30.5 2.1 %collective-permute-start.5 = (bf16[64,3200]{1,0:T(8,128)(2,1)S(1)}, bf16[64,3200]{1,0:T(8,128)(2,1)}, u32[]{:S(2)}, u32[]{:S(2)}) collective-permute-start(bf16[64,3200]{1,0:T(8,128)(2,1)S(1)} %slice.7), channel_id=1, source_target_pairs={{0,3},{1,0},{2,1},{3,2},{4,7},{5,4},{6,5},{7,6},{8,11},{9,8},{10,9... | collective-permute-start | bytes 1228808 | tf_op jit(solution)/shard_map/ppermute | solution.py:321
  33.2 2.8 %pack.1 = bf16[16,3,128,128]{3,2,1,0:T(8,128)(2,1)} custom-call(bf16[128,2048]{1,0:T(8,128)(2,1)} %bitcast.43, bf16[128,2048]{1,0:T(8,128)(2,1)} %bitcast.44, bf16[128,2048]{1,0:T(8,128)(2,1)} %bitcast.45), custom_call_target="tpu_custom_call" | custom-call | flops 1150000 | bytes 3600 | tf_op jit(solution)/shard_map/pack/pallas_call | solution.py:138
  36.0 4.9 %all-to-all-start.1 = ((bf16[16,3,128,128]{3,2,1,0:T(8,128)(2,1)}), bf16[16,3,128,128]{3,2,1,0:T(8,128)(2,1)S(1)}, u32[]{:S(2)}, u32[]{:S(2)}) async-start(bf16[16,3,128,128]{3,2,1,0:T(8,128)(2,1)} %pack.1), calls=%async_computation.1 | async-start | bytes 3145728 | tf_op jit(solution)/shard_map/all_to_all | solution.py:323
  43.2 10.8 %blocks.1 = (bf16[8,200,512]{2,1,0:T(8,128)(2,1)}, bf16[2,200,512]{2,1,0:T(8,128)(2,1)}, bf16[2,200,512]{2,1,0:T(8,128)(2,1)}, bf16[2,200,512]{2,1,0:T(8,128)(2,...) custom-call(s32[4]{0:T(128)} %pad_add_fusion.at.xi, ...), custom_call_target="tpu_custom_call" | custom-call | flops 10350000128 | bytes 32400000 | tf_op jit(solution)/shard_map/blocks/pallas_call | solution.py:264
  56.1 2.1 %collective-permute-start.13 = (bf16[528,128]{1,0:T(8,128)(2,1)}, bf16[528,128]{1,0:T(8,128)(2,1)S(1)}, u32[]{:S(2)}, u32[]{:S(2)}) collective-permute-start(bf16[528,128]{1,0:T(8,128)(2,1)} %get-tuple-element.53), channel_id=1, source_target_pairs={{0,8},{1,9},{2,10},{3,11},{4,12},{5,13},{6,14},{7,15},{8,0},{9,1},... | collective-permute-start | bytes 405512 | tf_op jit(solution)/shard_map/ppermute | solution.py:327
  58.2 1.7 %collective-permute-start.14 = (bf16[528,128]{1,0:T(8,128)(2,1)}, bf16[528,128]{1,0:T(8,128)(2,1)}, u32[]{:S(2)}, u32[]{:S(2)}) collective-permute-start(bf16[528,128]{1,0:T(8,128)(2,1)} %get-tuple-element.54), channel_id=1, source_target_pairs={{0,4},{1,5},{2,6},{3,7},{4,8},{5,9},{6,10},{7,11},{8,12},{9,13},{1... | collective-permute-start | bytes 405512 | tf_op jit(solution)/shard_map/ppermute | solution.py:327
  60.8 3.4 %pair_sum.1 = (bf16[8,200,128]{2,1,0:T(8,128)(2,1)}, bf16[8,200,128]{2,1,0:T(8,128)(2,1)}, bf16[8,200,128]{2,1,0:T(8,128)(2,1)}, bf16[8,200,128]{2,1,0:T(8,128)(2,1)}) custom-call(s32[4]{0:T(128)} %pad_add_fusion.at.xi, bf16[8,200,512]{2,1,0:T(8,128)(2,1)} %get-tuple-element.41.mine, bf16[2,200,512]{2,1,0:T(8,128)(2,1)} %copy-done.4, ...), custom_call_target="tpu_custom_call" | custom-call | flops 1 | bytes 1 | tf_op jit(solution)/shard_map/pair_sum/pallas_call | solution.py:294
  64.2 2.5 %collective-permute-start.15 = (bf16[8,200,128]{2,1,0:T(8,128)(2,1)}, bf16[8,200,128]{2,1,0:T(8,128)(2,1)S(1)}, u32[]{:S(2)}, u32[]{:S(2)}) collective-permute-start(bf16[8,200,128]{2,1,0:T(8,128)(2,1)} %get-tuple-element.59), channel_id=1, source_target_pairs={{0,4},{1,5},{2,6},{3,7},{4,8},{5,9},{6,10},{7,11},{8,12},{9,13},{1... | collective-permute-start | bytes 1228808 | tf_op jit(solution)/shard_map/ppermute | solution.py:337
  66.7 2.5 %collective-permute-start.16 = (bf16[8,200,128]{2,1,0:T(8,128)(2,1)}, bf16[8,200,128]{2,1,0:T(8,128)(2,1)S(1)}, u32[]{:S(2)}, u32[]{:S(2)}) collective-permute-start(bf16[8,200,128]{2,1,0:T(8,128)(2,1)} %get-tuple-element.60), channel_id=1, source_target_pairs={{0,8},{1,9},{2,10},{3,11},{4,12},{5,13},{6,14},{7,15},{8,0},{9,1},... | collective-permute-start | bytes 1228808 | tf_op jit(solution)/shard_map/ppermute | solution.py:337
  70.3 9.1 %attention.1 = bf16[16,3,128,128]{3,2,1,0:T(8,128)(2,1)} custom-call(s32[4]{0:T(128)} %pad_add_fusion.at.xi, s32[8]{0:T(128)} %bitcast.52, bf16[16,3,128,128]{3,2,1,0:T(8,128)(2,1)} %copy-done, bf16[528,128]{1,0:T(8,128)(2,1)} %get-tuple-element.51.h0, bf16[528,128]{1,0:T(8,128)(2,1)} %copy-done.10, bf16[528,128]{1,0:T(8,128)(2,1)} %copy-done.11, ...), custom_call_target="tpu_custom_call" | custom-call | flops 10350000128 | bytes 32400000 | tf_op jit(solution)/shard_map/attention/pallas_call | solution.py:116
  79.4 6.0 %all-to-all-start.2 = ((bf16[16,3,128,128]{3,2,1,0:T(8,128)(2,1)}), bf16[16,3,128,128]{3,2,1,0:T(8,128)(2,1)}, u32[]{:S(2)}, u32[]{:S(2)}) async-start(bf16[16,3,128,128]{3,2,1,0:T(8,128)(2,1)} %attention.1), calls=%async_computation.2 | async-start | bytes 3145728 | tf_op jit(solution)/shard_map/all_to_all | solution.py:332
  85.4 1.6 %collective-permute-done.17 = bf16[8,200,128]{2,1,0:T(8,128)(2,1)S(1)} collective-permute-done((bf16[8,200,128]{2,1,0:T(8,128)(2,1)}, bf16[8,200,128]{2,1,0:T(8,128)(2,1)S(1)}, u32[]{:S(2)}, u32[]{:S(2)}) %collective-permute-start.17) | collective-permute-done | bytes 409632 | tf_op jit(solution)/shard_map/ppermute | solution.py:337
  87.3 2.2 %collective-permute-start.18 = (bf16[4,200,128]{2,1,0:T(8,128)(2,1)S(1)}, bf16[4,200,128]{2,1,0:T(8,128)(2,1)S(1)}, u32[]{:S(2)}, u32[]{:S(2)}) collective-permute-start(bf16[4,200,128]{2,1,0:T(8,128)(2,1)S(1)} %fusion), channel_id=1, source_target_pairs={{0,32},{16,48},{32,0},{48,16},{64,96},{80,112},{96,64},{112,80},{1... | collective-permute-start | bytes 614408 | tf_op jit(solution)/shard_map/ppermute | solution.py:341
  89.5 5.0 %collective-permute-done.18 = bf16[4,200,128]{2,1,0:T(8,128)(2,1)S(1)} collective-permute-done((bf16[4,200,128]{2,1,0:T(8,128)(2,1)S(1)}, bf16[4,200,128]{2,1,0:T(8,128)(2,1)S(1)}, u32[]{:S(2)}, u32[]{:S(2)}) %collective-permute-start.18) | collective-permute-done | bytes 204832 | tf_op jit(solution)/shard_map/ppermute | solution.py:341
  94.5 3.1 %collective-permute-start.19 = (bf16[200,128]{1,0:T(8,128)(2,1)S(1)}, bf16[200,128]{1,0:T(8,128)(2,1)S(1)}, u32[]{:S(2)}, u32[]{:S(2)}) collective-permute-start(bf16[200,128]{1,0:T(8,128)(2,1)S(1)} %get-tuple-element.62), channel_id=1, source_target_pairs={{0,64},{16,80},{32,96},{48,112},{64,128},{80,144},{96,160},{112,17... | collective-permute-start | bytes 153608 | tf_op jit(solution)/shard_map/ppermute | solution.py:345
  97.7 5.4 %collective-permute-start.20 = (bf16[200,128]{1,0:T(8,128)(2,1)S(1)}, bf16[200,128]{1,0:T(8,128)(2,1)S(1)}, u32[]{:S(2)}, u32[]{:S(2)}) collective-permute-start(bf16[200,128]{1,0:T(8,128)(2,1)S(1)} %get-tuple-element.64), channel_id=1, source_target_pairs={{0,128},{16,144},{32,160},{48,176},{64,192},{80,208},{96,224},{112... | collective-permute-start | bytes 153608 | tf_op jit(solution)/shard_map/ppermute | solution.py:345
  103.1 2.2 %collective-permute-start.21 = (bf16[200,128]{1,0:T(8,128)(2,1)S(1)}, bf16[200,128]{1,0:T(8,128)(2,1)S(1)}, u32[]{:S(2)}, u32[]{:S(2)}) collective-permute-start(bf16[200,128]{1,0:T(8,128)(2,1)S(1)} %get-tuple-element.63), channel_id=1, source_target_pairs={{0,192},{16,208},{32,224},{48,240},{64,0},{80,16},{96,32},{112,48}... | collective-permute-start | bytes 153608 | tf_op jit(solution)/shard_map/ppermute | solution.py:345
  105.8 3.2 %collective-permute-done.21 = bf16[200,128]{1,0:T(8,128)(2,1)S(1)} collective-permute-done((bf16[200,128]{1,0:T(8,128)(2,1)S(1)}, bf16[200,128]{1,0:T(8,128)(2,1)S(1)}, u32[]{:S(2)}, u32[]{:S(2)}) %collective-permute-start.21) | collective-permute-done | bytes 51232 | tf_op jit(solution)/shard_map/ppermute | solution.py:345
  109.7 2.5 %unpack.1 = (bf16[128,2048]{1,0:T(8,128)(2,1)}, bf16[128,2048]{1,0:T(8,128)(2,1)}, bf16[128,2048]{1,0:T(8,128)(2,1)}) custom-call(bf16[16,3,128,128]{3,2,1,0:T(8,128)(2,1)} %all-to-all-done.2.grads), custom_call_target="tpu_custom_call" | custom-call | flops 1 | bytes 1 | tf_op jit(solution)/shard_map/unpack/pallas_call | solution.py:158
  (64 shorter events, 12.3 us)
Async XLA Ops:
  0.6 28.5 %collective-permute-start = (bf16[128,3200]{1,0:T(8,128)(2,1)}, bf16[128,3200]{1,0:T(8,128)(2,1)S(1)}, u32[]{:S(2)}, u32[]{:S(2)}) collective-permute-start(bf16[128,3200]{1,0:T(8,128)(2,1)} %bitcast.46), channel_id=1, source_target_pairs={{0,1},{1,2},{2,3},{3,0},{4,5},{5,6},{6,7},{7,4},{8,9},{9,10},{10,1... | collective-permute-start | bytes 2457608 | tf_op jit(solution)/shard_map/ppermute | solution.py:313
  2.3 26.8 %collective-permute-start.1 = (bf16[128,3200]{1,0:T(8,128)(2,1)}, bf16[128,3200]{1,0:T(8,128)(2,1)S(1)}, u32[]{:S(2)}, u32[]{:S(2)}) collective-permute-start(bf16[128,3200]{1,0:T(8,128)(2,1)} %bitcast.47), channel_id=1, source_target_pairs={{0,3},{1,0},{2,1},{3,2},{4,7},{5,4},{6,5},{7,6},{8,11},{9,8},{10,9... | collective-permute-start | bytes 2457608 | tf_op jit(solution)/shard_map/ppermute | solution.py:313
  3.9 25.2 %collective-permute-start.2 = (bf16[128,3200]{1,0:T(8,128)(2,1)}, bf16[128,3200]{1,0:T(8,128)(2,1)}, u32[]{:S(2)}, u32[]{:S(2)}) collective-permute-start(bf16[128,3200]{1,0:T(8,128)(2,1)} %refs_5_.1), channel_id=1, source_target_pairs={{0,4},{1,5},{2,6},{3,7},{4,8},{5,9},{6,10},{7,11},{8,12},{9,13},{1... | collective-permute-start | bytes 2457608 | tf_op jit(solution)/shard_map/ppermute | solution.py:314
  6.5 22.6 %collective-permute-start.3 = (bf16[64,3200]{1,0:T(8,128)(2,1)S(1)}, bf16[64,3200]{1,0:T(8,128)(2,1)S(1)}, u32[]{:S(2)}, u32[]{:S(2)}) collective-permute-start(bf16[64,3200]{1,0:T(8,128)(2,1)S(1)} %constant_dynamic-slice_fusion), channel_id=1, source_target_pairs={{0,8},{1,9},{2,10},{3,11},{4,12},{5,13},{6,14},{7,15},{8,0},{9,1},... | collective-permute-start | bytes 1228808 | tf_op jit(solution)/shard_map/ppermute | solution.py:315
  29.1 13.3 %collective-permute-start.6 = (bf16[128,3200]{1,0:T(8,128)(2,1)}, bf16[128,3200]{1,0:T(8,128)(2,1)}, u32[]{:S(2)}, u32[]{:S(2)}) collective-permute-start(bf16[128,3200]{1,0:T(8,128)(2,1)} %collective-permute-done.2.refs_6_), channel_id=1, source_target_pairs={{0,16},{16,0},{32,48},{48,32},{64,80},{80,64},{96,112},{112,96},{1... | collective-permute-start | bytes 2457608 | tf_op jit(solution)/shard_map/ppermute | solution.py:322
  29.3 13.1 %collective-permute-start.4 = (bf16[64,3200]{1,0:T(8,128)(2,1)S(1)}, bf16[64,3200]{1,0:T(8,128)(2,1)S(1)}, u32[]{:S(2)}, u32[]{:S(2)}) collective-permute-start(bf16[64,3200]{1,0:T(8,128)(2,1)S(1)} %slice.6), channel_id=1, source_target_pairs={{0,1},{1,2},{2,3},{3,0},{4,5},{5,6},{6,7},{7,4},{8,9},{9,10},{10,1... | collective-permute-start | bytes 1228808 | tf_op jit(solution)/shard_map/ppermute | solution.py:321
  30.5 11.9 %collective-permute-start.5 = (bf16[64,3200]{1,0:T(8,128)(2,1)S(1)}, bf16[64,3200]{1,0:T(8,128)(2,1)}, u32[]{:S(2)}, u32[]{:S(2)}) collective-permute-start(bf16[64,3200]{1,0:T(8,128)(2,1)S(1)} %slice.7), channel_id=1, source_target_pairs={{0,3},{1,0},{2,1},{3,2},{4,7},{5,4},{6,5},{7,6},{8,11},{9,8},{10,9... | collective-permute-start | bytes 1228808 | tf_op jit(solution)/shard_map/ppermute | solution.py:321
  32.6 9.8 %collective-permute-start.7 = (bf16[64,3200]{1,0:T(8,128)(2,1)S(1)}, bf16[64,3200]{1,0:T(8,128)(2,1)}, u32[]{:S(2)}, u32[]{:S(2)}) collective-permute-start(bf16[64,3200]{1,0:T(8,128)(2,1)S(1)} %collective-permute-done.3.refs_8_), channel_id=1, source_target_pairs={{0,16},{16,0},{32,48},{48,32},{64,80},{80,64},{96,112},{112,96},{1... | collective-permute-start | bytes 1228808 | tf_op jit(solution)/shard_map/ppermute | solution.py:322
  36.0 28.1 %all-to-all-start.1 = ((bf16[16,3,128,128]{3,2,1,0:T(8,128)(2,1)}), bf16[16,3,128,128]{3,2,1,0:T(8,128)(2,1)S(1)}, u32[]{:S(2)}, u32[]{:S(2)}) async-start(bf16[16,3,128,128]{3,2,1,0:T(8,128)(2,1)} %pack.1), calls=%async_computation.1 | async-start | bytes 3145728 | tf_op jit(solution)/shard_map/all_to_all | solution.py:323
  54.0 2.0 %collective-permute-start.10 = (bf16[2,200,512]{2,1,0:T(8,128)(2,1)}, bf16[2,200,512]{2,1,0:T(8,128)(2,1)S(1)}, u32[]{:S(2)}, u32[]{:S(2)}) collective-permute-start(bf16[2,200,512]{2,1,0:T(8,128)(2,1)} %get-tuple-element.44), channel_id=1, source_target_pairs={{0,16},{16,0},{32,48},{48,32},{64,80},{80,64},{96,112},{112,96},{1... | collective-permute-start | bytes 1228808 | tf_op jit(solution)/shard_map/ppermute | solution.py:329
  54.1 4.1 %collective-permute-start.11 = (bf16[2,200,512]{2,1,0:T(8,128)(2,1)}, bf16[2,200,512]{2,1,0:T(8,128)(2,1)S(1)}, u32[]{:S(2)}, u32[]{:S(2)}) collective-permute-start(bf16[2,200,512]{2,1,0:T(8,128)(2,1)} %get-tuple-element.45), channel_id=1, source_target_pairs={{0,16},{16,0},{32,48},{48,32},{64,80},{80,64},{96,112},{112,96},{1... | collective-permute-start | bytes 1228808 | tf_op jit(solution)/shard_map/ppermute | solution.py:329
  54.6 5.3 %collective-permute-start.8 = (bf16[2,200,512]{2,1,0:T(8,128)(2,1)}, bf16[2,200,512]{2,1,0:T(8,128)(2,1)S(1)}, u32[]{:S(2)}, u32[]{:S(2)}) collective-permute-start(bf16[2,200,512]{2,1,0:T(8,128)(2,1)} %get-tuple-element.42), channel_id=1, source_target_pairs={{0,16},{16,0},{32,48},{48,32},{64,80},{80,64},{96,112},{112,96},{1... | collective-permute-start | bytes 1228808 | tf_op jit(solution)/shard_map/ppermute | solution.py:329
  54.7 5.2 %collective-permute-start.9 = (bf16[2,200,512]{2,1,0:T(8,128)(2,1)}, bf16[2,200,512]{2,1,0:T(8,128)(2,1)S(1)}, u32[]{:S(2)}, u32[]{:S(2)}) collective-permute-start(bf16[2,200,512]{2,1,0:T(8,128)(2,1)} %get-tuple-element.43), channel_id=1, source_target_pairs={{0,16},{16,0},{32,48},{48,32},{64,80},{80,64},{96,112},{112,96},{1... | collective-permute-start | bytes 1228808 | tf_op jit(solution)/shard_map/ppermute | solution.py:329
  55.1 14.1 %collective-permute-start.12 = (bf16[528,128]{1,0:T(8,128)(2,1)}, bf16[528,128]{1,0:T(8,128)(2,1)S(1)}, u32[]{:S(2)}, u32[]{:S(2)}) collective-permute-start(bf16[528,128]{1,0:T(8,128)(2,1)} %get-tuple-element.52), channel_id=1, source_target_pairs={{0,12},{1,13},{2,14},{3,15},{4,0},{5,1},{6,2},{7,3},{8,4},{9,5},{1... | collective-permute-start | bytes 405512 | tf_op jit(solution)/shard_map/ppermute | solution.py:327
  56.1 13.6 %collective-permute-start.13 = (bf16[528,128]{1,0:T(8,128)(2,1)}, bf16[528,128]{1,0:T(8,128)(2,1)S(1)}, u32[]{:S(2)}, u32[]{:S(2)}) collective-permute-start(bf16[528,128]{1,0:T(8,128)(2,1)} %get-tuple-element.53), channel_id=1, source_target_pairs={{0,8},{1,9},{2,10},{3,11},{4,12},{5,13},{6,14},{7,15},{8,0},{9,1},... | collective-permute-start | bytes 405512 | tf_op jit(solution)/shard_map/ppermute | solution.py:327
  58.2 11.5 %collective-permute-start.14 = (bf16[528,128]{1,0:T(8,128)(2,1)}, bf16[528,128]{1,0:T(8,128)(2,1)}, u32[]{:S(2)}, u32[]{:S(2)}) collective-permute-start(bf16[528,128]{1,0:T(8,128)(2,1)} %get-tuple-element.54), channel_id=1, source_target_pairs={{0,4},{1,5},{2,6},{3,7},{4,8},{5,9},{6,10},{7,11},{8,12},{9,13},{1... | collective-permute-start | bytes 405512 | tf_op jit(solution)/shard_map/ppermute | solution.py:327
  64.2 21.2 %collective-permute-start.15 = (bf16[8,200,128]{2,1,0:T(8,128)(2,1)}, bf16[8,200,128]{2,1,0:T(8,128)(2,1)S(1)}, u32[]{:S(2)}, u32[]{:S(2)}) collective-permute-start(bf16[8,200,128]{2,1,0:T(8,128)(2,1)} %get-tuple-element.59), channel_id=1, source_target_pairs={{0,4},{1,5},{2,6},{3,7},{4,8},{5,9},{6,10},{7,11},{8,12},{9,13},{1... | collective-permute-start | bytes 1228808 | tf_op jit(solution)/shard_map/ppermute | solution.py:337
  66.7 18.8 %collective-permute-start.16 = (bf16[8,200,128]{2,1,0:T(8,128)(2,1)}, bf16[8,200,128]{2,1,0:T(8,128)(2,1)S(1)}, u32[]{:S(2)}, u32[]{:S(2)}) collective-permute-start(bf16[8,200,128]{2,1,0:T(8,128)(2,1)} %get-tuple-element.60), channel_id=1, source_target_pairs={{0,8},{1,9},{2,10},{3,11},{4,12},{5,13},{6,14},{7,15},{8,0},{9,1},... | collective-permute-start | bytes 1228808 | tf_op jit(solution)/shard_map/ppermute | solution.py:337
  69.2 17.9 %collective-permute-start.17 = (bf16[8,200,128]{2,1,0:T(8,128)(2,1)}, bf16[8,200,128]{2,1,0:T(8,128)(2,1)S(1)}, u32[]{:S(2)}, u32[]{:S(2)}) collective-permute-start(bf16[8,200,128]{2,1,0:T(8,128)(2,1)} %get-tuple-element.61), channel_id=1, source_target_pairs={{0,12},{1,13},{2,14},{3,15},{4,0},{5,1},{6,2},{7,3},{8,4},{9,5},{1... | collective-permute-start | bytes 1228808 | tf_op jit(solution)/shard_map/ppermute | solution.py:337
  79.4 30.3 %all-to-all-start.2 = ((bf16[16,3,128,128]{3,2,1,0:T(8,128)(2,1)}), bf16[16,3,128,128]{3,2,1,0:T(8,128)(2,1)}, u32[]{:S(2)}, u32[]{:S(2)}) async-start(bf16[16,3,128,128]{3,2,1,0:T(8,128)(2,1)} %attention.1), calls=%async_computation.2 | async-start | bytes 3145728 | tf_op jit(solution)/shard_map/all_to_all | solution.py:332
  87.3 7.2 %collective-permute-start.18 = (bf16[4,200,128]{2,1,0:T(8,128)(2,1)S(1)}, bf16[4,200,128]{2,1,0:T(8,128)(2,1)S(1)}, u32[]{:S(2)}, u32[]{:S(2)}) collective-permute-start(bf16[4,200,128]{2,1,0:T(8,128)(2,1)S(1)} %fusion), channel_id=1, source_target_pairs={{0,32},{16,48},{32,0},{48,16},{64,96},{80,112},{96,64},{112,80},{1... | collective-permute-start | bytes 614408 | tf_op jit(solution)/shard_map/ppermute | solution.py:341
  94.5 10.7 %collective-permute-start.19 = (bf16[200,128]{1,0:T(8,128)(2,1)S(1)}, bf16[200,128]{1,0:T(8,128)(2,1)S(1)}, u32[]{:S(2)}, u32[]{:S(2)}) collective-permute-start(bf16[200,128]{1,0:T(8,128)(2,1)S(1)} %get-tuple-element.62), channel_id=1, source_target_pairs={{0,64},{16,80},{32,96},{48,112},{64,128},{80,144},{96,160},{112,17... | collective-permute-start | bytes 153608 | tf_op jit(solution)/shard_map/ppermute | solution.py:345
  97.7 8.2 %collective-permute-start.20 = (bf16[200,128]{1,0:T(8,128)(2,1)S(1)}, bf16[200,128]{1,0:T(8,128)(2,1)S(1)}, u32[]{:S(2)}, u32[]{:S(2)}) collective-permute-start(bf16[200,128]{1,0:T(8,128)(2,1)S(1)} %get-tuple-element.64), channel_id=1, source_target_pairs={{0,128},{16,144},{32,160},{48,176},{64,192},{80,208},{96,224},{112... | collective-permute-start | bytes 153608 | tf_op jit(solution)/shard_map/ppermute | solution.py:345
  103.1 5.9 %collective-permute-start.21 = (bf16[200,128]{1,0:T(8,128)(2,1)S(1)}, bf16[200,128]{1,0:T(8,128)(2,1)S(1)}, u32[]{:S(2)}, u32[]{:S(2)}) collective-permute-start(bf16[200,128]{1,0:T(8,128)(2,1)S(1)} %get-tuple-element.63), channel_id=1, source_target_pairs={{0,192},{16,208},{32,224},{48,240},{64,0},{80,16},{96,32},{112,48}... | collective-permute-start | bytes 153608 | tf_op jit(solution)/shard_map/ppermute | solution.py:345
  (12 other events, 49.7 us)

commit v5 on v4

--- a/solution.py
+++ b/solution.py
@@ -119,7 +119,7 @@
         in_specs=[sm, sm] + [vm] * 5,
         out_specs=vm,
         scratch_shapes=[pltpu.VMEM((PACK + IMG, HEAD), BF)] * 4 + [pltpu.VMEM((24, HEAD), F32)] + [pltpu.VMEM((PACK + IMG, HEAD), BF)] * 3,
-        compiler_params=pltpu.CompilerParams(vmem_limit_bytes=60 * 1024 * 1024),
+        compiler_params=pltpu.CompilerParams(vmem_limit_bytes=32 * 1024 * 1024),
         cost_estimate=pl.CostEstimate(flops=10350000000, bytes_accessed=32400000, transcendentals=0),
         name="attention",
     )(xi, units, qkv, *hs)
@@ -212,7 +212,7 @@
 
 def block_kernel(at, *refs):
     g, (w, wa, wb, wc, wd, o), (mine, *other), hs = refs[:5], refs[5:11], refs[11:16], refs[16:20]
-    gs, ws, term, acc, gsem, wsem = refs[20:]
+    gs, ws, term, staged, acc, gsem, wsem, osem = refs[20:]
     x, y, core = at[0], at[1], at[2]
     g_pieces = grad_pieces(y, *g)
     near = lax.select(core == 0, 1, 3)
@@ -234,6 +234,13 @@
         for copy in g_copies[c]:
             copy.wait()
         term[cols, :] = tn(gs[:, cols], outs)
+        for m in range(CHUNK * c // 200, CHUNK * (c + 1) // 200):
+            staged[m] = term[pl.ds(200 * m, 200), :].astype(BF)
+            z = m // 2
+            inside = staged.at[m], mine.at[z], osem.at[m]
+            outside = staged.at[m], other[z // 2].at[z % 2], osem.at[m]
+            pl.when(core == m % 2)(lambda refs=inside: pltpu.make_async_copy(*refs).start())
+            pl.when(core != m % 2)(lambda refs=outside: pltpu.make_async_copy(*refs).start())
         for copy in w_copies[c]:
             copy.wait()
         part = nt(gs[:, cols], ws[:, cols])
@@ -251,9 +258,8 @@
             product = h.astype(F32) * o[j, :, own].astype(F32)
             lines.append(jnp.sum(product.T, axis=0, keepdims=True))
         hs[k][pl.ds(4 * TOK, 16), :] = three_terms(jnp.concatenate(lines, axis=0))
-    for z in range(8):
-        mine[z] = term[pl.ds(pl.multiple_of(400 * z + 200 * core, 8), 200), :].astype(BF)
-        other[z // 2][z % 2] = term[pl.ds(pl.multiple_of(400 * z + 200 - 200 * core, 8), 200), :].astype(BF)
+    for m in range(16):
+        pltpu.make_async_copy(staged.at[m], mine.at[m // 2], osem.at[m]).wait()
 
 
 def blocks(at, g, w, o):
@@ -265,14 +271,16 @@
         block_kernel,
         out_shape=[jax.ShapeDtypeStruct(size, BF) for size in sizes],
         in_specs=[sm] + [hbm] * 10 + [vm],
-        out_specs=[vm] * 9,
+        out_specs=[hbm] * 5 + [vm] * 4,
         scratch_shapes=[
             pltpu.VMEM((4 * TOK, MODEL), BF),
             pltpu.VMEM((4 * HEAD, MODEL), BF),
             pltpu.VMEM((MODEL, 4 * HEAD), F32),
+            pltpu.VMEM((16, 200, 4 * HEAD), BF),
             pltpu.VMEM((4 * TOK, 4 * HEAD), F32),
             pltpu.SemaphoreType.DMA((MODEL // CHUNK, 5)),
             pltpu.SemaphoreType.DMA((MODEL // CHUNK, 5)),
+            pltpu.SemaphoreType.DMA((16,)),
         ],
         compiler_params=pltpu.CompilerParams(vmem_limit_bytes=60 * 1024 * 1024),
         cost_estimate=pl.CostEstimate(flops=10350000000, bytes_accessed=32400000, transcendentals=0),
@@ -327,7 +335,7 @@
     heads = [h0] + [move(h, "seq", XS[4 - k]) for k, h in ((1, h1), (2, h2), (3, h3))]
 
     pairs = pair_sum(at, mine, *[move(part, "dp", CORES) for part in other])
-    qkv, *pairs = after((qkv, *pairs))
+    qkv, *_ = after((qkv, *pairs))
     grads = attention(at, image_units[0], qkv, heads)
     sent = lax.all_to_all(grads, "seq", split_axis=0, concat_axis=0, tiled=True)
     query_grad, key_grad, value_grad = unpack(sent)
@@ -339,10 +347,12 @@
     bit, quarter = lax.rem(z, 2), lax.div(z, 2)
     away = lax.dynamic_index_in_dim(total, 1 - bit, 1, keepdims=False).astype(BF)
     total = lax.dynamic_index_in_dim(total, bit, 1, keepdims=False) + move(away, "dp", ZNEAR).astype(F32)
-    last = lax.dynamic_index_in_dim(total, quarter, 0, keepdims=False)
+    parts = [lax.dynamic_index_in_dim(total, quarter, 0, keepdims=False)]
     for k in (1, 2, 3):
         part = lax.dynamic_index_in_dim(total, lax.rem(quarter + k, 4), 0, keepdims=False).astype(BF)
-        last = last + move(part, "dp", ZFAR[k]).astype(F32)
+        parts.append(move(part, "dp", ZFAR[k]))
+    *parts, query_grad, key_grad, value_grad = after((*parts, query_grad, key_grad, value_grad))
+    last = sum([part.astype(F32) for part in parts[1:]], parts[0])
     weight_grad = last.T * (1.0 / math.sqrt(PACK * 16))
     return query_grad[None], key_grad[None], value_grad[None], weight_grad
 

time: 113 us -> 110 us (0.973)
  Pallas kernels: 30.5 us -> 28.4 us
    ppermute x3, waiting for transfers between devices: 3.74 us -> 0.01 us  [on_device(): parts.append(move(part, 'dp', ZFAR[k]))]
    ppermute x3, waiting for transfers between devices: 1.61 us -> 4.11 us  [on_device(): total = total + move(pairs[k], 'seq', XS[k]).astype(F32)]
    pallas_call x1, Pallas kernels: 9.09 us -> 7.81 us  [attention(): pl.pallas_call(attention_kernel, out_shape=jax.ShapeDtypeStruct((16, 3, T...]
    ppermute x3, waiting for transfers between devices: 0.46 us -> 1.61 us  [on_device(): move(h, 'seq', XS[4 - k])]
  transfers between devices with their start and end apart: 24 -> 24, of which waited for: 7 -> 6; matrix products, arithmetic and copies ran while one was open for 2% -> 2% of each run, Pallas kernels for 25% -> 26%
where the time goes in v5:
time: 110 us; the launch traced here: 109 us
  starting transfers between devices  44.8 us (41%)
  Pallas kernels  28.4 us (26%)
  blocking collectives  17.7 us (16%)
  waiting for transfers between devices  12.7 us (12%)
  local copies, waits for them, and re-layouts  2.83 us (3%)
  other arithmetic  1.55 us (1%)
    all_to_all x1, blocking collectives, on_device(): lax.all_to_all(pack_out(saved_out[0]), 'seq', split_axis=0, concat_axis=0...  17.7 us
    ppermute x3, starting transfers between devices, on_device(): parts.append(move(part, 'dp', ZFAR[k]))  11.2 us
    pallas_call x1, Pallas kernels, blocks(): pl.pallas_call(block_kernel, out_shape=[jax.ShapeDtypeStruct(size, BF) fo...  9.92 us
    pallas_call x1, Pallas kernels, attention(): pl.pallas_call(attention_kernel, out_shape=jax.ShapeDtypeStruct((16, 3, T...  7.81 us
    all_to_all x1, starting transfers between devices, on_device(): sent = lax.all_to_all(grads, 'seq', split_axis=0, concat_axis=0, tiled=True)  5.61 us
    ppermute x1, waiting for transfers between devices, on_device(): move(away, 'dp', ZNEAR).astype(F32)  5.12 us
    all_to_all x1, starting transfers between devices, on_device(): lax.all_to_all(pack(q, keys_in[0], values_in[0]), 'seq', split_axis=0, co...  4.94 us
    ppermute x3, starting transfers between devices, on_device(): total = total + move(pairs[k], 'seq', XS[k]).astype(F32)  4.45 us
  transfers between devices with their start and end apart: 24, of which 6 were waited for; matrix products, arithmetic and copies ran while one was open for 2% of the time, Pallas kernels for 26%

profile of v5, /device:TPU:2, one launch (start us, length us, event | category | flops | bytes accessed | tf_op | source)
XLA Modules:
  0.0 108.9 jit_solution(8172283574262192465)
XLA Ops:
  0.6 1.7 %collective-permute-start = (bf16[128,3200]{1,0:T(8,128)(2,1)}, bf16[128,3200]{1,0:T(8,128)(2,1)S(1)}, u32[]{:S(2)}, u32[]{:S(2)}) collective-permute-start(bf16[128,3200]{1,0:T(8,128)(2,1)} %bitcast.39), channel_id=1, source_target_pairs={{0,1},{1,2},{2,3},{3,0},{4,5},{5,6},{6,7},{7,4},{8,9},{9,10},{10,1... | collective-permute-start | bytes 2457608 | tf_op jit(solution)/shard_map/ppermute | solution.py:321
  2.3 1.7 %collective-permute-start.1 = (bf16[128,3200]{1,0:T(8,128)(2,1)}, bf16[128,3200]{1,0:T(8,128)(2,1)S(1)}, u32[]{:S(2)}, u32[]{:S(2)}) collective-permute-start(bf16[128,3200]{1,0:T(8,128)(2,1)} %bitcast.40), channel_id=1, source_target_pairs={{0,3},{1,0},{2,1},{3,2},{4,7},{5,4},{6,5},{7,6},{8,11},{9,8},{10,9... | collective-permute-start | bytes 2457608 | tf_op jit(solution)/shard_map/ppermute | solution.py:321
  6.5 2.9 %collective-permute-start.3 = (bf16[64,3200]{1,0:T(8,128)(2,1)S(1)}, bf16[64,3200]{1,0:T(8,128)(2,1)S(1)}, u32[]{:S(2)}, u32[]{:S(2)}) collective-permute-start(bf16[64,3200]{1,0:T(8,128)(2,1)S(1)} %constant_dynamic-slice_fusion), channel_id=1, source_target_pairs={{0,8},{1,9},{2,10},{3,11},{4,12},{5,13},{6,14},{7,15},{8,0},{9,1},... | collective-permute-start | bytes 1228808 | tf_op jit(solution)/shard_map/ppermute | solution.py:323
  9.4 1.9 %pack_out.1 = bf16[4,128,512]{2,1,0:T(8,128)(2,1)} custom-call(bf16[128,2048]{1,0:T(8,128)(2,1)} %bitcast.35), custom_call_target="tpu_custom_call" | custom-call | flops 1 | bytes 1 | tf_op jit(solution)/shard_map/pack_out/pallas_call | solution.py:185
  11.4 17.7 %all_to_all.15.refs_10_ = bf16[4,128,512]{2,1,0:T(8,128)(2,1)} all-to-all(bf16[4,128,512]{2,1,0:T(8,128)(2,1)} %pack_out.1), channel_id=1, replica_groups={{0,1,2,3},{4,5,6,7},{8,9,10,11},{12,13,14,15},{16,17,18,19},{20,21,22,2..., dimensions={0} | all-to-all | bytes 1048576 | tf_op jit(solution)/shard_map/all_to_all | solution.py:324
  30.5 2.1 %collective-permute-start.5 = (bf16[64,3200]{1,0:T(8,128)(2,1)S(1)}, bf16[64,3200]{1,0:T(8,128)(2,1)}, u32[]{:S(2)}, u32[]{:S(2)}) collective-permute-start(bf16[64,3200]{1,0:T(8,128)(2,1)S(1)} %slice.7), channel_id=1, source_target_pairs={{0,3},{1,0},{2,1},{3,2},{4,7},{5,4},{6,5},{7,6},{8,11},{9,8},{10,9... | collective-permute-start | bytes 1228808 | tf_op jit(solution)/shard_map/ppermute | solution.py:329
  33.2 2.8 %pack.1 = bf16[16,3,128,128]{3,2,1,0:T(8,128)(2,1)} custom-call(bf16[128,2048]{1,0:T(8,128)(2,1)} %bitcast.36, bf16[128,2048]{1,0:T(8,128)(2,1)} %bitcast.37, bf16[128,2048]{1,0:T(8,128)(2,1)} %bitcast.38), custom_call_target="tpu_custom_call" | custom-call | flops 1150000 | bytes 3600 | tf_op jit(solution)/shard_map/pack/pallas_call | solution.py:138
  36.0 4.9 %all-to-all-start.1 = ((bf16[16,3,128,128]{3,2,1,0:T(8,128)(2,1)}), bf16[16,3,128,128]{3,2,1,0:T(8,128)(2,1)S(1)}, u32[]{:S(2)}, u32[]{:S(2)}) async-start(bf16[16,3,128,128]{3,2,1,0:T(8,128)(2,1)} %pack.1), calls=%async_computation.1 | async-start | bytes 3145728 | tf_op jit(solution)/shard_map/all_to_all | solution.py:331
  43.2 9.9 %blocks.1 = (bf16[8,200,512]{2,1,0:T(8,128)(2,1)}, bf16[2,200,512]{2,1,0:T(8,128)(2,1)}, bf16[2,200,512]{2,1,0:T(8,128)(2,1)}, bf16[2,200,512]{2,1,0:T(8,128)(2,...) custom-call(s32[4]{0:T(128)} %pad_add_fusion.at.xi, ...), custom_call_target="tpu_custom_call" | custom-call | flops 10350000128 | bytes 32400000 | tf_op jit(solution)/shard_map/blocks/pallas_call | solution.py:270
  55.2 2.1 %collective-permute-start.20 = (bf16[528,128]{1,0:T(8,128)(2,1)}, bf16[528,128]{1,0:T(8,128)(2,1)S(1)}, u32[]{:S(2)}, u32[]{:S(2)}) collective-permute-start(bf16[528,128]{1,0:T(8,128)(2,1)} %get-tuple-element.56), channel_id=1, source_target_pairs={{0,8},{1,9},{2,10},{3,11},{4,12},{5,13},{6,14},{7,15},{8,0},{9,1},... | collective-permute-start | bytes 405512 | tf_op jit(solution)/shard_map/ppermute | solution.py:335
  57.3 1.7 %collective-permute-start.21 = (bf16[528,128]{1,0:T(8,128)(2,1)}, bf16[528,128]{1,0:T(8,128)(2,1)S(1)}, u32[]{:S(2)}, u32[]{:S(2)}) collective-permute-start(bf16[528,128]{1,0:T(8,128)(2,1)} %get-tuple-element.57), channel_id=1, source_target_pairs={{0,4},{1,5},{2,6},{3,7},{4,8},{5,9},{6,10},{7,11},{8,12},{9,13},{1... | collective-permute-start | bytes 405512 | tf_op jit(solution)/shard_map/ppermute | solution.py:335
  59.9 3.4 %pair_sum.1 = (bf16[8,200,128]{2,1,0:T(8,128)(2,1)}, bf16[8,200,128]{2,1,0:T(8,128)(2,1)}, bf16[8,200,128]{2,1,0:T(8,128)(2,1)}, bf16[8,200,128]{2,1,0:T(8,128)(2,1)}) custom-call(s32[4]{0:T(128)} %pad_add_fusion.at.xi, bf16[8,200,512]{2,1,0:T(8,128)(2,1)} %get-tuple-element.43.mine, bf16[2,200,512]{2,1,0:T(8,128)(2,1)} %copy-done.6, ...), custom_call_target="tpu_custom_call" | custom-call | flops 1 | bytes 1 | tf_op jit(solution)/shard_map/pair_sum/pallas_call | solution.py:302
  63.6 2.1 %collective-permute-start.13 = (bf16[8,200,128]{2,1,0:T(8,128)(2,1)}, bf16[8,200,128]{2,1,0:T(8,128)(2,1)S(1)}, u32[]{:S(2)}, u32[]{:S(2)}) collective-permute-start(bf16[8,200,128]{2,1,0:T(8,128)(2,1)} %get-tuple-element.50), channel_id=1, source_target_pairs={{0,8},{1,9},{2,10},{3,11},{4,12},{5,13},{6,14},{7,15},{8,0},{9,1},... | collective-permute-start | bytes 1228808 | tf_op jit(solution)/shard_map/ppermute | solution.py:345
  65.7 2.1 %collective-permute-start.14 = (bf16[8,200,128]{2,1,0:T(8,128)(2,1)}, bf16[8,200,128]{2,1,0:T(8,128)(2,1)S(1)}, u32[]{:S(2)}, u32[]{:S(2)}) collective-permute-start(bf16[8,200,128]{2,1,0:T(8,128)(2,1)} %get-tuple-element.51), channel_id=1, source_target_pairs={{0,12},{1,13},{2,14},{3,15},{4,0},{5,1},{6,2},{7,3},{8,4},{9,5},{1... | collective-permute-start | bytes 1228808 | tf_op jit(solution)/shard_map/ppermute | solution.py:345
  67.8 1.6 %collective-permute-done.20.h2 = bf16[528,128]{1,0:T(8,128)(2,1)S(1)} collective-permute-done((bf16[528,128]{1,0:T(8,128)(2,1)}, bf16[528,128]{1,0:T(8,128)(2,1)S(1)}, u32[]{:S(2)}, u32[]{:S(2)}) %collective-permute-start.20) | collective-permute-done | bytes 135200 | tf_op jit(solution)/shard_map/ppermute | solution.py:335
  69.4 7.8 %attention.1 = bf16[16,3,128,128]{3,2,1,0:T(8,128)(2,1)} custom-call(s32[4]{0:T(128)S(1)} %copy-done, s32[8]{0:T(128)S(1)} %bitcast.32, bf16[16,3,128,128]{3,2,1,0:T(8,128)(2,1)S(1)} %all-to-all-done.1.qkv, bf16[528,128]{1,0:T(8,128)(2,1)S(1)} %copy-done.2, bf16[528,128]{1,0:T(8,128)(2,1)S(1)} %collective-permute-done.19.h1, ...), custom_call_target="tpu_custom_call" | custom-call | flops 10350000128 | bytes 32400000 | tf_op jit(solution)/shard_map/attention/pallas_call | solution.py:116
  77.2 5.6 %all-to-all-start.2 = ((bf16[16,3,128,128]{3,2,1,0:T(8,128)(2,1)}), bf16[16,3,128,128]{3,2,1,0:T(8,128)(2,1)}, u32[]{:S(2)}, u32[]{:S(2)}) async-start(bf16[16,3,128,128]{3,2,1,0:T(8,128)(2,1)} %attention.1), calls=%async_computation.2 | async-start | bytes 3145728 | tf_op jit(solution)/shard_map/all_to_all | solution.py:340
  83.8 3.1 %collective-permute-done.14 = bf16[8,200,128]{2,1,0:T(8,128)(2,1)S(1)} collective-permute-done((bf16[8,200,128]{2,1,0:T(8,128)(2,1)}, bf16[8,200,128]{2,1,0:T(8,128)(2,1)S(1)}, u32[]{:S(2)}, u32[]{:S(2)}) %collective-permute-start.14) | collective-permute-done | bytes 409632 | tf_op jit(solution)/shard_map/ppermute | solution.py:345
  87.2 2.0 %collective-permute-start.15 = (bf16[4,200,128]{2,1,0:T(8,128)(2,1)S(1)}, bf16[4,200,128]{2,1,0:T(8,128)(2,1)S(1)}, u32[]{:S(2)}, u32[]{:S(2)}) collective-permute-start(bf16[4,200,128]{2,1,0:T(8,128)(2,1)S(1)} %fusion), channel_id=1, source_target_pairs={{0,32},{16,48},{32,0},{48,16},{64,96},{80,112},{96,64},{112,80},{1... | collective-permute-start | bytes 614408 | tf_op jit(solution)/shard_map/ppermute | solution.py:349
  89.2 5.1 %collective-permute-done.15 = bf16[4,200,128]{2,1,0:T(8,128)(2,1)S(1)} collective-permute-done((bf16[4,200,128]{2,1,0:T(8,128)(2,1)S(1)}, bf16[4,200,128]{2,1,0:T(8,128)(2,1)S(1)}, u32[]{:S(2)}, u32[]{:S(2)}) %collective-permute-start.15) | collective-permute-done | bytes 204832 | tf_op jit(solution)/shard_map/ppermute | solution.py:349
  94.4 3.3 %collective-permute-start.16 = (bf16[200,128]{1,0:T(8,128)(2,1)S(1)}, bf16[200,128]{1,0:T(8,128)(2,1)S(1)}, u32[]{:S(2)}, u32[]{:S(2)}) collective-permute-start(bf16[200,128]{1,0:T(8,128)(2,1)S(1)} %get-tuple-element.70), channel_id=1, source_target_pairs={{0,64},{16,80},{32,96},{48,112},{64,128},{80,144},{96,160},{112,17... | collective-permute-start | bytes 153608 | tf_op jit(solution)/shard_map/ppermute | solution.py:353
  97.8 5.2 %collective-permute-start.17 = (bf16[200,128]{1,0:T(8,128)(2,1)S(1)}, bf16[200,128]{1,0:T(8,128)(2,1)S(1)}, u32[]{:S(2)}, u32[]{:S(2)}) collective-permute-start(bf16[200,128]{1,0:T(8,128)(2,1)S(1)} %get-tuple-element.69), channel_id=1, source_target_pairs={{0,128},{16,144},{32,160},{48,176},{64,192},{80,208},{96,224},{112... | collective-permute-start | bytes 153608 | tf_op jit(solution)/shard_map/ppermute | solution.py:353
  103.0 2.7 %collective-permute-start.18 = (bf16[200,128]{1,0:T(8,128)(2,1)S(1)}, bf16[200,128]{1,0:T(8,128)(2,1)S(1)}, u32[]{:S(2)}, u32[]{:S(2)}) collective-permute-start(bf16[200,128]{1,0:T(8,128)(2,1)S(1)} %get-tuple-element.68), channel_id=1, source_target_pairs={{0,192},{16,208},{32,224},{48,240},{64,0},{80,16},{96,32},{112,48}... | collective-permute-start | bytes 153608 | tf_op jit(solution)/shard_map/ppermute | solution.py:353
  105.7 2.5 %unpack.1 = (bf16[128,2048]{1,0:T(8,128)(2,1)}, bf16[128,2048]{1,0:T(8,128)(2,1)}, bf16[128,2048]{1,0:T(8,128)(2,1)}) custom-call(bf16[16,3,128,128]{3,2,1,0:T(8,128)(2,1)} %all-to-all-done.2.grads), custom_call_target="tpu_custom_call" | custom-call | flops 1 | bytes 1 | tf_op jit(solution)/shard_map/unpack/pallas_call | solution.py:158
  (65 shorter events, 12.0 us)
Async XLA Ops:
  0.6 28.5 %collective-permute-start = (bf16[128,3200]{1,0:T(8,128)(2,1)}, bf16[128,3200]{1,0:T(8,128)(2,1)S(1)}, u32[]{:S(2)}, u32[]{:S(2)}) collective-permute-start(bf16[128,3200]{1,0:T(8,128)(2,1)} %bitcast.39), channel_id=1, source_target_pairs={{0,1},{1,2},{2,3},{3,0},{4,5},{5,6},{6,7},{7,4},{8,9},{9,10},{10,1... | collective-permute-start | bytes 2457608 | tf_op jit(solution)/shard_map/ppermute | solution.py:321
  2.3 26.8 %collective-permute-start.1 = (bf16[128,3200]{1,0:T(8,128)(2,1)}, bf16[128,3200]{1,0:T(8,128)(2,1)S(1)}, u32[]{:S(2)}, u32[]{:S(2)}) collective-permute-start(bf16[128,3200]{1,0:T(8,128)(2,1)} %bitcast.40), channel_id=1, source_target_pairs={{0,3},{1,0},{2,1},{3,2},{4,7},{5,4},{6,5},{7,6},{8,11},{9,8},{10,9... | collective-permute-start | bytes 2457608 | tf_op jit(solution)/shard_map/ppermute | solution.py:321
  3.9 25.2 %collective-permute-start.2 = (bf16[128,3200]{1,0:T(8,128)(2,1)}, bf16[128,3200]{1,0:T(8,128)(2,1)}, u32[]{:S(2)}, u32[]{:S(2)}) collective-permute-start(bf16[128,3200]{1,0:T(8,128)(2,1)} %refs_5_.1), channel_id=1, source_target_pairs={{0,4},{1,5},{2,6},{3,7},{4,8},{5,9},{6,10},{7,11},{8,12},{9,13},{1... | collective-permute-start | bytes 2457608 | tf_op jit(solution)/shard_map/ppermute | solution.py:322
  6.5 22.6 %collective-permute-start.3 = (bf16[64,3200]{1,0:T(8,128)(2,1)S(1)}, bf16[64,3200]{1,0:T(8,128)(2,1)S(1)}, u32[]{:S(2)}, u32[]{:S(2)}) collective-permute-start(bf16[64,3200]{1,0:T(8,128)(2,1)S(1)} %constant_dynamic-slice_fusion), channel_id=1, source_target_pairs={{0,8},{1,9},{2,10},{3,11},{4,12},{5,13},{6,14},{7,15},{8,0},{9,1},... | collective-permute-start | bytes 1228808 | tf_op jit(solution)/shard_map/ppermute | solution.py:323
  29.1 13.3 %collective-permute-start.6 = (bf16[128,3200]{1,0:T(8,128)(2,1)}, bf16[128,3200]{1,0:T(8,128)(2,1)}, u32[]{:S(2)}, u32[]{:S(2)}) collective-permute-start(bf16[128,3200]{1,0:T(8,128)(2,1)} %collective-permute-done.2.refs_6_), channel_id=1, source_target_pairs={{0,16},{16,0},{32,48},{48,32},{64,80},{80,64},{96,112},{112,96},{1... | collective-permute-start | bytes 2457608 | tf_op jit(solution)/shard_map/ppermute | solution.py:330
  29.3 13.1 %collective-permute-start.4 = (bf16[64,3200]{1,0:T(8,128)(2,1)S(1)}, bf16[64,3200]{1,0:T(8,128)(2,1)S(1)}, u32[]{:S(2)}, u32[]{:S(2)}) collective-permute-start(bf16[64,3200]{1,0:T(8,128)(2,1)S(1)} %slice.6), channel_id=1, source_target_pairs={{0,1},{1,2},{2,3},{3,0},{4,5},{5,6},{6,7},{7,4},{8,9},{9,10},{10,1... | collective-permute-start | bytes 1228808 | tf_op jit(solution)/shard_map/ppermute | solution.py:329
  30.5 11.9 %collective-permute-start.5 = (bf16[64,3200]{1,0:T(8,128)(2,1)S(1)}, bf16[64,3200]{1,0:T(8,128)(2,1)}, u32[]{:S(2)}, u32[]{:S(2)}) collective-permute-start(bf16[64,3200]{1,0:T(8,128)(2,1)S(1)} %slice.7), channel_id=1, source_target_pairs={{0,3},{1,0},{2,1},{3,2},{4,7},{5,4},{6,5},{7,6},{8,11},{9,8},{10,9... | collective-permute-start | bytes 1228808 | tf_op jit(solution)/shard_map/ppermute | solution.py:329
  32.6 9.8 %collective-permute-start.7 = (bf16[64,3200]{1,0:T(8,128)(2,1)S(1)}, bf16[64,3200]{1,0:T(8,128)(2,1)}, u32[]{:S(2)}, u32[]{:S(2)}) collective-permute-start(bf16[64,3200]{1,0:T(8,128)(2,1)S(1)} %collective-permute-done.3.refs_8_), channel_id=1, source_target_pairs={{0,16},{16,0},{32,48},{48,32},{64,80},{80,64},{96,112},{112,96},{1... | collective-permute-start | bytes 1228808 | tf_op jit(solution)/shard_map/ppermute | solution.py:330
  36.0 29.7 %all-to-all-start.1 = ((bf16[16,3,128,128]{3,2,1,0:T(8,128)(2,1)}), bf16[16,3,128,128]{3,2,1,0:T(8,128)(2,1)S(1)}, u32[]{:S(2)}, u32[]{:S(2)}) async-start(bf16[16,3,128,128]{3,2,1,0:T(8,128)(2,1)} %pack.1), calls=%async_computation.1 | async-start | bytes 3145728 | tf_op jit(solution)/shard_map/all_to_all | solution.py:331
  53.1 2.0 %collective-permute-start.10 = (bf16[2,200,512]{2,1,0:T(8,128)(2,1)}, bf16[2,200,512]{2,1,0:T(8,128)(2,1)S(1)}, u32[]{:S(2)}, u32[]{:S(2)}) collective-permute-start(bf16[2,200,512]{2,1,0:T(8,128)(2,1)} %get-tuple-element.46), channel_id=1, source_target_pairs={{0,16},{16,0},{32,48},{48,32},{64,80},{80,64},{96,112},{112,96},{1... | collective-permute-start | bytes 1228808 | tf_op jit(solution)/shard_map/ppermute | solution.py:337
  53.2 4.1 %collective-permute-start.11 = (bf16[2,200,512]{2,1,0:T(8,128)(2,1)}, bf16[2,200,512]{2,1,0:T(8,128)(2,1)S(1)}, u32[]{:S(2)}, u32[]{:S(2)}) collective-permute-start(bf16[2,200,512]{2,1,0:T(8,128)(2,1)} %get-tuple-element.47), channel_id=1, source_target_pairs={{0,16},{16,0},{32,48},{48,32},{64,80},{80,64},{96,112},{112,96},{1... | collective-permute-start | bytes 1228808 | tf_op jit(solution)/shard_map/ppermute | solution.py:337
  53.7 5.3 %collective-permute-start.8 = (bf16[2,200,512]{2,1,0:T(8,128)(2,1)}, bf16[2,200,512]{2,1,0:T(8,128)(2,1)S(1)}, u32[]{:S(2)}, u32[]{:S(2)}) collective-permute-start(bf16[2,200,512]{2,1,0:T(8,128)(2,1)} %get-tuple-element.44), channel_id=1, source_target_pairs={{0,16},{16,0},{32,48},{48,32},{64,80},{80,64},{96,112},{112,96},{1... | collective-permute-start | bytes 1228808 | tf_op jit(solution)/shard_map/ppermute | solution.py:337
  53.8 5.2 %collective-permute-start.9 = (bf16[2,200,512]{2,1,0:T(8,128)(2,1)}, bf16[2,200,512]{2,1,0:T(8,128)(2,1)S(1)}, u32[]{:S(2)}, u32[]{:S(2)}) collective-permute-start(bf16[2,200,512]{2,1,0:T(8,128)(2,1)} %get-tuple-element.45), channel_id=1, source_target_pairs={{0,16},{16,0},{32,48},{48,32},{64,80},{80,64},{96,112},{112,96},{1... | collective-permute-start | bytes 1228808 | tf_op jit(solution)/shard_map/ppermute | solution.py:337
  54.2 11.5 %collective-permute-start.19 = (bf16[528,128]{1,0:T(8,128)(2,1)}, bf16[528,128]{1,0:T(8,128)(2,1)S(1)}, u32[]{:S(2)}, u32[]{:S(2)}) collective-permute-start(bf16[528,128]{1,0:T(8,128)(2,1)} %get-tuple-element.55), channel_id=1, source_target_pairs={{0,12},{1,13},{2,14},{3,15},{4,0},{5,1},{6,2},{7,3},{8,4},{9,5},{1... | collective-permute-start | bytes 405512 | tf_op jit(solution)/shard_map/ppermute | solution.py:335
  55.2 14.2 %collective-permute-start.20 = (bf16[528,128]{1,0:T(8,128)(2,1)}, bf16[528,128]{1,0:T(8,128)(2,1)S(1)}, u32[]{:S(2)}, u32[]{:S(2)}) collective-permute-start(bf16[528,128]{1,0:T(8,128)(2,1)} %get-tuple-element.56), channel_id=1, source_target_pairs={{0,8},{1,9},{2,10},{3,11},{4,12},{5,13},{6,14},{7,15},{8,0},{9,1},... | collective-permute-start | bytes 405512 | tf_op jit(solution)/shard_map/ppermute | solution.py:335
  57.3 12.1 %collective-permute-start.21 = (bf16[528,128]{1,0:T(8,128)(2,1)}, bf16[528,128]{1,0:T(8,128)(2,1)S(1)}, u32[]{:S(2)}, u32[]{:S(2)}) collective-permute-start(bf16[528,128]{1,0:T(8,128)(2,1)} %get-tuple-element.57), channel_id=1, source_target_pairs={{0,4},{1,5},{2,6},{3,7},{4,8},{5,9},{6,10},{7,11},{8,12},{9,13},{1... | collective-permute-start | bytes 405512 | tf_op jit(solution)/shard_map/ppermute | solution.py:335
  63.3 20.5 %collective-permute-start.12 = (bf16[8,200,128]{2,1,0:T(8,128)(2,1)}, bf16[8,200,128]{2,1,0:T(8,128)(2,1)S(1)}, u32[]{:S(2)}, u32[]{:S(2)}) collective-permute-start(bf16[8,200,128]{2,1,0:T(8,128)(2,1)} %get-tuple-element.49), channel_id=1, source_target_pairs={{0,4},{1,5},{2,6},{3,7},{4,8},{5,9},{6,10},{7,11},{8,12},{9,13},{1... | collective-permute-start | bytes 1228808 | tf_op jit(solution)/shard_map/ppermute | solution.py:345
  63.6 20.2 %collective-permute-start.13 = (bf16[8,200,128]{2,1,0:T(8,128)(2,1)}, bf16[8,200,128]{2,1,0:T(8,128)(2,1)S(1)}, u32[]{:S(2)}, u32[]{:S(2)}) collective-permute-start(bf16[8,200,128]{2,1,0:T(8,128)(2,1)} %get-tuple-element.50), channel_id=1, source_target_pairs={{0,8},{1,9},{2,10},{3,11},{4,12},{5,13},{6,14},{7,15},{8,0},{9,1},... | collective-permute-start | bytes 1228808 | tf_op jit(solution)/shard_map/ppermute | solution.py:345
  65.7 21.2 %collective-permute-start.14 = (bf16[8,200,128]{2,1,0:T(8,128)(2,1)}, bf16[8,200,128]{2,1,0:T(8,128)(2,1)S(1)}, u32[]{:S(2)}, u32[]{:S(2)}) collective-permute-start(bf16[8,200,128]{2,1,0:T(8,128)(2,1)} %get-tuple-element.51), channel_id=1, source_target_pairs={{0,12},{1,13},{2,14},{3,15},{4,0},{5,1},{6,2},{7,3},{8,4},{9,5},{1... | collective-permute-start | bytes 1228808 | tf_op jit(solution)/shard_map/ppermute | solution.py:345
  77.2 28.4 %all-to-all-start.2 = ((bf16[16,3,128,128]{3,2,1,0:T(8,128)(2,1)}), bf16[16,3,128,128]{3,2,1,0:T(8,128)(2,1)}, u32[]{:S(2)}, u32[]{:S(2)}) async-start(bf16[16,3,128,128]{3,2,1,0:T(8,128)(2,1)} %attention.1), calls=%async_computation.2 | async-start | bytes 3145728 | tf_op jit(solution)/shard_map/all_to_all | solution.py:340
  87.2 7.1 %collective-permute-start.15 = (bf16[4,200,128]{2,1,0:T(8,128)(2,1)S(1)}, bf16[4,200,128]{2,1,0:T(8,128)(2,1)S(1)}, u32[]{:S(2)}, u32[]{:S(2)}) collective-permute-start(bf16[4,200,128]{2,1,0:T(8,128)(2,1)S(1)} %fusion), channel_id=1, source_target_pairs={{0,32},{16,48},{32,0},{48,16},{64,96},{80,112},{96,64},{112,80},{1... | collective-permute-start | bytes 614408 | tf_op jit(solution)/shard_map/ppermute | solution.py:349
  94.4 13.7 %collective-permute-start.16 = (bf16[200,128]{1,0:T(8,128)(2,1)S(1)}, bf16[200,128]{1,0:T(8,128)(2,1)S(1)}, u32[]{:S(2)}, u32[]{:S(2)}) collective-permute-start(bf16[200,128]{1,0:T(8,128)(2,1)S(1)} %get-tuple-element.70), channel_id=1, source_target_pairs={{0,64},{16,80},{32,96},{48,112},{64,128},{80,144},{96,160},{112,17... | collective-permute-start | bytes 153608 | tf_op jit(solution)/shard_map/ppermute | solution.py:353
  97.8 10.4 %collective-permute-start.17 = (bf16[200,128]{1,0:T(8,128)(2,1)S(1)}, bf16[200,128]{1,0:T(8,128)(2,1)S(1)}, u32[]{:S(2)}, u32[]{:S(2)}) collective-permute-start(bf16[200,128]{1,0:T(8,128)(2,1)S(1)} %get-tuple-element.69), channel_id=1, source_target_pairs={{0,128},{16,144},{32,160},{48,176},{64,192},{80,208},{96,224},{112... | collective-permute-start | bytes 153608 | tf_op jit(solution)/shard_map/ppermute | solution.py:353
  103.0 5.2 %collective-permute-start.18 = (bf16[200,128]{1,0:T(8,128)(2,1)S(1)}, bf16[200,128]{1,0:T(8,128)(2,1)S(1)}, u32[]{:S(2)}, u32[]{:S(2)}) collective-permute-start(bf16[200,128]{1,0:T(8,128)(2,1)S(1)} %get-tuple-element.68), channel_id=1, source_target_pairs={{0,192},{16,208},{32,224},{48,240},{64,0},{80,16},{96,32},{112,48}... | collective-permute-start | bytes 153608 | tf_op jit(solution)/shard_map/ppermute | solution.py:353
  (12 other events, 75.1 us)

commit v6 on v5

--- a/solution.py
+++ b/solution.py
@@ -119,7 +119,7 @@
         in_specs=[sm, sm] + [vm] * 5,
         out_specs=vm,
         scratch_shapes=[pltpu.VMEM((PACK + IMG, HEAD), BF)] * 4 + [pltpu.VMEM((24, HEAD), F32)] + [pltpu.VMEM((PACK + IMG, HEAD), BF)] * 3,
-        compiler_params=pltpu.CompilerParams(vmem_limit_bytes=32 * 1024 * 1024),
+        compiler_params=pltpu.CompilerParams(vmem_limit_bytes=24 * 1024 * 1024),
         cost_estimate=pl.CostEstimate(flops=10350000000, bytes_accessed=32400000, transcendentals=0),
         name="attention",
     )(xi, units, qkv, *hs)
@@ -211,8 +211,8 @@
 
 
 def block_kernel(at, *refs):
-    g, (w, wa, wb, wc, wd, o), (mine, *other), hs = refs[:5], refs[5:11], refs[11:16], refs[16:20]
-    gs, ws, term, staged, acc, gsem, wsem, osem = refs[20:]
+    g, (w, wa, wb, wc, wd, o), (mine, *other), hs = refs[:5], refs[5:11], refs[11:14], refs[14:18]
+    gs, ws, term, staged, acc, gsem, wsem, osem = refs[18:]
     x, y, core = at[0], at[1], at[2]
     g_pieces = grad_pieces(y, *g)
     near = lax.select(core == 0, 1, 3)
@@ -238,7 +238,7 @@
             staged[m] = term[pl.ds(200 * m, 200), :].astype(BF)
             z = m // 2
             inside = staged.at[m], mine.at[z], osem.at[m]
-            outside = staged.at[m], other[z // 2].at[z % 2], osem.at[m]
+            outside = staged.at[m], other[z // 4].at[z % 4], osem.at[m]
             pl.when(core == m % 2)(lambda refs=inside: pltpu.make_async_copy(*refs).start())
             pl.when(core != m % 2)(lambda refs=outside: pltpu.make_async_copy(*refs).start())
         for copy in w_copies[c]:
@@ -266,12 +266,12 @@
     vm = pl.BlockSpec(memory_space=pltpu.VMEM)
     sm = pl.BlockSpec(memory_space=pltpu.SMEM)
     hbm = pl.BlockSpec(memory_space=pl.ANY)
-    sizes = [(n, 200, 4 * HEAD) for n in (8, 2, 2, 2, 2)] + [(4 * TOK + 16, HEAD)] * 4
+    sizes = [(n, 200, 4 * HEAD) for n in (8, 4, 4)] + [(4 * TOK + 16, HEAD)] * 4
     return pl.pallas_call(
         block_kernel,
         out_shape=[jax.ShapeDtypeStruct(size, BF) for size in sizes],
         in_specs=[sm] + [hbm] * 10 + [vm],
-        out_specs=[hbm] * 5 + [vm] * 4,
+        out_specs=[hbm] * 3 + [vm] * 4,
         scratch_shapes=[
             pltpu.VMEM((4 * TOK, MODEL), BF),
             pltpu.VMEM((4 * HEAD, MODEL), BF),
@@ -289,11 +289,11 @@
 
 
 def pair_kernel(at, mine, *refs):
-    other, outs = refs[:4], refs[4:]
+    other, outs = refs[:2], refs[2:]
     for k in range(4):
         cols = pl.ds(pl.multiple_of(lax.rem(at[0] + k, 4) * HEAD, HEAD), HEAD)
         for z in range(8):
-            outs[k][z] = (mine[z, :, cols].astype(F32) + other[z // 2][z % 2, :, cols].astype(F32)).astype(BF)
+            outs[k][z] = (mine[z, :, cols].astype(F32) + other[z // 4][z % 4, :, cols].astype(F32)).astype(BF)
 
 
 def pair_sum(at, mine, *other):
@@ -302,7 +302,7 @@
     return pl.pallas_call(
         pair_kernel,
         out_shape=[jax.ShapeDtypeStruct((8, 200, HEAD), BF)] * 4,
-        in_specs=[sm] + [vm] * 5,
+        in_specs=[sm] + [vm] * 3,
         out_specs=[vm] * 4,
         cost_estimate=pl.CostEstimate(flops=1, bytes_accessed=1, transcendentals=0),
         name="pair_sum",
@@ -324,7 +324,7 @@
     o_rows = lax.all_to_all(
         pack_out(saved_out[0]), "seq", split_axis=0, concat_axis=0, tiled=True, axis_index_groups=YGROUPS
     )
-    back, ahead, wa, wc, o_rows = after((back, ahead, wa, wc, o_rows))
+    back, ahead, wa, wc, o_rows, at = after((back, ahead, wa, wc, o_rows, at))
     q, fa, fb = after((queries[0], back[:64], ahead[64:]))
     fa, fb = move(fa, "seq", YS[1]), move(fb, "seq", YS[3])
     wb, wd = move(wa, "dp", CORES), move(wc, "dp", CORES)

time: 110 us -> 109 us (level)
  blocking collectives: 17.7 us -> 0 us
  waiting for transfers between devices: 12.7 us -> 26.4 us
  starting transfers between devices: 44.8 us -> 48.4 us
    all_to_all x1 -> x0, blocking collectives: 17.7 us -> none  [on_device(): lax.all_to_all(pack_out(saved_out[0]), 'seq', split_axis=0, concat_axis=0...]
    all_to_all x0 -> x1, waiting for transfers between devices: none -> 13.5 us  [on_device(): lax.all_to_all(pack_out(saved_out[0]), 'seq', split_axis=0, concat_axis=0...]
    all_to_all x0 -> x1, starting transfers between devices: none -> 3.47 us  [on_device(): lax.all_to_all(pack_out(saved_out[0]), 'seq', split_axis=0, concat_axis=0...]
  transfers between devices with their start and end apart: 24 -> 23, of which waited for: 6 -> 6; matrix products, arithmetic and copies ran while one was open for 2% -> 2% of each run, Pallas kernels for 26% -> 26%
where the time goes in v6:
time: 109 us; the launch traced here: 108 us
  starting transfers between devices  48.4 us (44%)
  Pallas kernels  28.5 us (26%)
  waiting for transfers between devices  26.4 us (24%)
  local copies, waits for them, and re-layouts  2.4 us (2%)
  other arithmetic  1.49 us (1%)
    all_to_all x1, waiting for transfers between devices, on_device(): lax.all_to_all(pack_out(saved_out[0]), 'seq', split_axis=0, concat_axis=0...  13.5 us
    ppermute x3, starting transfers between devices, on_device(): parts.append(move(part, 'dp', ZFAR[k]))  11.2 us
    pallas_call x1, Pallas kernels, blocks(): pl.pallas_call(block_kernel, out_shape=[jax.ShapeDtypeStruct(size, BF) fo...  9.95 us
    pallas_call x1, Pallas kernels, attention(): pl.pallas_call(attention_kernel, out_shape=jax.ShapeDtypeStruct((16, 3, T...  7.88 us
    all_to_all x1, starting transfers between devices, on_device(): sent = lax.all_to_all(grads, 'seq', split_axis=0, concat_axis=0, tiled=True)  5.7 us
    ppermute x1, waiting for transfers between devices, on_device(): move(away, 'dp', ZNEAR).astype(F32)  5.12 us
    all_to_all x1, starting transfers between devices, on_device(): lax.all_to_all(pack(q, keys_in[0], values_in[0]), 'seq', split_axis=0, co...  4.94 us
    ppermute x3, starting transfers between devices, on_device(): move(h, 'seq', XS[4 - k])  4.76 us
  transfers between devices with their start and end apart: 23, of which 6 were waited for; matrix products, arithmetic and copies ran while one was open for 2% of the time, Pallas kernels for 26%

profile of v6, /device:TPU:2, one launch (start us, length us, event | category | flops | bytes accessed | tf_op | source)
XLA Modules:
  0.0 108.0 jit_solution(11184342286799226455)
XLA Ops:
  2.3 1.7 %collective-permute-start.1 = (bf16[128,3200]{1,0:T(8,128)(2,1)}, bf16[128,3200]{1,0:T(8,128)(2,1)S(1)}, u32[]{:S(2)}, u32[]{:S(2)}) collective-permute-start(bf16[128,3200]{1,0:T(8,128)(2,1)} %bitcast.40), channel_id=1, source_target_pairs={{0,3},{1,0},{2,1},{3,2},{4,7},{5,4},{6,5},{7,6},{8,11},{9,8},{10,9... | collective-permute-start | bytes 2457608 | tf_op jit(solution)/shard_map/ppermute | solution.py:321
  6.5 2.9 %collective-permute-start.3 = (bf16[64,3200]{1,0:T(8,128)(2,1)S(1)}, bf16[64,3200]{1,0:T(8,128)(2,1)}, u32[]{:S(2)}, u32[]{:S(2)}) collective-permute-start(bf16[64,3200]{1,0:T(8,128)(2,1)S(1)} %constant_dynamic-slice_fusion), channel_id=1, source_target_pairs={{0,8},{1,9},{2,10},{3,11},{4,12},{5,13},{6,14},{7,15},{8,0},{9,1},... | collective-permute-start | bytes 1228808 | tf_op jit(solution)/shard_map/ppermute | solution.py:323
  9.4 1.9 %pack_out.1 = bf16[4,128,512]{2,1,0:T(8,128)(2,1)} custom-call(bf16[128,2048]{1,0:T(8,128)(2,1)} %bitcast.35), custom_call_target="tpu_custom_call" | custom-call | flops 1 | bytes 1 | tf_op jit(solution)/shard_map/pack_out/pallas_call | solution.py:185
  11.4 3.5 %all-to-all-start = ((bf16[4,128,512]{2,1,0:T(8,128)(2,1)}), bf16[4,128,512]{2,1,0:T(8,128)(2,1)S(1)}, u32[]{:S(2)}, u32[]{:S(2)}) async-start(bf16[4,128,512]{2,1,0:T(8,128)(2,1)} %pack_out.1), calls=%async_computation | async-start | bytes 1048576 | tf_op jit(solution)/shard_map/all_to_all | solution.py:324
  15.4 13.5 %all-to-all-done.refs_10_ = bf16[4,128,512]{2,1,0:T(8,128)(2,1)S(1)} async-done(((bf16[4,128,512]{2,1,0:T(8,128)(2,1)}), bf16[4,128,512]{2,1,0:T(8,128)(2,1)S(1)}, u32[]{:S(2)}, u32[]{:S(2)}) %all-to-all-start) | async-done | bytes 524320 | tf_op jit(solution)/shard_map/all_to_all | solution.py:324
  30.4 2.1 %collective-permute-start.5 = (bf16[64,3200]{1,0:T(8,128)(2,1)S(1)}, bf16[64,3200]{1,0:T(8,128)(2,1)}, u32[]{:S(2)}, u32[]{:S(2)}) collective-permute-start(bf16[64,3200]{1,0:T(8,128)(2,1)S(1)} %slice.7), channel_id=1, source_target_pairs={{0,3},{1,0},{2,1},{3,2},{4,7},{5,4},{6,5},{7,6},{8,11},{9,8},{10,9... | collective-permute-start | bytes 1228808 | tf_op jit(solution)/shard_map/ppermute | solution.py:329
  32.5 2.8 %pack.1 = bf16[16,3,128,128]{3,2,1,0:T(8,128)(2,1)} custom-call(bf16[128,2048]{1,0:T(8,128)(2,1)} %bitcast.36, bf16[128,2048]{1,0:T(8,128)(2,1)} %bitcast.37, bf16[128,2048]{1,0:T(8,128)(2,1)} %bitcast.38), custom_call_target="tpu_custom_call" | custom-call | flops 1150000 | bytes 3600 | tf_op jit(solution)/shard_map/pack/pallas_call | solution.py:138
  35.3 4.9 %all-to-all-start.1 = ((bf16[16,3,128,128]{3,2,1,0:T(8,128)(2,1)}), bf16[16,3,128,128]{3,2,1,0:T(8,128)(2,1)S(1)}, u32[]{:S(2)}, u32[]{:S(2)}) async-start(bf16[16,3,128,128]{3,2,1,0:T(8,128)(2,1)} %pack.1), calls=%async_computation.1 | async-start | bytes 3145728 | tf_op jit(solution)/shard_map/all_to_all | solution.py:331
  40.3 2.2 %collective-permute-done.4.refs_3_ = bf16[64,3200]{1,0:T(8,128)(2,1)} collective-permute-done((bf16[64,3200]{1,0:T(8,128)(2,1)S(1)}, bf16[64,3200]{1,0:T(8,128)(2,1)}, u32[]{:S(2)}, u32[]{:S(2)}) %collective-permute-start.4) | collective-permute-done | bytes 409632 | tf_op jit(solution)/shard_map/ppermute | solution.py:329
  42.5 9.9 %blocks.1 = (bf16[8,200,512]{2,1,0:T(8,128)(2,1)}, bf16[4,200,512]{2,1,0:T(8,128)(2,1)}, bf16[4,200,512]{2,1,0:T(8,128)(2,1)}, bf16[528,128]{1,0:T(8,128)(2,1)},...) custom-call(s32[4]{0:T(128)} %pad_add_fusion.at.xi, bf16[128,3200]{1,0:T(8,128)(2,1)} %bitcast.41, ...), custom_call_target="tpu_custom_call" | custom-call | flops 10350000128 | bytes 32400000 | tf_op jit(solution)/shard_map/blocks/pallas_call | solution.py:270
  53.6 2.4 %collective-permute-start.18 = (bf16[528,128]{1,0:T(8,128)(2,1)}, bf16[528,128]{1,0:T(8,128)(2,1)S(1)}, u32[]{:S(2)}, u32[]{:S(2)}) collective-permute-start(bf16[528,128]{1,0:T(8,128)(2,1)} %get-tuple-element.54), channel_id=1, source_target_pairs={{0,8},{1,9},{2,10},{3,11},{4,12},{5,13},{6,14},{7,15},{8,0},{9,1},... | collective-permute-start | bytes 405512 | tf_op jit(solution)/shard_map/ppermute | solution.py:335
  56.0 1.8 %collective-permute-start.19 = (bf16[528,128]{1,0:T(8,128)(2,1)}, bf16[528,128]{1,0:T(8,128)(2,1)S(1)}, u32[]{:S(2)}, u32[]{:S(2)}) collective-permute-start(bf16[528,128]{1,0:T(8,128)(2,1)} %get-tuple-element.55), channel_id=1, source_target_pairs={{0,4},{1,5},{2,6},{3,7},{4,8},{5,9},{6,10},{7,11},{8,12},{9,13},{1... | collective-permute-start | bytes 405512 | tf_op jit(solution)/shard_map/ppermute | solution.py:335
  59.0 3.5 %pair_sum.1 = (bf16[8,200,128]{2,1,0:T(8,128)(2,1)}, bf16[8,200,128]{2,1,0:T(8,128)(2,1)}, bf16[8,200,128]{2,1,0:T(8,128)(2,1)}, bf16[8,200,128]{2,1,0:T(8,128)(2,1)}) custom-call(s32[4]{0:T(128)} %pad_add_fusion.at.xi, bf16[8,200,512]{2,1,0:T(8,128)(2,1)} %get-tuple-element.43.mine, bf16[4,200,512]{2,1,0:T(8,128)(2,1)} %copy-done.3, ...), custom_call_target="tpu_custom_call" | custom-call | flops 1 | bytes 1 | tf_op jit(solution)/shard_map/pair_sum/pallas_call | solution.py:302
  62.5 2.3 %collective-permute-start.11 = (bf16[8,200,128]{2,1,0:T(8,128)(2,1)}, bf16[8,200,128]{2,1,0:T(8,128)(2,1)S(1)}, u32[]{:S(2)}, u32[]{:S(2)}) collective-permute-start(bf16[8,200,128]{2,1,0:T(8,128)(2,1)} %get-tuple-element.48), channel_id=1, source_target_pairs={{0,8},{1,9},{2,10},{3,11},{4,12},{5,13},{6,14},{7,15},{8,0},{9,1},... | collective-permute-start | bytes 1228808 | tf_op jit(solution)/shard_map/ppermute | solution.py:345
  64.8 2.3 %collective-permute-start.12 = (bf16[8,200,128]{2,1,0:T(8,128)(2,1)}, bf16[8,200,128]{2,1,0:T(8,128)(2,1)S(1)}, u32[]{:S(2)}, u32[]{:S(2)}) collective-permute-start(bf16[8,200,128]{2,1,0:T(8,128)(2,1)} %get-tuple-element.49), channel_id=1, source_target_pairs={{0,12},{1,13},{2,14},{3,15},{4,0},{5,1},{6,2},{7,3},{8,4},{9,5},{1... | collective-permute-start | bytes 1228808 | tf_op jit(solution)/shard_map/ppermute | solution.py:345
  68.6 7.9 %attention.1 = bf16[16,3,128,128]{3,2,1,0:T(8,128)(2,1)} custom-call(s32[4]{0:T(128)S(1)} %copy-done, s32[8]{0:T(128)S(1)} %bitcast.32, bf16[16,3,128,128]{3,2,1,0:T(8,128)(2,1)S(1)} %all-to-all-done.1.qkv, bf16[528,128]{1,0:T(8,128)(2,1)S(1)} %copy-done.2, bf16[528,128]{1,0:T(8,128)(2,1)S(1)} %collective-permute-done.17.h1, ...), custom_call_target="tpu_custom_call" | custom-call | flops 10350000128 | bytes 32400000 | tf_op jit(solution)/shard_map/attention/pallas_call | solution.py:116
  76.5 5.7 %all-to-all-start.2 = ((bf16[16,3,128,128]{3,2,1,0:T(8,128)(2,1)}), bf16[16,3,128,128]{3,2,1,0:T(8,128)(2,1)}, u32[]{:S(2)}, u32[]{:S(2)}) async-start(bf16[16,3,128,128]{3,2,1,0:T(8,128)(2,1)} %attention.1), calls=%async_computation.2 | async-start | bytes 3145728 | tf_op jit(solution)/shard_map/all_to_all | solution.py:340
  83.1 3.1 %collective-permute-done.12 = bf16[8,200,128]{2,1,0:T(8,128)(2,1)S(1)} collective-permute-done((bf16[8,200,128]{2,1,0:T(8,128)(2,1)}, bf16[8,200,128]{2,1,0:T(8,128)(2,1)S(1)}, u32[]{:S(2)}, u32[]{:S(2)}) %collective-permute-start.12) | collective-permute-done | bytes 409632 | tf_op jit(solution)/shard_map/ppermute | solution.py:345
  86.4 2.0 %collective-permute-start.13 = (bf16[4,200,128]{2,1,0:T(8,128)(2,1)S(1)}, bf16[4,200,128]{2,1,0:T(8,128)(2,1)S(1)}, u32[]{:S(2)}, u32[]{:S(2)}) collective-permute-start(bf16[4,200,128]{2,1,0:T(8,128)(2,1)S(1)} %fusion), channel_id=1, source_target_pairs={{0,32},{16,48},{32,0},{48,16},{64,96},{80,112},{96,64},{112,80},{1... | collective-permute-start | bytes 614408 | tf_op jit(solution)/shard_map/ppermute | solution.py:349
  88.4 5.1 %collective-permute-done.13 = bf16[4,200,128]{2,1,0:T(8,128)(2,1)S(1)} collective-permute-done((bf16[4,200,128]{2,1,0:T(8,128)(2,1)S(1)}, bf16[4,200,128]{2,1,0:T(8,128)(2,1)S(1)}, u32[]{:S(2)}, u32[]{:S(2)}) %collective-permute-start.13) | collective-permute-done | bytes 204832 | tf_op jit(solution)/shard_map/ppermute | solution.py:349
  93.6 3.3 %collective-permute-start.14 = (bf16[200,128]{1,0:T(8,128)(2,1)S(1)}, bf16[200,128]{1,0:T(8,128)(2,1)S(1)}, u32[]{:S(2)}, u32[]{:S(2)}) collective-permute-start(bf16[200,128]{1,0:T(8,128)(2,1)S(1)} %get-tuple-element.68), channel_id=1, source_target_pairs={{0,64},{16,80},{32,96},{48,112},{64,128},{80,144},{96,160},{112,17... | collective-permute-start | bytes 153608 | tf_op jit(solution)/shard_map/ppermute | solution.py:353
  97.0 5.2 %collective-permute-start.15 = (bf16[200,128]{1,0:T(8,128)(2,1)S(1)}, bf16[200,128]{1,0:T(8,128)(2,1)S(1)}, u32[]{:S(2)}, u32[]{:S(2)}) collective-permute-start(bf16[200,128]{1,0:T(8,128)(2,1)S(1)} %get-tuple-element.67), channel_id=1, source_target_pairs={{0,128},{16,144},{32,160},{48,176},{64,192},{80,208},{96,224},{112... | collective-permute-start | bytes 153608 | tf_op jit(solution)/shard_map/ppermute | solution.py:353
  102.2 2.7 %collective-permute-start.16 = (bf16[200,128]{1,0:T(8,128)(2,1)S(1)}, bf16[200,128]{1,0:T(8,128)(2,1)S(1)}, u32[]{:S(2)}, u32[]{:S(2)}) collective-permute-start(bf16[200,128]{1,0:T(8,128)(2,1)S(1)} %get-tuple-element.66), channel_id=1, source_target_pairs={{0,192},{16,208},{32,224},{48,240},{64,0},{80,16},{96,32},{112,48}... | collective-permute-start | bytes 153608 | tf_op jit(solution)/shard_map/ppermute | solution.py:353
  104.9 2.5 %unpack.1 = (bf16[128,2048]{1,0:T(8,128)(2,1)}, bf16[128,2048]{1,0:T(8,128)(2,1)}, bf16[128,2048]{1,0:T(8,128)(2,1)}) custom-call(bf16[16,3,128,128]{3,2,1,0:T(8,128)(2,1)} %all-to-all-done.2.grads), custom_call_target="tpu_custom_call" | custom-call | flops 1 | bytes 1 | tf_op jit(solution)/shard_map/unpack/pallas_call | solution.py:158
  (56 shorter events, 12.0 us)
Async XLA Ops:
  0.6 28.3 %collective-permute-start = (bf16[128,3200]{1,0:T(8,128)(2,1)}, bf16[128,3200]{1,0:T(8,128)(2,1)S(1)}, u32[]{:S(2)}, u32[]{:S(2)}) collective-permute-start(bf16[128,3200]{1,0:T(8,128)(2,1)} %bitcast.39), channel_id=1, source_target_pairs={{0,1},{1,2},{2,3},{3,0},{4,5},{5,6},{6,7},{7,4},{8,9},{9,10},{10,1... | collective-permute-start | bytes 2457608 | tf_op jit(solution)/shard_map/ppermute | solution.py:321
  2.3 26.7 %collective-permute-start.1 = (bf16[128,3200]{1,0:T(8,128)(2,1)}, bf16[128,3200]{1,0:T(8,128)(2,1)S(1)}, u32[]{:S(2)}, u32[]{:S(2)}) collective-permute-start(bf16[128,3200]{1,0:T(8,128)(2,1)} %bitcast.40), channel_id=1, source_target_pairs={{0,3},{1,0},{2,1},{3,2},{4,7},{5,4},{6,5},{7,6},{8,11},{9,8},{10,9... | collective-permute-start | bytes 2457608 | tf_op jit(solution)/shard_map/ppermute | solution.py:321
  3.9 25.1 %collective-permute-start.2 = (bf16[128,3200]{1,0:T(8,128)(2,1)}, bf16[128,3200]{1,0:T(8,128)(2,1)}, u32[]{:S(2)}, u32[]{:S(2)}) collective-permute-start(bf16[128,3200]{1,0:T(8,128)(2,1)} %refs_5_.1), channel_id=1, source_target_pairs={{0,4},{1,5},{2,6},{3,7},{4,8},{5,9},{6,10},{7,11},{8,12},{9,13},{1... | collective-permute-start | bytes 2457608 | tf_op jit(solution)/shard_map/ppermute | solution.py:322
  6.5 22.5 %collective-permute-start.3 = (bf16[64,3200]{1,0:T(8,128)(2,1)S(1)}, bf16[64,3200]{1,0:T(8,128)(2,1)}, u32[]{:S(2)}, u32[]{:S(2)}) collective-permute-start(bf16[64,3200]{1,0:T(8,128)(2,1)S(1)} %constant_dynamic-slice_fusion), channel_id=1, source_target_pairs={{0,8},{1,9},{2,10},{3,11},{4,12},{5,13},{6,14},{7,15},{8,0},{9,1},... | collective-permute-start | bytes 1228808 | tf_op jit(solution)/shard_map/ppermute | solution.py:323
  11.4 17.6 %all-to-all-start = ((bf16[4,128,512]{2,1,0:T(8,128)(2,1)}), bf16[4,128,512]{2,1,0:T(8,128)(2,1)S(1)}, u32[]{:S(2)}, u32[]{:S(2)}) async-start(bf16[4,128,512]{2,1,0:T(8,128)(2,1)} %pack_out.1), calls=%async_computation | async-start | bytes 1048576 | tf_op jit(solution)/shard_map/all_to_all | solution.py:324
  29.0 13.5 %copy-start.8 = (bf16[128,3200]{1,0:T(8,128)(2,1)}, bf16[128,3200]{1,0:T(8,128)(2,1)S(1)}, u32[]{:S(2)}) copy-start(bf16[128,3200]{1,0:T(8,128)(2,1)S(1)} %collective-permute-done.1.refs_2_) | copy-start | bytes 2457604
  29.0 13.4 %collective-permute-start.6 = (bf16[128,3200]{1,0:T(8,128)(2,1)}, bf16[128,3200]{1,0:T(8,128)(2,1)}, u32[]{:S(2)}, u32[]{:S(2)}) collective-permute-start(bf16[128,3200]{1,0:T(8,128)(2,1)} %collective-permute-done.2.refs_6_), channel_id=1, source_target_pairs={{0,16},{16,0},{32,48},{48,32},{64,80},{80,64},{96,112},{112,96},{1... | collective-permute-start | bytes 2457608 | tf_op jit(solution)/shard_map/ppermute | solution.py:330
  29.2 13.3 %collective-permute-start.4 = (bf16[64,3200]{1,0:T(8,128)(2,1)S(1)}, bf16[64,3200]{1,0:T(8,128)(2,1)}, u32[]{:S(2)}, u32[]{:S(2)}) collective-permute-start(bf16[64,3200]{1,0:T(8,128)(2,1)S(1)} %slice.6), channel_id=1, source_target_pairs={{0,1},{1,2},{2,3},{3,0},{4,5},{5,6},{6,7},{7,4},{8,9},{9,10},{10,1... | collective-permute-start | bytes 1228808 | tf_op jit(solution)/shard_map/ppermute | solution.py:329
  30.4 12.0 %collective-permute-start.5 = (bf16[64,3200]{1,0:T(8,128)(2,1)S(1)}, bf16[64,3200]{1,0:T(8,128)(2,1)}, u32[]{:S(2)}, u32[]{:S(2)}) collective-permute-start(bf16[64,3200]{1,0:T(8,128)(2,1)S(1)} %slice.7), channel_id=1, source_target_pairs={{0,3},{1,0},{2,1},{3,2},{4,7},{5,4},{6,5},{7,6},{8,11},{9,8},{10,9... | collective-permute-start | bytes 1228808 | tf_op jit(solution)/shard_map/ppermute | solution.py:329
  32.5 9.9 %collective-permute-start.7 = (bf16[64,3200]{1,0:T(8,128)(2,1)}, bf16[64,3200]{1,0:T(8,128)(2,1)}, u32[]{:S(2)}, u32[]{:S(2)}) collective-permute-start(bf16[64,3200]{1,0:T(8,128)(2,1)} %collective-permute-done.3.refs_8_), channel_id=1, source_target_pairs={{0,16},{16,0},{32,48},{48,32},{64,80},{80,64},{96,112},{112,96},{1... | collective-permute-start | bytes 1228808 | tf_op jit(solution)/shard_map/ppermute | solution.py:330
  35.3 29.4 %all-to-all-start.1 = ((bf16[16,3,128,128]{3,2,1,0:T(8,128)(2,1)}), bf16[16,3,128,128]{3,2,1,0:T(8,128)(2,1)S(1)}, u32[]{:S(2)}, u32[]{:S(2)}) async-start(bf16[16,3,128,128]{3,2,1,0:T(8,128)(2,1)} %pack.1), calls=%async_computation.1 | async-start | bytes 3145728 | tf_op jit(solution)/shard_map/all_to_all | solution.py:331
  52.4 5.4 %collective-permute-start.8 = (bf16[4,200,512]{2,1,0:T(8,128)(2,1)}, bf16[4,200,512]{2,1,0:T(8,128)(2,1)S(1)}, u32[]{:S(2)}, u32[]{:S(2)}) collective-permute-start(bf16[4,200,512]{2,1,0:T(8,128)(2,1)} %get-tuple-element.44), channel_id=1, source_target_pairs={{0,16},{16,0},{32,48},{48,32},{64,80},{80,64},{96,112},{112,96},{1... | collective-permute-start | bytes 2457608 | tf_op jit(solution)/shard_map/ppermute | solution.py:337
  52.5 5.3 %collective-permute-start.9 = (bf16[4,200,512]{2,1,0:T(8,128)(2,1)}, bf16[4,200,512]{2,1,0:T(8,128)(2,1)S(1)}, u32[]{:S(2)}, u32[]{:S(2)}) collective-permute-start(bf16[4,200,512]{2,1,0:T(8,128)(2,1)} %get-tuple-element.45), channel_id=1, source_target_pairs={{0,16},{16,0},{32,48},{48,32},{64,80},{80,64},{96,112},{112,96},{1... | collective-permute-start | bytes 2457608 | tf_op jit(solution)/shard_map/ppermute | solution.py:337
  53.0 11.7 %collective-permute-start.17 = (bf16[528,128]{1,0:T(8,128)(2,1)}, bf16[528,128]{1,0:T(8,128)(2,1)S(1)}, u32[]{:S(2)}, u32[]{:S(2)}) collective-permute-start(bf16[528,128]{1,0:T(8,128)(2,1)} %get-tuple-element.53), channel_id=1, source_target_pairs={{0,12},{1,13},{2,14},{3,15},{4,0},{5,1},{6,2},{7,3},{8,4},{9,5},{1... | collective-permute-start | bytes 405512 | tf_op jit(solution)/shard_map/ppermute | solution.py:335
  53.6 15.0 %collective-permute-start.18 = (bf16[528,128]{1,0:T(8,128)(2,1)}, bf16[528,128]{1,0:T(8,128)(2,1)S(1)}, u32[]{:S(2)}, u32[]{:S(2)}) collective-permute-start(bf16[528,128]{1,0:T(8,128)(2,1)} %get-tuple-element.54), channel_id=1, source_target_pairs={{0,8},{1,9},{2,10},{3,11},{4,12},{5,13},{6,14},{7,15},{8,0},{9,1},... | collective-permute-start | bytes 405512 | tf_op jit(solution)/shard_map/ppermute | solution.py:335
  56.0 12.6 %collective-permute-start.19 = (bf16[528,128]{1,0:T(8,128)(2,1)}, bf16[528,128]{1,0:T(8,128)(2,1)S(1)}, u32[]{:S(2)}, u32[]{:S(2)}) collective-permute-start(bf16[528,128]{1,0:T(8,128)(2,1)} %get-tuple-element.55), channel_id=1, source_target_pairs={{0,4},{1,5},{2,6},{3,7},{4,8},{5,9},{6,10},{7,11},{8,12},{9,13},{1... | collective-permute-start | bytes 405512 | tf_op jit(solution)/shard_map/ppermute | solution.py:335
  62.5 20.6 %collective-permute-start.10 = (bf16[8,200,128]{2,1,0:T(8,128)(2,1)}, bf16[8,200,128]{2,1,0:T(8,128)(2,1)S(1)}, u32[]{:S(2)}, u32[]{:S(2)}) collective-permute-start(bf16[8,200,128]{2,1,0:T(8,128)(2,1)} %get-tuple-element.47), channel_id=1, source_target_pairs={{0,4},{1,5},{2,6},{3,7},{4,8},{5,9},{6,10},{7,11},{8,12},{9,13},{1... | collective-permute-start | bytes 1228808 | tf_op jit(solution)/shard_map/ppermute | solution.py:345
  62.5 20.6 %collective-permute-start.11 = (bf16[8,200,128]{2,1,0:T(8,128)(2,1)}, bf16[8,200,128]{2,1,0:T(8,128)(2,1)S(1)}, u32[]{:S(2)}, u32[]{:S(2)}) collective-permute-start(bf16[8,200,128]{2,1,0:T(8,128)(2,1)} %get-tuple-element.48), channel_id=1, source_target_pairs={{0,8},{1,9},{2,10},{3,11},{4,12},{5,13},{6,14},{7,15},{8,0},{9,1},... | collective-permute-start | bytes 1228808 | tf_op jit(solution)/shard_map/ppermute | solution.py:345
  64.8 21.4 %collective-permute-start.12 = (bf16[8,200,128]{2,1,0:T(8,128)(2,1)}, bf16[8,200,128]{2,1,0:T(8,128)(2,1)S(1)}, u32[]{:S(2)}, u32[]{:S(2)}) collective-permute-start(bf16[8,200,128]{2,1,0:T(8,128)(2,1)} %get-tuple-element.49), channel_id=1, source_target_pairs={{0,12},{1,13},{2,14},{3,15},{4,0},{5,1},{6,2},{7,3},{8,4},{9,5},{1... | collective-permute-start | bytes 1228808 | tf_op jit(solution)/shard_map/ppermute | solution.py:345
  76.5 28.3 %all-to-all-start.2 = ((bf16[16,3,128,128]{3,2,1,0:T(8,128)(2,1)}), bf16[16,3,128,128]{3,2,1,0:T(8,128)(2,1)}, u32[]{:S(2)}, u32[]{:S(2)}) async-start(bf16[16,3,128,128]{3,2,1,0:T(8,128)(2,1)} %attention.1), calls=%async_computation.2 | async-start | bytes 3145728 | tf_op jit(solution)/shard_map/all_to_all | solution.py:340
  86.4 7.1 %collective-permute-start.13 = (bf16[4,200,128]{2,1,0:T(8,128)(2,1)S(1)}, bf16[4,200,128]{2,1,0:T(8,128)(2,1)S(1)}, u32[]{:S(2)}, u32[]{:S(2)}) collective-permute-start(bf16[4,200,128]{2,1,0:T(8,128)(2,1)S(1)} %fusion), channel_id=1, source_target_pairs={{0,32},{16,48},{32,0},{48,16},{64,96},{80,112},{96,64},{112,80},{1... | collective-permute-start | bytes 614408 | tf_op jit(solution)/shard_map/ppermute | solution.py:349
  93.6 13.7 %collective-permute-start.14 = (bf16[200,128]{1,0:T(8,128)(2,1)S(1)}, bf16[200,128]{1,0:T(8,128)(2,1)S(1)}, u32[]{:S(2)}, u32[]{:S(2)}) collective-permute-start(bf16[200,128]{1,0:T(8,128)(2,1)S(1)} %get-tuple-element.68), channel_id=1, source_target_pairs={{0,64},{16,80},{32,96},{48,112},{64,128},{80,144},{96,160},{112,17... | collective-permute-start | bytes 153608 | tf_op jit(solution)/shard_map/ppermute | solution.py:353
  97.0 10.4 %collective-permute-start.15 = (bf16[200,128]{1,0:T(8,128)(2,1)S(1)}, bf16[200,128]{1,0:T(8,128)(2,1)S(1)}, u32[]{:S(2)}, u32[]{:S(2)}) collective-permute-start(bf16[200,128]{1,0:T(8,128)(2,1)S(1)} %get-tuple-element.67), channel_id=1, source_target_pairs={{0,128},{16,144},{32,160},{48,176},{64,192},{80,208},{96,224},{112... | collective-permute-start | bytes 153608 | tf_op jit(solution)/shard_map/ppermute | solution.py:353
  102.2 5.2 %collective-permute-start.16 = (bf16[200,128]{1,0:T(8,128)(2,1)S(1)}, bf16[200,128]{1,0:T(8,128)(2,1)S(1)}, u32[]{:S(2)}, u32[]{:S(2)}) collective-permute-start(bf16[200,128]{1,0:T(8,128)(2,1)S(1)} %get-tuple-element.66), channel_id=1, source_target_pairs={{0,192},{16,208},{32,224},{48,240},{64,0},{80,16},{96,32},{112,48}... | collective-permute-start | bytes 153608 | tf_op jit(solution)/shard_map/ppermute | solution.py:353
  (8 other events, 53.4 us)

commit v7 on v6

--- a/solution.py
+++ b/solution.py
@@ -288,24 +288,24 @@
     )(at, *g, *w, o)
 
 
-def pair_kernel(at, mine, *refs):
+def pair_kernel(ks, at, mine, *refs):
     other, outs = refs[:2], refs[2:]
-    for k in range(4):
+    for n, k in enumerate(ks):
         cols = pl.ds(pl.multiple_of(lax.rem(at[0] + k, 4) * HEAD, HEAD), HEAD)
         for z in range(8):
-            outs[k][z] = (mine[z, :, cols].astype(F32) + other[z // 4][z % 4, :, cols].astype(F32)).astype(BF)
-
-
-def pair_sum(at, mine, *other):
+            outs[n][z] = (mine[z, :, cols].astype(F32) + other[z // 4][z % 4, :, cols].astype(F32)).astype(BF)
+
+
+def pair_sum(ks, at, mine, *other):
     vm = pl.BlockSpec(memory_space=pltpu.VMEM)
     sm = pl.BlockSpec(memory_space=pltpu.SMEM)
     return pl.pallas_call(
-        pair_kernel,
-        out_shape=[jax.ShapeDtypeStruct((8, 200, HEAD), BF)] * 4,
+        lambda *refs: pair_kernel(ks, *refs),
+        out_shape=[jax.ShapeDtypeStruct((8, 200, HEAD), BF)] * len(ks),
         in_specs=[sm] + [vm] * 3,
-        out_specs=[vm] * 4,
+        out_specs=[vm] * len(ks),
         cost_estimate=pl.CostEstimate(flops=1, bytes_accessed=1, transcendentals=0),
-        name="pair_sum",
+        name=f"pair_sum_{len(ks)}",
     )(at, mine, *other)
 
 
@@ -334,15 +334,17 @@
     mine, *other, h0, h1, h2, h3 = blocks(at, g_pieces, (out_weight, wa, wb, wc, wd), o_rows)
     heads = [h0] + [move(h, "seq", XS[4 - k]) for k, h in ((1, h1), (2, h2), (3, h3))]
 
-    pairs = pair_sum(at, mine, *[move(part, "dp", CORES) for part in other])
+    other = [move(part, "dp", CORES) for part in other]
+    pairs = pair_sum((1, 2, 3), at, mine, *other)
     qkv, *_ = after((qkv, *pairs))
     grads = attention(at, image_units[0], qkv, heads)
+    grads, mine, *other = after((grads, mine, *other))
     sent = lax.all_to_all(grads, "seq", split_axis=0, concat_axis=0, tiled=True)
     query_grad, key_grad, value_grad = unpack(sent)
 
-    total = pairs[0].astype(F32)
+    total = pair_sum((0,), at, mine, *other)[0].astype(F32)
     for k in (1, 2, 3):
-        total = total + move(pairs[k], "seq", XS[k]).astype(F32)
+        total = total + move(pairs[k - 1], "seq", XS[k]).astype(F32)
     total = total.reshape(4, 2, 200, HEAD)
     bit, quarter = lax.rem(z, 2), lax.div(z, 2)
     away = lax.dynamic_index_in_dim(total, 1 - bit, 1, keepdims=False).astype(BF)

time: 109 us -> 110 us (level)
  waiting for transfers between devices: 26.4 us -> 23.6 us
  Pallas kernels: 28.5 us -> 31.2 us
    ppermute x5, waiting for transfers between devices: 3.96 us -> 1.12 us  [the longest x3 1.11 us: on_device(): total = total + move(pairs[k - 1], 'seq', XS[k]).astype(F32)]
    pallas_call x1 -> x2, Pallas kernels: 3.47 us -> 5.97 us  [pair_sum(): pl.pallas_call(lambda *refs: pair_kernel(ks, *refs), out_shape=[jax.Shape...]
  transfers between devices with their start and end apart: 23 -> 23, of which waited for: 6 -> 5; matrix products, arithmetic and copies ran while one was open for 2% -> 3% of each run, Pallas kernels for 26% -> 29%
where the time goes in v7:
time: 110 us; the launch traced here: 109 us
  starting transfers between devices  48.4 us (44%)
  Pallas kernels  31.2 us (28%)
  waiting for transfers between devices  23.6 us (21%)
  other arithmetic  2.51 us (2%)
  local copies, waits for them, and re-layouts  2.44 us (2%)
    all_to_all x1, waiting for transfers between devices, on_device(): lax.all_to_all(pack_out(saved_out[0]), 'seq', split_axis=0, concat_axis=0...  13.5 us
    ppermute x3, starting transfers between devices, on_device(): parts.append(move(part, 'dp', ZFAR[k]))  11.2 us
    pallas_call x1, Pallas kernels, blocks(): pl.pallas_call(block_kernel, out_shape=[jax.ShapeDtypeStruct(size, BF) fo...  9.97 us
    pallas_call x1, Pallas kernels, attention(): pl.pallas_call(attention_kernel, out_shape=jax.ShapeDtypeStruct((16, 3, T...  8.09 us
    pallas_call x2, Pallas kernels, pair_sum(): pl.pallas_call(lambda *refs: pair_kernel(ks, *refs), out_shape=[jax.Shape...  5.97 us
    all_to_all x1, starting transfers between devices, on_device(): sent = lax.all_to_all(grads, 'seq', split_axis=0, concat_axis=0, tiled=True)  5.57 us
    ppermute x1, waiting for transfers between devices, on_device(): move(away, 'dp', ZNEAR).astype(F32)  5.12 us
    all_to_all x1, starting transfers between devices, on_device(): lax.all_to_all(pack(q, keys_in[0], values_in[0]), 'seq', split_axis=0, co...  4.94 us
  transfers between devices with their start and end apart: 23, of which 5 were waited for; matrix products, arithmetic and copies ran while one was open for 3% of the time, Pallas kernels for 29%

profile of v7, /device:TPU:2, one launch (start us, length us, event | category | flops | bytes accessed | tf_op | source)
XLA Modules:
  0.0 109.0 jit_solution(7564952713952675048)
XLA Ops:
  2.3 1.7 %collective-permute-start.1 = (bf16[128,3200]{1,0:T(8,128)(2,1)}, bf16[128,3200]{1,0:T(8,128)(2,1)S(1)}, u32[]{:S(2)}, u32[]{:S(2)}) collective-permute-start(bf16[128,3200]{1,0:T(8,128)(2,1)} %bitcast.40), channel_id=1, source_target_pairs={{0,3},{1,0},{2,1},{3,2},{4,7},{5,4},{6,5},{7,6},{8,11},{9,8},{10,9... | collective-permute-start | bytes 2457608 | tf_op jit(solution)/shard_map/ppermute | solution.py:321
  6.5 2.9 %collective-permute-start.3 = (bf16[64,3200]{1,0:T(8,128)(2,1)S(1)}, bf16[64,3200]{1,0:T(8,128)(2,1)}, u32[]{:S(2)}, u32[]{:S(2)}) collective-permute-start(bf16[64,3200]{1,0:T(8,128)(2,1)S(1)} %constant_dynamic-slice_fusion), channel_id=1, source_target_pairs={{0,8},{1,9},{2,10},{3,11},{4,12},{5,13},{6,14},{7,15},{8,0},{9,1},... | collective-permute-start | bytes 1228808 | tf_op jit(solution)/shard_map/ppermute | solution.py:323
  9.4 1.9 %pack_out.1 = bf16[4,128,512]{2,1,0:T(8,128)(2,1)} custom-call(bf16[128,2048]{1,0:T(8,128)(2,1)} %bitcast.35), custom_call_target="tpu_custom_call" | custom-call | flops 1 | bytes 1 | tf_op jit(solution)/shard_map/pack_out/pallas_call | solution.py:185
  11.4 3.5 %all-to-all-start = ((bf16[4,128,512]{2,1,0:T(8,128)(2,1)}), bf16[4,128,512]{2,1,0:T(8,128)(2,1)S(1)}, u32[]{:S(2)}, u32[]{:S(2)}) async-start(bf16[4,128,512]{2,1,0:T(8,128)(2,1)} %pack_out.1), calls=%async_computation | async-start | bytes 1048576 | tf_op jit(solution)/shard_map/all_to_all | solution.py:324
  15.5 13.5 %all-to-all-done.refs_10_ = bf16[4,128,512]{2,1,0:T(8,128)(2,1)S(1)} async-done(((bf16[4,128,512]{2,1,0:T(8,128)(2,1)}), bf16[4,128,512]{2,1,0:T(8,128)(2,1)S(1)}, u32[]{:S(2)}, u32[]{:S(2)}) %all-to-all-start) | async-done | bytes 524320 | tf_op jit(solution)/shard_map/all_to_all | solution.py:324
  30.4 2.1 %collective-permute-start.5 = (bf16[64,3200]{1,0:T(8,128)(2,1)S(1)}, bf16[64,3200]{1,0:T(8,128)(2,1)}, u32[]{:S(2)}, u32[]{:S(2)}) collective-permute-start(bf16[64,3200]{1,0:T(8,128)(2,1)S(1)} %slice.7), channel_id=1, source_target_pairs={{0,3},{1,0},{2,1},{3,2},{4,7},{5,4},{6,5},{7,6},{8,11},{9,8},{10,9... | collective-permute-start | bytes 1228808 | tf_op jit(solution)/shard_map/ppermute | solution.py:329
  32.5 2.8 %pack.1 = bf16[16,3,128,128]{3,2,1,0:T(8,128)(2,1)} custom-call(bf16[128,2048]{1,0:T(8,128)(2,1)} %bitcast.36, bf16[128,2048]{1,0:T(8,128)(2,1)} %bitcast.37, bf16[128,2048]{1,0:T(8,128)(2,1)} %bitcast.38), custom_call_target="tpu_custom_call" | custom-call | flops 1150000 | bytes 3600 | tf_op jit(solution)/shard_map/pack/pallas_call | solution.py:138
  35.3 4.9 %all-to-all-start.1 = ((bf16[16,3,128,128]{3,2,1,0:T(8,128)(2,1)}), bf16[16,3,128,128]{3,2,1,0:T(8,128)(2,1)S(1)}, u32[]{:S(2)}, u32[]{:S(2)}) async-start(bf16[16,3,128,128]{3,2,1,0:T(8,128)(2,1)} %pack.1), calls=%async_computation.1 | async-start | bytes 3145728 | tf_op jit(solution)/shard_map/all_to_all | solution.py:331
  40.3 2.2 %collective-permute-done.4.refs_3_ = bf16[64,3200]{1,0:T(8,128)(2,1)} collective-permute-done((bf16[64,3200]{1,0:T(8,128)(2,1)S(1)}, bf16[64,3200]{1,0:T(8,128)(2,1)}, u32[]{:S(2)}, u32[]{:S(2)}) %collective-permute-start.4) | collective-permute-done | bytes 409632 | tf_op jit(solution)/shard_map/ppermute | solution.py:329
  42.5 10.0 %blocks.1 = (bf16[8,200,512]{2,1,0:T(8,128)(2,1)}, bf16[4,200,512]{2,1,0:T(8,128)(2,1)}, bf16[4,200,512]{2,1,0:T(8,128)(2,1)}, bf16[528,128]{1,0:T(8,128)(2,1)},...) custom-call(s32[4]{0:T(128)} %pad_add_fusion.at.refs_0_.xi, ...), custom_call_target="tpu_custom_call" | custom-call | flops 10350000128 | bytes 32400000 | tf_op jit(solution)/shard_map/blocks/pallas_call | solution.py:270
  53.6 2.4 %collective-permute-start.11 = (bf16[528,128]{1,0:T(8,128)(2,1)}, bf16[528,128]{1,0:T(8,128)(2,1)S(1)}, u32[]{:S(2)}, u32[]{:S(2)}) collective-permute-start(bf16[528,128]{1,0:T(8,128)(2,1)} %get-tuple-element.56), channel_id=1, source_target_pairs={{0,8},{1,9},{2,10},{3,11},{4,12},{5,13},{6,14},{7,15},{8,0},{9,1},... | collective-permute-start | bytes 405512 | tf_op jit(solution)/shard_map/ppermute | solution.py:335
  56.0 1.8 %collective-permute-start.12 = (bf16[528,128]{1,0:T(8,128)(2,1)}, bf16[528,128]{1,0:T(8,128)(2,1)S(1)}, u32[]{:S(2)}, u32[]{:S(2)}) collective-permute-start(bf16[528,128]{1,0:T(8,128)(2,1)} %get-tuple-element.57), channel_id=1, source_target_pairs={{0,4},{1,5},{2,6},{3,7},{4,8},{5,9},{6,10},{7,11},{8,12},{9,13},{1... | collective-permute-start | bytes 405512 | tf_op jit(solution)/shard_map/ppermute | solution.py:335
  59.0 3.2 %pair_sum_3.1 = (bf16[8,200,128]{2,1,0:T(8,128)(2,1)}, bf16[8,200,128]{2,1,0:T(8,128)(2,1)}, bf16[8,200,128]{2,1,0:T(8,128)(2,1)}) custom-call(s32[4]{0:T(128)} %pad_add_fusion.at.refs_0_.xi, bf16[8,200,512]{2,1,0:T(8,128)(2,1)} %get-tuple-element.58.refs_1_, bf16[4,200,512]{2,1,0:T(8,128)(2,1)} %copy-done.3, bf16[4,200,512]{2,1,0:T(8,128)(2,1)} %copy-done.4), custom_call_target="tpu_custom_call" | custom-call | flops 1 | bytes 1 | tf_op jit(solution)/shard_map/pair_sum_3/pallas_call | solution.py:302
  62.3 2.3 %collective-permute-start.14 = (bf16[8,200,128]{2,1,0:T(8,128)(2,1)}, bf16[8,200,128]{2,1,0:T(8,128)(2,1)S(1)}, u32[]{:S(2)}, u32[]{:S(2)}) collective-permute-start(bf16[8,200,128]{2,1,0:T(8,128)(2,1)} %get-tuple-element.51), channel_id=1, source_target_pairs={{0,8},{1,9},{2,10},{3,11},{4,12},{5,13},{6,14},{7,15},{8,0},{9,1},... | collective-permute-start | bytes 1228808 | tf_op jit(solution)/shard_map/ppermute | solution.py:347
  64.6 2.4 %collective-permute-start.15 = (bf16[8,200,128]{2,1,0:T(8,128)(2,1)}, bf16[8,200,128]{2,1,0:T(8,128)(2,1)S(1)}, u32[]{:S(2)}, u32[]{:S(2)}) collective-permute-start(bf16[8,200,128]{2,1,0:T(8,128)(2,1)} %get-tuple-element.52), channel_id=1, source_target_pairs={{0,12},{1,13},{2,14},{3,15},{4,0},{5,1},{6,2},{7,3},{8,4},{9,5},{1... | collective-permute-start | bytes 1228808 | tf_op jit(solution)/shard_map/ppermute | solution.py:347
  68.6 8.1 %attention.1 = bf16[16,3,128,128]{3,2,1,0:T(8,128)(2,1)} custom-call(s32[4]{0:T(128)S(1)} %copy-done, s32[8]{0:T(128)S(1)} %bitcast.32, bf16[16,3,128,128]{3,2,1,0:T(8,128)(2,1)S(1)} %all-to-all-done.1.qkv, bf16[528,128]{1,0:T(8,128)(2,1)S(1)} %copy-done.2, bf16[528,128]{1,0:T(8,128)(2,1)S(1)} %collective-permute-done.10.h1, ...), custom_call_target="tpu_custom_call" | custom-call | flops 10350000128 | bytes 32400000 | tf_op jit(solution)/shard_map/attention/pallas_call | solution.py:116
  76.7 5.6 %all-to-all-start.2 = ((bf16[16,3,128,128]{3,2,1,0:T(8,128)(2,1)}), bf16[16,3,128,128]{3,2,1,0:T(8,128)(2,1)}, u32[]{:S(2)}, u32[]{:S(2)}) async-start(bf16[16,3,128,128]{3,2,1,0:T(8,128)(2,1)} %attention.1), calls=%async_computation.2 | async-start | bytes 3145728 | tf_op jit(solution)/shard_map/all_to_all | solution.py:342
  82.3 2.8 %pair_sum_1.1 = bf16[8,200,128]{2,1,0:T(8,128)(2,1)} custom-call(s32[4]{0:T(128)} %pad_add_fusion.at.refs_0_.xi, bf16[8,200,512]{2,1,0:T(8,128)(2,1)} %get-tuple-element.58.refs_1_, bf16[4,200,512]{2,1,0:T(8,128)(2,1)} %copy-done.3, bf16[4,200,512]{2,1,0:T(8,128)(2,1)} %copy-done.4), custom_call_target="tpu_custom_call" | custom-call | flops 1 | bytes 1 | tf_op jit(solution)/shard_map/pair_sum_1/pallas_call | solution.py:302
  87.4 2.0 %collective-permute-start.16 = (bf16[4,200,128]{2,1,0:T(8,128)(2,1)S(1)}, bf16[4,200,128]{2,1,0:T(8,128)(2,1)S(1)}, u32[]{:S(2)}, u32[]{:S(2)}) collective-permute-start(bf16[4,200,128]{2,1,0:T(8,128)(2,1)S(1)} %fusion), channel_id=1, source_target_pairs={{0,32},{16,48},{32,0},{48,16},{64,96},{80,112},{96,64},{112,80},{1... | collective-permute-start | bytes 614408 | tf_op jit(solution)/shard_map/ppermute | solution.py:351
  89.4 5.1 %collective-permute-done.16 = bf16[4,200,128]{2,1,0:T(8,128)(2,1)S(1)} collective-permute-done((bf16[4,200,128]{2,1,0:T(8,128)(2,1)S(1)}, bf16[4,200,128]{2,1,0:T(8,128)(2,1)S(1)}, u32[]{:S(2)}, u32[]{:S(2)}) %collective-permute-start.16) | collective-permute-done | bytes 204832 | tf_op jit(solution)/shard_map/ppermute | solution.py:351
  94.6 3.3 %collective-permute-start.17 = (bf16[200,128]{1,0:T(8,128)(2,1)S(1)}, bf16[200,128]{1,0:T(8,128)(2,1)S(1)}, u32[]{:S(2)}, u32[]{:S(2)}) collective-permute-start(bf16[200,128]{1,0:T(8,128)(2,1)S(1)} %get-tuple-element.74), channel_id=1, source_target_pairs={{0,64},{16,80},{32,96},{48,112},{64,128},{80,144},{96,160},{112,17... | collective-permute-start | bytes 153608 | tf_op jit(solution)/shard_map/ppermute | solution.py:355
  97.9 5.2 %collective-permute-start.18 = (bf16[200,128]{1,0:T(8,128)(2,1)S(1)}, bf16[200,128]{1,0:T(8,128)(2,1)S(1)}, u32[]{:S(2)}, u32[]{:S(2)}) collective-permute-start(bf16[200,128]{1,0:T(8,128)(2,1)S(1)} %get-tuple-element.73), channel_id=1, source_target_pairs={{0,128},{16,144},{32,160},{48,176},{64,192},{80,208},{96,224},{112... | collective-permute-start | bytes 153608 | tf_op jit(solution)/shard_map/ppermute | solution.py:355
  103.2 2.7 %collective-permute-start.19 = (bf16[200,128]{1,0:T(8,128)(2,1)S(1)}, bf16[200,128]{1,0:T(8,128)(2,1)S(1)}, u32[]{:S(2)}, u32[]{:S(2)}) collective-permute-start(bf16[200,128]{1,0:T(8,128)(2,1)S(1)} %get-tuple-element.72), channel_id=1, source_target_pairs={{0,192},{16,208},{32,224},{48,240},{64,0},{80,16},{96,32},{112,48}... | collective-permute-start | bytes 153608 | tf_op jit(solution)/shard_map/ppermute | solution.py:355
  105.8 2.5 %unpack.1 = (bf16[128,2048]{1,0:T(8,128)(2,1)}, bf16[128,2048]{1,0:T(8,128)(2,1)}, bf16[128,2048]{1,0:T(8,128)(2,1)}) custom-call(bf16[16,3,128,128]{3,2,1,0:T(8,128)(2,1)} %all-to-all-done.2.grads), custom_call_target="tpu_custom_call" | custom-call | flops 1 | bytes 1 | tf_op jit(solution)/shard_map/unpack/pallas_call | solution.py:158
  (55 shorter events, 13.3 us)
Async XLA Ops:
  0.6 28.3 %collective-permute-start = (bf16[128,3200]{1,0:T(8,128)(2,1)}, bf16[128,3200]{1,0:T(8,128)(2,1)S(1)}, u32[]{:S(2)}, u32[]{:S(2)}) collective-permute-start(bf16[128,3200]{1,0:T(8,128)(2,1)} %bitcast.39), channel_id=1, source_target_pairs={{0,1},{1,2},{2,3},{3,0},{4,5},{5,6},{6,7},{7,4},{8,9},{9,10},{10,1... | collective-permute-start | bytes 2457608 | tf_op jit(solution)/shard_map/ppermute | solution.py:321
  2.3 26.7 %collective-permute-start.1 = (bf16[128,3200]{1,0:T(8,128)(2,1)}, bf16[128,3200]{1,0:T(8,128)(2,1)S(1)}, u32[]{:S(2)}, u32[]{:S(2)}) collective-permute-start(bf16[128,3200]{1,0:T(8,128)(2,1)} %bitcast.40), channel_id=1, source_target_pairs={{0,3},{1,0},{2,1},{3,2},{4,7},{5,4},{6,5},{7,6},{8,11},{9,8},{10,9... | collective-permute-start | bytes 2457608 | tf_op jit(solution)/shard_map/ppermute | solution.py:321
  3.9 25.1 %collective-permute-start.2 = (bf16[128,3200]{1,0:T(8,128)(2,1)}, bf16[128,3200]{1,0:T(8,128)(2,1)}, u32[]{:S(2)}, u32[]{:S(2)}) collective-permute-start(bf16[128,3200]{1,0:T(8,128)(2,1)} %refs_5_.1), channel_id=1, source_target_pairs={{0,4},{1,5},{2,6},{3,7},{4,8},{5,9},{6,10},{7,11},{8,12},{9,13},{1... | collective-permute-start | bytes 2457608 | tf_op jit(solution)/shard_map/ppermute | solution.py:322
  6.5 22.5 %collective-permute-start.3 = (bf16[64,3200]{1,0:T(8,128)(2,1)S(1)}, bf16[64,3200]{1,0:T(8,128)(2,1)}, u32[]{:S(2)}, u32[]{:S(2)}) collective-permute-start(bf16[64,3200]{1,0:T(8,128)(2,1)S(1)} %constant_dynamic-slice_fusion), channel_id=1, source_target_pairs={{0,8},{1,9},{2,10},{3,11},{4,12},{5,13},{6,14},{7,15},{8,0},{9,1},... | collective-permute-start | bytes 1228808 | tf_op jit(solution)/shard_map/ppermute | solution.py:323
  11.4 17.6 %all-to-all-start = ((bf16[4,128,512]{2,1,0:T(8,128)(2,1)}), bf16[4,128,512]{2,1,0:T(8,128)(2,1)S(1)}, u32[]{:S(2)}, u32[]{:S(2)}) async-start(bf16[4,128,512]{2,1,0:T(8,128)(2,1)} %pack_out.1), calls=%async_computation | async-start | bytes 1048576 | tf_op jit(solution)/shard_map/all_to_all | solution.py:324
  29.0 13.5 %copy-start.7 = (bf16[128,3200]{1,0:T(8,128)(2,1)}, bf16[128,3200]{1,0:T(8,128)(2,1)S(1)}, u32[]{:S(2)}) copy-start(bf16[128,3200]{1,0:T(8,128)(2,1)S(1)} %collective-permute-done.1.refs_2_) | copy-start | bytes 2457604
  29.0 13.4 %collective-permute-start.6 = (bf16[128,3200]{1,0:T(8,128)(2,1)}, bf16[128,3200]{1,0:T(8,128)(2,1)}, u32[]{:S(2)}, u32[]{:S(2)}) collective-permute-start(bf16[128,3200]{1,0:T(8,128)(2,1)} %collective-permute-done.2.refs_6_), channel_id=1, source_target_pairs={{0,16},{16,0},{32,48},{48,32},{64,80},{80,64},{96,112},{112,96},{1... | collective-permute-start | bytes 2457608 | tf_op jit(solution)/shard_map/ppermute | solution.py:330
  29.2 13.3 %collective-permute-start.4 = (bf16[64,3200]{1,0:T(8,128)(2,1)S(1)}, bf16[64,3200]{1,0:T(8,128)(2,1)}, u32[]{:S(2)}, u32[]{:S(2)}) collective-permute-start(bf16[64,3200]{1,0:T(8,128)(2,1)S(1)} %slice.6), channel_id=1, source_target_pairs={{0,1},{1,2},{2,3},{3,0},{4,5},{5,6},{6,7},{7,4},{8,9},{9,10},{10,1... | collective-permute-start | bytes 1228808 | tf_op jit(solution)/shard_map/ppermute | solution.py:329
  30.4 12.0 %collective-permute-start.5 = (bf16[64,3200]{1,0:T(8,128)(2,1)S(1)}, bf16[64,3200]{1,0:T(8,128)(2,1)}, u32[]{:S(2)}, u32[]{:S(2)}) collective-permute-start(bf16[64,3200]{1,0:T(8,128)(2,1)S(1)} %slice.7), channel_id=1, source_target_pairs={{0,3},{1,0},{2,1},{3,2},{4,7},{5,4},{6,5},{7,6},{8,11},{9,8},{10,9... | collective-permute-start | bytes 1228808 | tf_op jit(solution)/shard_map/ppermute | solution.py:329
  32.5 9.9 %collective-permute-start.7 = (bf16[64,3200]{1,0:T(8,128)(2,1)}, bf16[64,3200]{1,0:T(8,128)(2,1)}, u32[]{:S(2)}, u32[]{:S(2)}) collective-permute-start(bf16[64,3200]{1,0:T(8,128)(2,1)} %collective-permute-done.3.refs_8_), channel_id=1, source_target_pairs={{0,16},{16,0},{32,48},{48,32},{64,80},{80,64},{96,112},{112,96},{1... | collective-permute-start | bytes 1228808 | tf_op jit(solution)/shard_map/ppermute | solution.py:330
  35.3 29.2 %all-to-all-start.1 = ((bf16[16,3,128,128]{3,2,1,0:T(8,128)(2,1)}), bf16[16,3,128,128]{3,2,1,0:T(8,128)(2,1)S(1)}, u32[]{:S(2)}, u32[]{:S(2)}) async-start(bf16[16,3,128,128]{3,2,1,0:T(8,128)(2,1)} %pack.1), calls=%async_computation.1 | async-start | bytes 3145728 | tf_op jit(solution)/shard_map/all_to_all | solution.py:331
  52.5 5.4 %collective-permute-start.8 = (bf16[4,200,512]{2,1,0:T(8,128)(2,1)}, bf16[4,200,512]{2,1,0:T(8,128)(2,1)S(1)}, u32[]{:S(2)}, u32[]{:S(2)}) collective-permute-start(bf16[4,200,512]{2,1,0:T(8,128)(2,1)} %get-tuple-element.48), channel_id=1, source_target_pairs={{0,16},{16,0},{32,48},{48,32},{64,80},{80,64},{96,112},{112,96},{1... | collective-permute-start | bytes 2457608 | tf_op jit(solution)/shard_map/ppermute | solution.py:337
  52.6 5.3 %collective-permute-start.9 = (bf16[4,200,512]{2,1,0:T(8,128)(2,1)}, bf16[4,200,512]{2,1,0:T(8,128)(2,1)S(1)}, u32[]{:S(2)}, u32[]{:S(2)}) collective-permute-start(bf16[4,200,512]{2,1,0:T(8,128)(2,1)} %get-tuple-element.49), channel_id=1, source_target_pairs={{0,16},{16,0},{32,48},{48,32},{64,80},{80,64},{96,112},{112,96},{1... | collective-permute-start | bytes 2457608 | tf_op jit(solution)/shard_map/ppermute | solution.py:337
  53.0 11.5 %collective-permute-start.10 = (bf16[528,128]{1,0:T(8,128)(2,1)}, bf16[528,128]{1,0:T(8,128)(2,1)S(1)}, u32[]{:S(2)}, u32[]{:S(2)}) collective-permute-start(bf16[528,128]{1,0:T(8,128)(2,1)} %get-tuple-element.55), channel_id=1, source_target_pairs={{0,12},{1,13},{2,14},{3,15},{4,0},{5,1},{6,2},{7,3},{8,4},{9,5},{1... | collective-permute-start | bytes 405512 | tf_op jit(solution)/shard_map/ppermute | solution.py:335
  53.6 15.0 %collective-permute-start.11 = (bf16[528,128]{1,0:T(8,128)(2,1)}, bf16[528,128]{1,0:T(8,128)(2,1)S(1)}, u32[]{:S(2)}, u32[]{:S(2)}) collective-permute-start(bf16[528,128]{1,0:T(8,128)(2,1)} %get-tuple-element.56), channel_id=1, source_target_pairs={{0,8},{1,9},{2,10},{3,11},{4,12},{5,13},{6,14},{7,15},{8,0},{9,1},... | collective-permute-start | bytes 405512 | tf_op jit(solution)/shard_map/ppermute | solution.py:335
  56.0 12.6 %collective-permute-start.12 = (bf16[528,128]{1,0:T(8,128)(2,1)}, bf16[528,128]{1,0:T(8,128)(2,1)S(1)}, u32[]{:S(2)}, u32[]{:S(2)}) collective-permute-start(bf16[528,128]{1,0:T(8,128)(2,1)} %get-tuple-element.57), channel_id=1, source_target_pairs={{0,4},{1,5},{2,6},{3,7},{4,8},{5,9},{6,10},{7,11},{8,12},{9,13},{1... | collective-permute-start | bytes 405512 | tf_op jit(solution)/shard_map/ppermute | solution.py:335
  62.3 22.8 %collective-permute-start.13 = (bf16[8,200,128]{2,1,0:T(8,128)(2,1)}, bf16[8,200,128]{2,1,0:T(8,128)(2,1)S(1)}, u32[]{:S(2)}, u32[]{:S(2)}) collective-permute-start(bf16[8,200,128]{2,1,0:T(8,128)(2,1)} %get-tuple-element.50), channel_id=1, source_target_pairs={{0,4},{1,5},{2,6},{3,7},{4,8},{5,9},{6,10},{7,11},{8,12},{9,13},{1... | collective-permute-start | bytes 1228808 | tf_op jit(solution)/shard_map/ppermute | solution.py:347
  62.3 22.8 %collective-permute-start.14 = (bf16[8,200,128]{2,1,0:T(8,128)(2,1)}, bf16[8,200,128]{2,1,0:T(8,128)(2,1)S(1)}, u32[]{:S(2)}, u32[]{:S(2)}) collective-permute-start(bf16[8,200,128]{2,1,0:T(8,128)(2,1)} %get-tuple-element.51), channel_id=1, source_target_pairs={{0,8},{1,9},{2,10},{3,11},{4,12},{5,13},{6,14},{7,15},{8,0},{9,1},... | collective-permute-start | bytes 1228808 | tf_op jit(solution)/shard_map/ppermute | solution.py:347
  64.6 21.6 %collective-permute-start.15 = (bf16[8,200,128]{2,1,0:T(8,128)(2,1)}, bf16[8,200,128]{2,1,0:T(8,128)(2,1)S(1)}, u32[]{:S(2)}, u32[]{:S(2)}) collective-permute-start(bf16[8,200,128]{2,1,0:T(8,128)(2,1)} %get-tuple-element.52), channel_id=1, source_target_pairs={{0,12},{1,13},{2,14},{3,15},{4,0},{5,1},{6,2},{7,3},{8,4},{9,5},{1... | collective-permute-start | bytes 1228808 | tf_op jit(solution)/shard_map/ppermute | solution.py:347
  76.7 29.1 %all-to-all-start.2 = ((bf16[16,3,128,128]{3,2,1,0:T(8,128)(2,1)}), bf16[16,3,128,128]{3,2,1,0:T(8,128)(2,1)}, u32[]{:S(2)}, u32[]{:S(2)}) async-start(bf16[16,3,128,128]{3,2,1,0:T(8,128)(2,1)} %attention.1), calls=%async_computation.2 | async-start | bytes 3145728 | tf_op jit(solution)/shard_map/all_to_all | solution.py:342
  87.4 7.1 %collective-permute-start.16 = (bf16[4,200,128]{2,1,0:T(8,128)(2,1)S(1)}, bf16[4,200,128]{2,1,0:T(8,128)(2,1)S(1)}, u32[]{:S(2)}, u32[]{:S(2)}) collective-permute-start(bf16[4,200,128]{2,1,0:T(8,128)(2,1)S(1)} %fusion), channel_id=1, source_target_pairs={{0,32},{16,48},{32,0},{48,16},{64,96},{80,112},{96,64},{112,80},{1... | collective-permute-start | bytes 614408 | tf_op jit(solution)/shard_map/ppermute | solution.py:351
  94.6 13.7 %collective-permute-start.17 = (bf16[200,128]{1,0:T(8,128)(2,1)S(1)}, bf16[200,128]{1,0:T(8,128)(2,1)S(1)}, u32[]{:S(2)}, u32[]{:S(2)}) collective-permute-start(bf16[200,128]{1,0:T(8,128)(2,1)S(1)} %get-tuple-element.74), channel_id=1, source_target_pairs={{0,64},{16,80},{32,96},{48,112},{64,128},{80,144},{96,160},{112,17... | collective-permute-start | bytes 153608 | tf_op jit(solution)/shard_map/ppermute | solution.py:355
  97.9 10.4 %collective-permute-start.18 = (bf16[200,128]{1,0:T(8,128)(2,1)S(1)}, bf16[200,128]{1,0:T(8,128)(2,1)S(1)}, u32[]{:S(2)}, u32[]{:S(2)}) collective-permute-start(bf16[200,128]{1,0:T(8,128)(2,1)S(1)} %get-tuple-element.73), channel_id=1, source_target_pairs={{0,128},{16,144},{32,160},{48,176},{64,192},{80,208},{96,224},{112... | collective-permute-start | bytes 153608 | tf_op jit(solution)/shard_map/ppermute | solution.py:355
  103.2 5.2 %collective-permute-start.19 = (bf16[200,128]{1,0:T(8,128)(2,1)S(1)}, bf16[200,128]{1,0:T(8,128)(2,1)S(1)}, u32[]{:S(2)}, u32[]{:S(2)}) collective-permute-start(bf16[200,128]{1,0:T(8,128)(2,1)S(1)} %get-tuple-element.72), channel_id=1, source_target_pairs={{0,192},{16,208},{32,224},{48,240},{64,0},{80,16},{96,32},{112,48}... | collective-permute-start | bytes 153608 | tf_op jit(solution)/shard_map/ppermute | solution.py:355
  (7 other events, 43.5 us)

commit v8 on v6

--- a/solution.py
+++ b/solution.py
@@ -145,26 +145,29 @@
     )(q, k, v)
 
 
-def unpack_kernel(grads, q, k, v):
+def unpack_kernel(grads, own, a, b, c, q, k, v, weight):
     for i in range(16):
         cols = pl.ds(i * HEAD, HEAD)
         q[:, cols] = grads[i, 0]
         k[:, cols] = grads[i, 1]
         v[:, cols] = grads[i, 2]
-
-
-def unpack(grads):
+    total = own[...] + a[...].astype(F32) + b[...].astype(F32) + c[...].astype(F32)
+    weight[...] = total * (1.0 / math.sqrt(PACK * 16))
+
+
+def unpack(grads, parts):
     rows = TOK // 2
+    whole = pl.BlockSpec((200, HEAD), lambda i: (0, 0))
     return pl.pallas_call(
         unpack_kernel,
         grid=(2,),
-        out_shape=[jax.ShapeDtypeStruct((TOK, 16 * HEAD), BF)] * 3,
-        in_specs=[pl.BlockSpec((16, 3, rows, HEAD), lambda i: (0, 0, i, 0))],
-        out_specs=[pl.BlockSpec((rows, 16 * HEAD), lambda i: (i, 0))] * 3,
+        out_shape=[jax.ShapeDtypeStruct((TOK, 16 * HEAD), BF)] * 3 + [jax.ShapeDtypeStruct((200, HEAD), F32)],
+        in_specs=[pl.BlockSpec((16, 3, rows, HEAD), lambda i: (0, 0, i, 0))] + [whole] * 4,
+        out_specs=[pl.BlockSpec((rows, 16 * HEAD), lambda i: (i, 0))] * 3 + [whole],
         compiler_params=pltpu.CompilerParams(vmem_limit_bytes=63 * 1024 * 1024),
         cost_estimate=pl.CostEstimate(flops=1, bytes_accessed=1, transcendentals=0),
         name="unpack",
-    )(grads)
+    )(grads, *parts)
 
 
 def three_terms(value):
@@ -338,7 +341,6 @@
     qkv, *_ = after((qkv, *pairs))
     grads = attention(at, image_units[0], qkv, heads)
     sent = lax.all_to_all(grads, "seq", split_axis=0, concat_axis=0, tiled=True)
-    query_grad, key_grad, value_grad = unpack(sent)
 
     total = pairs[0].astype(F32)
     for k in (1, 2, 3):
@@ -351,10 +353,8 @@
     for k in (1, 2, 3):
         part = lax.dynamic_index_in_dim(total, lax.rem(quarter + k, 4), 0, keepdims=False).astype(BF)
         parts.append(move(part, "dp", ZFAR[k]))
-    *parts, query_grad, key_grad, value_grad = after((*parts, query_grad, key_grad, value_grad))
-    last = sum([part.astype(F32) for part in parts[1:]], parts[0])
-    weight_grad = last.T * (1.0 / math.sqrt(PACK * 16))
-    return query_grad[None], key_grad[None], value_grad[None], weight_grad
+    query_grad, key_grad, value_grad, weight = unpack(sent, parts)
+    return query_grad[None], key_grad[None], value_grad[None], weight.T
 
 
 def solution(mesh):

time: 109 us -> 111 us (1.018)
  waiting for transfers between devices: 26.4 us -> 27.9 us
  local copies, waits for them, and re-layouts: 2.4 us -> 3.64 us
    ppermute x3, waiting for transfers between devices: 0.01 us -> 1.71 us  [on_device(): parts.append(move(part, 'dp', ZFAR[k]))]
  transfers between devices with their start and end apart: 23 -> 23, of which waited for: 6 -> 8; matrix products, arithmetic and copies ran while one was open for 2% -> 2% of each run, Pallas kernels for 26% -> 24%
where the time goes in v8:
time: 111 us
  starting transfers between devices  48.4 us (44%)
  Pallas kernels  28.8 us (26%)
  waiting for transfers between devices  27.9 us (25%)
  local copies, waits for them, and re-layouts  3.64 us (3%)
    all_to_all x1, waiting for transfers between devices, on_device(): lax.all_to_all(pack_out(saved_out[0]), 'seq', split_axis=0, concat_axis=0...  13.5 us
    ppermute x3, starting transfers between devices, on_device(): parts.append(move(part, 'dp', ZFAR[k]))  11.2 us
    pallas_call x1, Pallas kernels, blocks(): pl.pallas_call(block_kernel, out_shape=[jax.ShapeDtypeStruct(size, BF) fo...  9.96 us
    pallas_call x1, Pallas kernels, attention(): pl.pallas_call(attention_kernel, out_shape=jax.ShapeDtypeStruct((16, 3, T...  8.04 us
    all_to_all x1, starting transfers between devices, on_device(): sent = lax.all_to_all(grads, 'seq', split_axis=0, concat_axis=0, tiled=True)  5.69 us
    ppermute x1, waiting for transfers between devices, on_device(): move(away, 'dp', ZNEAR).astype(F32)  5.12 us
    all_to_all x1, starting transfers between devices, on_device(): lax.all_to_all(pack(q, keys_in[0], values_in[0]), 'seq', split_axis=0, co...  4.94 us
    ppermute x3, starting transfers between devices, on_device(): move(h, 'seq', XS[4 - k])  4.76 us
  transfers between devices with their start and end apart: 23, of which 8 were waited for; matrix products, arithmetic and copies ran while one was open for 2% of the time, Pallas kernels for 24%

profile of v8, /device:TPU:2, one launch (start us, length us, event | category | flops | bytes accessed | tf_op | source)
XLA Modules:
  0.0 110.5 jit_solution(10768785879451322029)
XLA Ops:
  2.3 1.7 %collective-permute-start.1 = (bf16[128,3200]{1,0:T(8,128)(2,1)}, bf16[128,3200]{1,0:T(8,128)(2,1)S(1)}, u32[]{:S(2)}, u32[]{:S(2)}) collective-permute-start(bf16[128,3200]{1,0:T(8,128)(2,1)} %bitcast.39), channel_id=1, source_target_pairs={{0,3},{1,0},{2,1},{3,2},{4,7},{5,4},{6,5},{7,6},{8,11},{9,8},{10,9... | collective-permute-start | bytes 2457608 | tf_op jit(solution)/shard_map/ppermute | solution.py:324
  6.5 2.9 %collective-permute-start.3 = (bf16[64,3200]{1,0:T(8,128)(2,1)S(1)}, bf16[64,3200]{1,0:T(8,128)(2,1)}, u32[]{:S(2)}, u32[]{:S(2)}) collective-permute-start(bf16[64,3200]{1,0:T(8,128)(2,1)S(1)} %constant_dynamic-slice_fusion), channel_id=1, source_target_pairs={{0,8},{1,9},{2,10},{3,11},{4,12},{5,13},{6,14},{7,15},{8,0},{9,1},... | collective-permute-start | bytes 1228808 | tf_op jit(solution)/shard_map/ppermute | solution.py:326
  9.4 1.9 %pack_out.1 = bf16[4,128,512]{2,1,0:T(8,128)(2,1)} custom-call(bf16[128,2048]{1,0:T(8,128)(2,1)} %bitcast.34), custom_call_target="tpu_custom_call" | custom-call | flops 1 | bytes 1 | tf_op jit(solution)/shard_map/pack_out/pallas_call | solution.py:188
  11.4 3.5 %all-to-all-start = ((bf16[4,128,512]{2,1,0:T(8,128)(2,1)}), bf16[4,128,512]{2,1,0:T(8,128)(2,1)S(1)}, u32[]{:S(2)}, u32[]{:S(2)}) async-start(bf16[4,128,512]{2,1,0:T(8,128)(2,1)} %pack_out.1), calls=%async_computation | async-start | bytes 1048576 | tf_op jit(solution)/shard_map/all_to_all | solution.py:327
  15.5 13.5 %all-to-all-done.refs_10_ = bf16[4,128,512]{2,1,0:T(8,128)(2,1)S(1)} async-done(((bf16[4,128,512]{2,1,0:T(8,128)(2,1)}), bf16[4,128,512]{2,1,0:T(8,128)(2,1)S(1)}, u32[]{:S(2)}, u32[]{:S(2)}) %all-to-all-start) | async-done | bytes 524320 | tf_op jit(solution)/shard_map/all_to_all | solution.py:327
  30.4 2.1 %collective-permute-start.5 = (bf16[64,3200]{1,0:T(8,128)(2,1)S(1)}, bf16[64,3200]{1,0:T(8,128)(2,1)}, u32[]{:S(2)}, u32[]{:S(2)}) collective-permute-start(bf16[64,3200]{1,0:T(8,128)(2,1)S(1)} %slice.7), channel_id=1, source_target_pairs={{0,3},{1,0},{2,1},{3,2},{4,7},{5,4},{6,5},{7,6},{8,11},{9,8},{10,9... | collective-permute-start | bytes 1228808 | tf_op jit(solution)/shard_map/ppermute | solution.py:332
  32.5 2.8 %pack.1 = bf16[16,3,128,128]{3,2,1,0:T(8,128)(2,1)} custom-call(bf16[128,2048]{1,0:T(8,128)(2,1)} %bitcast.35, bf16[128,2048]{1,0:T(8,128)(2,1)} %bitcast.36, bf16[128,2048]{1,0:T(8,128)(2,1)} %bitcast.37), custom_call_target="tpu_custom_call" | custom-call | flops 1150000 | bytes 3600 | tf_op jit(solution)/shard_map/pack/pallas_call | solution.py:138
  35.3 4.9 %all-to-all-start.1 = ((bf16[16,3,128,128]{3,2,1,0:T(8,128)(2,1)}), bf16[16,3,128,128]{3,2,1,0:T(8,128)(2,1)S(1)}, u32[]{:S(2)}, u32[]{:S(2)}) async-start(bf16[16,3,128,128]{3,2,1,0:T(8,128)(2,1)} %pack.1), calls=%async_computation.1 | async-start | bytes 3145728 | tf_op jit(solution)/shard_map/all_to_all | solution.py:334
  40.3 2.2 %collective-permute-done.4.refs_3_ = bf16[64,3200]{1,0:T(8,128)(2,1)} collective-permute-done((bf16[64,3200]{1,0:T(8,128)(2,1)S(1)}, bf16[64,3200]{1,0:T(8,128)(2,1)}, u32[]{:S(2)}, u32[]{:S(2)}) %collective-permute-start.4) | collective-permute-done | bytes 409632 | tf_op jit(solution)/shard_map/ppermute | solution.py:332
  42.5 10.0 %blocks.1 = (bf16[8,200,512]{2,1,0:T(8,128)(2,1)}, bf16[4,200,512]{2,1,0:T(8,128)(2,1)}, bf16[4,200,512]{2,1,0:T(8,128)(2,1)}, bf16[528,128]{1,0:T(8,128)(2,1)},...) custom-call(s32[4]{0:T(128)} %pad_add_fusion.at.xi, bf16[128,3200]{1,0:T(8,128)(2,1)} %bitcast.40, ...), custom_call_target="tpu_custom_call" | custom-call | flops 10350000128 | bytes 32400000 | tf_op jit(solution)/shard_map/blocks/pallas_call | solution.py:273
  53.6 2.4 %collective-permute-start.11 = (bf16[528,128]{1,0:T(8,128)(2,1)}, bf16[528,128]{1,0:T(8,128)(2,1)S(1)}, u32[]{:S(2)}, u32[]{:S(2)}) collective-permute-start(bf16[528,128]{1,0:T(8,128)(2,1)} %get-tuple-element.48), channel_id=1, source_target_pairs={{0,8},{1,9},{2,10},{3,11},{4,12},{5,13},{6,14},{7,15},{8,0},{9,1},... | collective-permute-start | bytes 405512 | tf_op jit(solution)/shard_map/ppermute | solution.py:338
  56.0 1.8 %collective-permute-start.12 = (bf16[528,128]{1,0:T(8,128)(2,1)}, bf16[528,128]{1,0:T(8,128)(2,1)S(1)}, u32[]{:S(2)}, u32[]{:S(2)}) collective-permute-start(bf16[528,128]{1,0:T(8,128)(2,1)} %get-tuple-element.49), channel_id=1, source_target_pairs={{0,4},{1,5},{2,6},{3,7},{4,8},{5,9},{6,10},{7,11},{8,12},{9,13},{1... | collective-permute-start | bytes 405512 | tf_op jit(solution)/shard_map/ppermute | solution.py:338
  59.0 3.5 %pair_sum.1 = (bf16[8,200,128]{2,1,0:T(8,128)(2,1)}, bf16[8,200,128]{2,1,0:T(8,128)(2,1)}, bf16[8,200,128]{2,1,0:T(8,128)(2,1)}, bf16[8,200,128]{2,1,0:T(8,128)(2,1)}) custom-call(s32[4]{0:T(128)} %pad_add_fusion.at.xi, bf16[8,200,512]{2,1,0:T(8,128)(2,1)} %get-tuple-element.38.mine, bf16[4,200,512]{2,1,0:T(8,128)(2,1)} %copy-done.3, ...), custom_call_target="tpu_custom_call" | custom-call | flops 1 | bytes 1 | tf_op jit(solution)/shard_map/pair_sum/pallas_call | solution.py:305
  62.5 2.3 %collective-permute-start.14 = (bf16[8,200,128]{2,1,0:T(8,128)(2,1)}, bf16[8,200,128]{2,1,0:T(8,128)(2,1)S(1)}, u32[]{:S(2)}, u32[]{:S(2)}) collective-permute-start(bf16[8,200,128]{2,1,0:T(8,128)(2,1)} %get-tuple-element.43), channel_id=1, source_target_pairs={{0,8},{1,9},{2,10},{3,11},{4,12},{5,13},{6,14},{7,15},{8,0},{9,1},... | collective-permute-start | bytes 1228808 | tf_op jit(solution)/shard_map/ppermute | solution.py:347
  64.8 2.2 %collective-permute-start.15 = (bf16[8,200,128]{2,1,0:T(8,128)(2,1)}, bf16[8,200,128]{2,1,0:T(8,128)(2,1)S(1)}, u32[]{:S(2)}, u32[]{:S(2)}) collective-permute-start(bf16[8,200,128]{2,1,0:T(8,128)(2,1)} %get-tuple-element.44), channel_id=1, source_target_pairs={{0,12},{1,13},{2,14},{3,15},{4,0},{5,1},{6,2},{7,3},{8,4},{9,5},{1... | collective-permute-start | bytes 1228808 | tf_op jit(solution)/shard_map/ppermute | solution.py:347
  68.6 8.0 %attention.1 = bf16[16,3,128,128]{3,2,1,0:T(8,128)(2,1)} custom-call(s32[4]{0:T(128)S(1)} %copy-done, s32[8]{0:T(128)S(1)} %bitcast.31, bf16[16,3,128,128]{3,2,1,0:T(8,128)(2,1)S(1)} %all-to-all-done.1.qkv, bf16[528,128]{1,0:T(8,128)(2,1)S(1)} %copy-done.2, bf16[528,128]{1,0:T(8,128)(2,1)S(1)} %collective-permute-done.10.h1, ...), custom_call_target="tpu_custom_call" | custom-call | flops 10350000128 | bytes 32400000 | tf_op jit(solution)/shard_map/attention/pallas_call | solution.py:116
  76.7 5.7 %all-to-all-start.2 = ((bf16[16,3,128,128]{3,2,1,0:T(8,128)(2,1)}), bf16[16,3,128,128]{3,2,1,0:T(8,128)(2,1)}, u32[]{:S(2)}, u32[]{:S(2)}) async-start(bf16[16,3,128,128]{3,2,1,0:T(8,128)(2,1)} %attention.1), calls=%async_computation.2 | async-start | bytes 3145728 | tf_op jit(solution)/shard_map/all_to_all | solution.py:343
  83.1 3.1 %collective-permute-done.15 = bf16[8,200,128]{2,1,0:T(8,128)(2,1)S(1)} collective-permute-done((bf16[8,200,128]{2,1,0:T(8,128)(2,1)}, bf16[8,200,128]{2,1,0:T(8,128)(2,1)S(1)}, u32[]{:S(2)}, u32[]{:S(2)}) %collective-permute-start.15) | collective-permute-done | bytes 409632 | tf_op jit(solution)/shard_map/ppermute | solution.py:347
  86.4 2.0 %collective-permute-start.16 = (bf16[4,200,128]{2,1,0:T(8,128)(2,1)S(1)}, bf16[4,200,128]{2,1,0:T(8,128)(2,1)S(1)}, u32[]{:S(2)}, u32[]{:S(2)}) collective-permute-start(bf16[4,200,128]{2,1,0:T(8,128)(2,1)S(1)} %fusion), channel_id=1, source_target_pairs={{0,32},{16,48},{32,0},{48,16},{64,96},{80,112},{96,64},{112,80},{1... | collective-permute-start | bytes 614408 | tf_op jit(solution)/shard_map/ppermute | solution.py:351
  88.4 5.1 %collective-permute-done.16 = bf16[4,200,128]{2,1,0:T(8,128)(2,1)S(1)} collective-permute-done((bf16[4,200,128]{2,1,0:T(8,128)(2,1)S(1)}, bf16[4,200,128]{2,1,0:T(8,128)(2,1)S(1)}, u32[]{:S(2)}, u32[]{:S(2)}) %collective-permute-start.16) | collective-permute-done | bytes 204832 | tf_op jit(solution)/shard_map/ppermute | solution.py:351
  93.6 3.3 %collective-permute-start.17 = (bf16[200,128]{1,0:T(8,128)(2,1)S(1)}, bf16[200,128]{1,0:T(8,128)(2,1)S(1)}, u32[]{:S(2)}, u32[]{:S(2)}) collective-permute-start(bf16[200,128]{1,0:T(8,128)(2,1)S(1)} %get-tuple-element.56), channel_id=1, source_target_pairs={{0,64},{16,80},{32,96},{48,112},{64,128},{80,144},{96,160},{112,17... | collective-permute-start | bytes 153608 | tf_op jit(solution)/shard_map/ppermute | solution.py:355
  97.0 5.2 %collective-permute-start.18 = (bf16[200,128]{1,0:T(8,128)(2,1)S(1)}, bf16[200,128]{1,0:T(8,128)(2,1)S(1)}, u32[]{:S(2)}, u32[]{:S(2)}) collective-permute-start(bf16[200,128]{1,0:T(8,128)(2,1)S(1)} %get-tuple-element.55), channel_id=1, source_target_pairs={{0,128},{16,144},{32,160},{48,176},{64,192},{80,208},{96,224},{112... | collective-permute-start | bytes 153608 | tf_op jit(solution)/shard_map/ppermute | solution.py:355
  102.2 2.7 %collective-permute-start.19 = (bf16[200,128]{1,0:T(8,128)(2,1)S(1)}, bf16[200,128]{1,0:T(8,128)(2,1)S(1)}, u32[]{:S(2)}, u32[]{:S(2)}) collective-permute-start(bf16[200,128]{1,0:T(8,128)(2,1)S(1)} %get-tuple-element.54), channel_id=1, source_target_pairs={{0,192},{16,208},{32,224},{48,240},{64,0},{80,16},{96,32},{112,48}... | collective-permute-start | bytes 153608 | tf_op jit(solution)/shard_map/ppermute | solution.py:355
  107.8 2.6 %unpack.1 = (bf16[128,2048]{1,0:T(8,128)(2,1)}, bf16[128,2048]{1,0:T(8,128)(2,1)}, bf16[128,2048]{1,0:T(8,128)(2,1)}, f32[200,128]{1,0:T(8,128)}) custom-call(bf16[16,3,128,128]{3,2,1,0:T(8,128)(2,1)} %all-to-all-done.2.grads, f32[200,128]{1,0:T(8,128)} %dynamic-slice_bitcast_fusion.own, bf16[200,128]{1,0:T(8,128)(2,1)} %copy-done.9, ...), custom_call_target="tpu_custom_call" | custom-call | flops 1 | bytes 1 | tf_op jit(solution)/shard_map/unpack/pallas_call | solution.py:161
  (61 shorter events, 14.2 us)
Async XLA Ops:
  0.6 28.3 %collective-permute-start = (bf16[128,3200]{1,0:T(8,128)(2,1)}, bf16[128,3200]{1,0:T(8,128)(2,1)S(1)}, u32[]{:S(2)}, u32[]{:S(2)}) collective-permute-start(bf16[128,3200]{1,0:T(8,128)(2,1)} %bitcast.38), channel_id=1, source_target_pairs={{0,1},{1,2},{2,3},{3,0},{4,5},{5,6},{6,7},{7,4},{8,9},{9,10},{10,1... | collective-permute-start | bytes 2457608 | tf_op jit(solution)/shard_map/ppermute | solution.py:324
  2.3 26.7 %collective-permute-start.1 = (bf16[128,3200]{1,0:T(8,128)(2,1)}, bf16[128,3200]{1,0:T(8,128)(2,1)S(1)}, u32[]{:S(2)}, u32[]{:S(2)}) collective-permute-start(bf16[128,3200]{1,0:T(8,128)(2,1)} %bitcast.39), channel_id=1, source_target_pairs={{0,3},{1,0},{2,1},{3,2},{4,7},{5,4},{6,5},{7,6},{8,11},{9,8},{10,9... | collective-permute-start | bytes 2457608 | tf_op jit(solution)/shard_map/ppermute | solution.py:324
  3.9 25.1 %collective-permute-start.2 = (bf16[128,3200]{1,0:T(8,128)(2,1)}, bf16[128,3200]{1,0:T(8,128)(2,1)}, u32[]{:S(2)}, u32[]{:S(2)}) collective-permute-start(bf16[128,3200]{1,0:T(8,128)(2,1)} %refs_5_.1), channel_id=1, source_target_pairs={{0,4},{1,5},{2,6},{3,7},{4,8},{5,9},{6,10},{7,11},{8,12},{9,13},{1... | collective-permute-start | bytes 2457608 | tf_op jit(solution)/shard_map/ppermute | solution.py:325
  6.5 22.5 %collective-permute-start.3 = (bf16[64,3200]{1,0:T(8,128)(2,1)S(1)}, bf16[64,3200]{1,0:T(8,128)(2,1)}, u32[]{:S(2)}, u32[]{:S(2)}) collective-permute-start(bf16[64,3200]{1,0:T(8,128)(2,1)S(1)} %constant_dynamic-slice_fusion), channel_id=1, source_target_pairs={{0,8},{1,9},{2,10},{3,11},{4,12},{5,13},{6,14},{7,15},{8,0},{9,1},... | collective-permute-start | bytes 1228808 | tf_op jit(solution)/shard_map/ppermute | solution.py:326
  11.4 17.6 %all-to-all-start = ((bf16[4,128,512]{2,1,0:T(8,128)(2,1)}), bf16[4,128,512]{2,1,0:T(8,128)(2,1)S(1)}, u32[]{:S(2)}, u32[]{:S(2)}) async-start(bf16[4,128,512]{2,1,0:T(8,128)(2,1)} %pack_out.1), calls=%async_computation | async-start | bytes 1048576 | tf_op jit(solution)/shard_map/all_to_all | solution.py:327
  29.0 13.5 %copy-start.8 = (bf16[128,3200]{1,0:T(8,128)(2,1)}, bf16[128,3200]{1,0:T(8,128)(2,1)S(1)}, u32[]{:S(2)}) copy-start(bf16[128,3200]{1,0:T(8,128)(2,1)S(1)} %collective-permute-done.1.refs_2_) | copy-start | bytes 2457604
  29.0 13.4 %collective-permute-start.6 = (bf16[128,3200]{1,0:T(8,128)(2,1)}, bf16[128,3200]{1,0:T(8,128)(2,1)}, u32[]{:S(2)}, u32[]{:S(2)}) collective-permute-start(bf16[128,3200]{1,0:T(8,128)(2,1)} %collective-permute-done.2.refs_6_), channel_id=1, source_target_pairs={{0,16},{16,0},{32,48},{48,32},{64,80},{80,64},{96,112},{112,96},{1... | collective-permute-start | bytes 2457608 | tf_op jit(solution)/shard_map/ppermute | solution.py:333
  29.2 13.3 %collective-permute-start.4 = (bf16[64,3200]{1,0:T(8,128)(2,1)S(1)}, bf16[64,3200]{1,0:T(8,128)(2,1)}, u32[]{:S(2)}, u32[]{:S(2)}) collective-permute-start(bf16[64,3200]{1,0:T(8,128)(2,1)S(1)} %slice.6), channel_id=1, source_target_pairs={{0,1},{1,2},{2,3},{3,0},{4,5},{5,6},{6,7},{7,4},{8,9},{9,10},{10,1... | collective-permute-start | bytes 1228808 | tf_op jit(solution)/shard_map/ppermute | solution.py:332
  30.4 12.0 %collective-permute-start.5 = (bf16[64,3200]{1,0:T(8,128)(2,1)S(1)}, bf16[64,3200]{1,0:T(8,128)(2,1)}, u32[]{:S(2)}, u32[]{:S(2)}) collective-permute-start(bf16[64,3200]{1,0:T(8,128)(2,1)S(1)} %slice.7), channel_id=1, source_target_pairs={{0,3},{1,0},{2,1},{3,2},{4,7},{5,4},{6,5},{7,6},{8,11},{9,8},{10,9... | collective-permute-start | bytes 1228808 | tf_op jit(solution)/shard_map/ppermute | solution.py:332
  32.5 9.9 %collective-permute-start.7 = (bf16[64,3200]{1,0:T(8,128)(2,1)}, bf16[64,3200]{1,0:T(8,128)(2,1)}, u32[]{:S(2)}, u32[]{:S(2)}) collective-permute-start(bf16[64,3200]{1,0:T(8,128)(2,1)} %collective-permute-done.3.refs_8_), channel_id=1, source_target_pairs={{0,16},{16,0},{32,48},{48,32},{64,80},{80,64},{96,112},{112,96},{1... | collective-permute-start | bytes 1228808 | tf_op jit(solution)/shard_map/ppermute | solution.py:333
  35.3 29.5 %all-to-all-start.1 = ((bf16[16,3,128,128]{3,2,1,0:T(8,128)(2,1)}), bf16[16,3,128,128]{3,2,1,0:T(8,128)(2,1)S(1)}, u32[]{:S(2)}, u32[]{:S(2)}) async-start(bf16[16,3,128,128]{3,2,1,0:T(8,128)(2,1)} %pack.1), calls=%async_computation.1 | async-start | bytes 3145728 | tf_op jit(solution)/shard_map/all_to_all | solution.py:334
  52.4 5.4 %collective-permute-start.8 = (bf16[4,200,512]{2,1,0:T(8,128)(2,1)}, bf16[4,200,512]{2,1,0:T(8,128)(2,1)S(1)}, u32[]{:S(2)}, u32[]{:S(2)}) collective-permute-start(bf16[4,200,512]{2,1,0:T(8,128)(2,1)} %get-tuple-element.39), channel_id=1, source_target_pairs={{0,16},{16,0},{32,48},{48,32},{64,80},{80,64},{96,112},{112,96},{1... | collective-permute-start | bytes 2457608 | tf_op jit(solution)/shard_map/ppermute | solution.py:340
  52.5 5.3 %collective-permute-start.9 = (bf16[4,200,512]{2,1,0:T(8,128)(2,1)}, bf16[4,200,512]{2,1,0:T(8,128)(2,1)S(1)}, u32[]{:S(2)}, u32[]{:S(2)}) collective-permute-start(bf16[4,200,512]{2,1,0:T(8,128)(2,1)} %get-tuple-element.40), channel_id=1, source_target_pairs={{0,16},{16,0},{32,48},{48,32},{64,80},{80,64},{96,112},{112,96},{1... | collective-permute-start | bytes 2457608 | tf_op jit(solution)/shard_map/ppermute | solution.py:340
  53.0 11.7 %collective-permute-start.10 = (bf16[528,128]{1,0:T(8,128)(2,1)}, bf16[528,128]{1,0:T(8,128)(2,1)S(1)}, u32[]{:S(2)}, u32[]{:S(2)}) collective-permute-start(bf16[528,128]{1,0:T(8,128)(2,1)} %get-tuple-element.47), channel_id=1, source_target_pairs={{0,12},{1,13},{2,14},{3,15},{4,0},{5,1},{6,2},{7,3},{8,4},{9,5},{1... | collective-permute-start | bytes 405512 | tf_op jit(solution)/shard_map/ppermute | solution.py:338
  53.6 15.0 %collective-permute-start.11 = (bf16[528,128]{1,0:T(8,128)(2,1)}, bf16[528,128]{1,0:T(8,128)(2,1)S(1)}, u32[]{:S(2)}, u32[]{:S(2)}) collective-permute-start(bf16[528,128]{1,0:T(8,128)(2,1)} %get-tuple-element.48), channel_id=1, source_target_pairs={{0,8},{1,9},{2,10},{3,11},{4,12},{5,13},{6,14},{7,15},{8,0},{9,1},... | collective-permute-start | bytes 405512 | tf_op jit(solution)/shard_map/ppermute | solution.py:338
  56.0 12.6 %collective-permute-start.12 = (bf16[528,128]{1,0:T(8,128)(2,1)}, bf16[528,128]{1,0:T(8,128)(2,1)S(1)}, u32[]{:S(2)}, u32[]{:S(2)}) collective-permute-start(bf16[528,128]{1,0:T(8,128)(2,1)} %get-tuple-element.49), channel_id=1, source_target_pairs={{0,4},{1,5},{2,6},{3,7},{4,8},{5,9},{6,10},{7,11},{8,12},{9,13},{1... | collective-permute-start | bytes 405512 | tf_op jit(solution)/shard_map/ppermute | solution.py:338
  62.5 20.6 %collective-permute-start.13 = (bf16[8,200,128]{2,1,0:T(8,128)(2,1)}, bf16[8,200,128]{2,1,0:T(8,128)(2,1)S(1)}, u32[]{:S(2)}, u32[]{:S(2)}) collective-permute-start(bf16[8,200,128]{2,1,0:T(8,128)(2,1)} %get-tuple-element.42), channel_id=1, source_target_pairs={{0,4},{1,5},{2,6},{3,7},{4,8},{5,9},{6,10},{7,11},{8,12},{9,13},{1... | collective-permute-start | bytes 1228808 | tf_op jit(solution)/shard_map/ppermute | solution.py:347
  62.5 20.6 %collective-permute-start.14 = (bf16[8,200,128]{2,1,0:T(8,128)(2,1)}, bf16[8,200,128]{2,1,0:T(8,128)(2,1)S(1)}, u32[]{:S(2)}, u32[]{:S(2)}) collective-permute-start(bf16[8,200,128]{2,1,0:T(8,128)(2,1)} %get-tuple-element.43), channel_id=1, source_target_pairs={{0,8},{1,9},{2,10},{3,11},{4,12},{5,13},{6,14},{7,15},{8,0},{9,1},... | collective-permute-start | bytes 1228808 | tf_op jit(solution)/shard_map/ppermute | solution.py:347
  64.8 21.4 %collective-permute-start.15 = (bf16[8,200,128]{2,1,0:T(8,128)(2,1)}, bf16[8,200,128]{2,1,0:T(8,128)(2,1)S(1)}, u32[]{:S(2)}, u32[]{:S(2)}) collective-permute-start(bf16[8,200,128]{2,1,0:T(8,128)(2,1)} %get-tuple-element.44), channel_id=1, source_target_pairs={{0,12},{1,13},{2,14},{3,15},{4,0},{5,1},{6,2},{7,3},{8,4},{9,5},{1... | collective-permute-start | bytes 1228808 | tf_op jit(solution)/shard_map/ppermute | solution.py:347
  76.7 30.5 %all-to-all-start.2 = ((bf16[16,3,128,128]{3,2,1,0:T(8,128)(2,1)}), bf16[16,3,128,128]{3,2,1,0:T(8,128)(2,1)}, u32[]{:S(2)}, u32[]{:S(2)}) async-start(bf16[16,3,128,128]{3,2,1,0:T(8,128)(2,1)} %attention.1), calls=%async_computation.2 | async-start | bytes 3145728 | tf_op jit(solution)/shard_map/all_to_all | solution.py:343
  86.4 7.1 %collective-permute-start.16 = (bf16[4,200,128]{2,1,0:T(8,128)(2,1)S(1)}, bf16[4,200,128]{2,1,0:T(8,128)(2,1)S(1)}, u32[]{:S(2)}, u32[]{:S(2)}) collective-permute-start(bf16[4,200,128]{2,1,0:T(8,128)(2,1)S(1)} %fusion), channel_id=1, source_target_pairs={{0,32},{16,48},{32,0},{48,16},{64,96},{80,112},{96,64},{112,80},{1... | collective-permute-start | bytes 614408 | tf_op jit(solution)/shard_map/ppermute | solution.py:351
  93.6 11.9 %collective-permute-start.17 = (bf16[200,128]{1,0:T(8,128)(2,1)S(1)}, bf16[200,128]{1,0:T(8,128)(2,1)S(1)}, u32[]{:S(2)}, u32[]{:S(2)}) collective-permute-start(bf16[200,128]{1,0:T(8,128)(2,1)S(1)} %get-tuple-element.56), channel_id=1, source_target_pairs={{0,64},{16,80},{32,96},{48,112},{64,128},{80,144},{96,160},{112,17... | collective-permute-start | bytes 153608 | tf_op jit(solution)/shard_map/ppermute | solution.py:355
  97.0 9.0 %collective-permute-start.18 = (bf16[200,128]{1,0:T(8,128)(2,1)S(1)}, bf16[200,128]{1,0:T(8,128)(2,1)S(1)}, u32[]{:S(2)}, u32[]{:S(2)}) collective-permute-start(bf16[200,128]{1,0:T(8,128)(2,1)S(1)} %get-tuple-element.55), channel_id=1, source_target_pairs={{0,128},{16,144},{32,160},{48,176},{64,192},{80,208},{96,224},{112... | collective-permute-start | bytes 153608 | tf_op jit(solution)/shard_map/ppermute | solution.py:355
  102.2 5.0 %collective-permute-start.19 = (bf16[200,128]{1,0:T(8,128)(2,1)S(1)}, bf16[200,128]{1,0:T(8,128)(2,1)S(1)}, u32[]{:S(2)}, u32[]{:S(2)}) collective-permute-start(bf16[200,128]{1,0:T(8,128)(2,1)S(1)} %get-tuple-element.54), channel_id=1, source_target_pairs={{0,192},{16,208},{32,224},{48,240},{64,0},{80,16},{96,32},{112,48}... | collective-permute-start | bytes 153608 | tf_op jit(solution)/shard_map/ppermute | solution.py:355
  (11 other events, 56.8 us)

commit v9 on v6

--- a/solution.py
+++ b/solution.py
@@ -134,13 +134,14 @@
 
 
 def pack(q, k, v):
-    vm = pl.BlockSpec(memory_space=pltpu.VMEM)
+    rows = TOK // 2
     return pl.pallas_call(
         pack_kernel,
+        grid=(2,),
         out_shape=jax.ShapeDtypeStruct((16, 3, TOK, HEAD), BF),
-        in_specs=[vm] * 3,
-        out_specs=vm,
-        cost_estimate=pl.CostEstimate(flops=1150000, bytes_accessed=3600, transcendentals=0),
+        in_specs=[pl.BlockSpec((rows, 16 * HEAD), lambda i: (i, 0))] * 3,
+        out_specs=pl.BlockSpec((16, 3, rows, HEAD), lambda i: (0, 0, i, 0)),
+        cost_estimate=pl.CostEstimate(flops=1, bytes_accessed=1, transcendentals=0),
         name="pack",
     )(q, k, v)
 

time: 109 us -> 109 us (level)
  no operation moved by 1% of the time
where the time goes in v9:
time: 109 us; the launch traced here: 108 us
  starting transfers between devices  48 us (44%)
  Pallas kernels  27.8 us (26%)
  waiting for transfers between devices  27.1 us (25%)
  local copies, waits for them, and re-layouts  2.4 us (2%)
  other arithmetic  1.49 us (1%)
    all_to_all x1, waiting for transfers between devices, on_device(): lax.all_to_all(pack_out(saved_out[0]), 'seq', split_axis=0, concat_axis=0...  13.5 us
    ppermute x3, starting transfers between devices, on_device(): parts.append(move(part, 'dp', ZFAR[k]))  11.2 us
    pallas_call x1, Pallas kernels, blocks(): pl.pallas_call(block_kernel, out_shape=[jax.ShapeDtypeStruct(size, BF) fo...  9.95 us
    pallas_call x1, Pallas kernels, attention(): pl.pallas_call(attention_kernel, out_shape=jax.ShapeDtypeStruct((16, 3, T...  7.59 us
    all_to_all x1, starting transfers between devices, on_device(): sent = lax.all_to_all(grads, 'seq', split_axis=0, concat_axis=0, tiled=True)  5.68 us
    ppermute x1, waiting for transfers between devices, on_device(): move(away, 'dp', ZNEAR).astype(F32)  5.12 us
    all_to_all x1, starting transfers between devices, on_device(): lax.all_to_all(pack(q, keys_in[0], values_in[0]), 'seq', split_axis=0, co...  4.95 us
    ppermute x3, starting transfers between devices, on_device(): move(h, 'seq', XS[4 - k])  4.76 us
  transfers between devices with their start and end apart: 23, of which 6 were waited for; matrix products, arithmetic and copies ran while one was open for 2% of the time, Pallas kernels for 26%

profile of v9, /device:TPU:2, one launch (start us, length us, event | category | flops | bytes accessed | tf_op | source)
XLA Modules:
  0.0 107.7 jit_solution(15555569610031534120)
XLA Ops:
  2.3 1.7 %collective-permute-start.1 = (bf16[128,3200]{1,0:T(8,128)(2,1)}, bf16[128,3200]{1,0:T(8,128)(2,1)S(1)}, u32[]{:S(2)}, u32[]{:S(2)}) collective-permute-start(bf16[128,3200]{1,0:T(8,128)(2,1)} %bitcast.40), channel_id=1, source_target_pairs={{0,3},{1,0},{2,1},{3,2},{4,7},{5,4},{6,5},{7,6},{8,11},{9,8},{10,9... | collective-permute-start | bytes 2457608 | tf_op jit(solution)/shard_map/ppermute | solution.py:322
  6.5 2.9 %collective-permute-start.3 = (bf16[64,3200]{1,0:T(8,128)(2,1)S(1)}, bf16[64,3200]{1,0:T(8,128)(2,1)}, u32[]{:S(2)}, u32[]{:S(2)}) collective-permute-start(bf16[64,3200]{1,0:T(8,128)(2,1)S(1)} %constant_dynamic-slice_fusion), channel_id=1, source_target_pairs={{0,8},{1,9},{2,10},{3,11},{4,12},{5,13},{6,14},{7,15},{8,0},{9,1},... | collective-permute-start | bytes 1228808 | tf_op jit(solution)/shard_map/ppermute | solution.py:324
  9.4 1.9 %pack_out.1 = bf16[4,128,512]{2,1,0:T(8,128)(2,1)} custom-call(bf16[128,2048]{1,0:T(8,128)(2,1)} %bitcast.35), custom_call_target="tpu_custom_call" | custom-call | flops 1 | bytes 1 | tf_op jit(solution)/shard_map/pack_out/pallas_call | solution.py:186
  11.4 3.5 %all-to-all-start = ((bf16[4,128,512]{2,1,0:T(8,128)(2,1)}), bf16[4,128,512]{2,1,0:T(8,128)(2,1)S(1)}, u32[]{:S(2)}, u32[]{:S(2)}) async-start(bf16[4,128,512]{2,1,0:T(8,128)(2,1)} %pack_out.1), calls=%async_computation | async-start | bytes 1048576 | tf_op jit(solution)/shard_map/all_to_all | solution.py:325
  15.4 13.5 %all-to-all-done.refs_10_ = bf16[4,128,512]{2,1,0:T(8,128)(2,1)S(1)} async-done(((bf16[4,128,512]{2,1,0:T(8,128)(2,1)}), bf16[4,128,512]{2,1,0:T(8,128)(2,1)S(1)}, u32[]{:S(2)}, u32[]{:S(2)}) %all-to-all-start) | async-done | bytes 524320 | tf_op jit(solution)/shard_map/all_to_all | solution.py:325
  30.4 2.1 %collective-permute-start.5 = (bf16[64,3200]{1,0:T(8,128)(2,1)S(1)}, bf16[64,3200]{1,0:T(8,128)(2,1)}, u32[]{:S(2)}, u32[]{:S(2)}) collective-permute-start(bf16[64,3200]{1,0:T(8,128)(2,1)S(1)} %slice.7), channel_id=1, source_target_pairs={{0,3},{1,0},{2,1},{3,2},{4,7},{5,4},{6,5},{7,6},{8,11},{9,8},{10,9... | collective-permute-start | bytes 1228808 | tf_op jit(solution)/shard_map/ppermute | solution.py:330
  32.5 2.4 %pack.1 = bf16[16,3,128,128]{3,2,1,0:T(8,128)(2,1)} custom-call(bf16[128,2048]{1,0:T(8,128)(2,1)} %bitcast.36, bf16[128,2048]{1,0:T(8,128)(2,1)} %bitcast.37, bf16[128,2048]{1,0:T(8,128)(2,1)} %bitcast.38), custom_call_target="tpu_custom_call" | custom-call | flops 1 | bytes 1 | tf_op jit(solution)/shard_map/pack/pallas_call | solution.py:138
  35.0 4.9 %all-to-all-start.1 = ((bf16[16,3,128,128]{3,2,1,0:T(8,128)(2,1)}), bf16[16,3,128,128]{3,2,1,0:T(8,128)(2,1)S(1)}, u32[]{:S(2)}, u32[]{:S(2)}) async-start(bf16[16,3,128,128]{3,2,1,0:T(8,128)(2,1)} %pack.1), calls=%async_computation.1 | async-start | bytes 3145728 | tf_op jit(solution)/shard_map/all_to_all | solution.py:332
  39.9 2.5 %collective-permute-done.4.refs_3_ = bf16[64,3200]{1,0:T(8,128)(2,1)} collective-permute-done((bf16[64,3200]{1,0:T(8,128)(2,1)S(1)}, bf16[64,3200]{1,0:T(8,128)(2,1)}, u32[]{:S(2)}, u32[]{:S(2)}) %collective-permute-start.4) | collective-permute-done | bytes 409632 | tf_op jit(solution)/shard_map/ppermute | solution.py:330
  42.5 9.9 %blocks.1 = (bf16[8,200,512]{2,1,0:T(8,128)(2,1)}, bf16[4,200,512]{2,1,0:T(8,128)(2,1)}, bf16[4,200,512]{2,1,0:T(8,128)(2,1)}, bf16[528,128]{1,0:T(8,128)(2,1)},...) custom-call(s32[4]{0:T(128)} %pad_add_fusion.at.xi, bf16[128,3200]{1,0:T(8,128)(2,1)} %bitcast.41, ...), custom_call_target="tpu_custom_call" | custom-call | flops 10350000128 | bytes 32400000 | tf_op jit(solution)/shard_map/blocks/pallas_call | solution.py:271
  53.6 2.4 %collective-permute-start.18 = (bf16[528,128]{1,0:T(8,128)(2,1)}, bf16[528,128]{1,0:T(8,128)(2,1)S(1)}, u32[]{:S(2)}, u32[]{:S(2)}) collective-permute-start(bf16[528,128]{1,0:T(8,128)(2,1)} %get-tuple-element.54), channel_id=1, source_target_pairs={{0,8},{1,9},{2,10},{3,11},{4,12},{5,13},{6,14},{7,15},{8,0},{9,1},... | collective-permute-start | bytes 405512 | tf_op jit(solution)/shard_map/ppermute | solution.py:336
  56.0 1.8 %collective-permute-start.19 = (bf16[528,128]{1,0:T(8,128)(2,1)}, bf16[528,128]{1,0:T(8,128)(2,1)S(1)}, u32[]{:S(2)}, u32[]{:S(2)}) collective-permute-start(bf16[528,128]{1,0:T(8,128)(2,1)} %get-tuple-element.55), channel_id=1, source_target_pairs={{0,4},{1,5},{2,6},{3,7},{4,8},{5,9},{6,10},{7,11},{8,12},{9,13},{1... | collective-permute-start | bytes 405512 | tf_op jit(solution)/shard_map/ppermute | solution.py:336
  59.0 3.5 %pair_sum.1 = (bf16[8,200,128]{2,1,0:T(8,128)(2,1)}, bf16[8,200,128]{2,1,0:T(8,128)(2,1)}, bf16[8,200,128]{2,1,0:T(8,128)(2,1)}, bf16[8,200,128]{2,1,0:T(8,128)(2,1)}) custom-call(s32[4]{0:T(128)} %pad_add_fusion.at.xi, bf16[8,200,512]{2,1,0:T(8,128)(2,1)} %get-tuple-element.43.mine, bf16[4,200,512]{2,1,0:T(8,128)(2,1)} %copy-done.3, ...), custom_call_target="tpu_custom_call" | custom-call | flops 1 | bytes 1 | tf_op jit(solution)/shard_map/pair_sum/pallas_call | solution.py:303
  62.5 2.3 %collective-permute-start.11 = (bf16[8,200,128]{2,1,0:T(8,128)(2,1)}, bf16[8,200,128]{2,1,0:T(8,128)(2,1)S(1)}, u32[]{:S(2)}, u32[]{:S(2)}) collective-permute-start(bf16[8,200,128]{2,1,0:T(8,128)(2,1)} %get-tuple-element.48), channel_id=1, source_target_pairs={{0,8},{1,9},{2,10},{3,11},{4,12},{5,13},{6,14},{7,15},{8,0},{9,1},... | collective-permute-start | bytes 1228808 | tf_op jit(solution)/shard_map/ppermute | solution.py:346
  64.8 1.9 %collective-permute-start.12 = (bf16[8,200,128]{2,1,0:T(8,128)(2,1)}, bf16[8,200,128]{2,1,0:T(8,128)(2,1)S(1)}, u32[]{:S(2)}, u32[]{:S(2)}) collective-permute-start(bf16[8,200,128]{2,1,0:T(8,128)(2,1)} %get-tuple-element.49), channel_id=1, source_target_pairs={{0,12},{1,13},{2,14},{3,15},{4,0},{5,1},{6,2},{7,3},{8,4},{9,5},{1... | collective-permute-start | bytes 1228808 | tf_op jit(solution)/shard_map/ppermute | solution.py:346
  68.3 7.6 %attention.1 = bf16[16,3,128,128]{3,2,1,0:T(8,128)(2,1)} custom-call(s32[4]{0:T(128)S(1)} %copy-done, s32[8]{0:T(128)S(1)} %bitcast.32, bf16[16,3,128,128]{3,2,1,0:T(8,128)(2,1)S(1)} %all-to-all-done.1.qkv, bf16[528,128]{1,0:T(8,128)(2,1)S(1)} %copy-done.2, bf16[528,128]{1,0:T(8,128)(2,1)S(1)} %collective-permute-done.17.h1, ...), custom_call_target="tpu_custom_call" | custom-call | flops 10350000128 | bytes 32400000 | tf_op jit(solution)/shard_map/attention/pallas_call | solution.py:116
  75.9 5.7 %all-to-all-start.2 = ((bf16[16,3,128,128]{3,2,1,0:T(8,128)(2,1)}), bf16[16,3,128,128]{3,2,1,0:T(8,128)(2,1)}, u32[]{:S(2)}, u32[]{:S(2)}) async-start(bf16[16,3,128,128]{3,2,1,0:T(8,128)(2,1)} %attention.1), calls=%async_computation.2 | async-start | bytes 3145728 | tf_op jit(solution)/shard_map/all_to_all | solution.py:341
  82.7 3.1 %collective-permute-done.12 = bf16[8,200,128]{2,1,0:T(8,128)(2,1)S(1)} collective-permute-done((bf16[8,200,128]{2,1,0:T(8,128)(2,1)}, bf16[8,200,128]{2,1,0:T(8,128)(2,1)S(1)}, u32[]{:S(2)}, u32[]{:S(2)}) %collective-permute-start.12) | collective-permute-done | bytes 409632 | tf_op jit(solution)/shard_map/ppermute | solution.py:346
  86.0 2.0 %collective-permute-start.13 = (bf16[4,200,128]{2,1,0:T(8,128)(2,1)S(1)}, bf16[4,200,128]{2,1,0:T(8,128)(2,1)S(1)}, u32[]{:S(2)}, u32[]{:S(2)}) collective-permute-start(bf16[4,200,128]{2,1,0:T(8,128)(2,1)S(1)} %fusion), channel_id=1, source_target_pairs={{0,32},{16,48},{32,0},{48,16},{64,96},{80,112},{96,64},{112,80},{1... | collective-permute-start | bytes 614408 | tf_op jit(solution)/shard_map/ppermute | solution.py:350
  88.0 5.1 %collective-permute-done.13 = bf16[4,200,128]{2,1,0:T(8,128)(2,1)S(1)} collective-permute-done((bf16[4,200,128]{2,1,0:T(8,128)(2,1)S(1)}, bf16[4,200,128]{2,1,0:T(8,128)(2,1)S(1)}, u32[]{:S(2)}, u32[]{:S(2)}) %collective-permute-start.13) | collective-permute-done | bytes 204832 | tf_op jit(solution)/shard_map/ppermute | solution.py:350
  93.2 3.3 %collective-permute-start.14 = (bf16[200,128]{1,0:T(8,128)(2,1)S(1)}, bf16[200,128]{1,0:T(8,128)(2,1)S(1)}, u32[]{:S(2)}, u32[]{:S(2)}) collective-permute-start(bf16[200,128]{1,0:T(8,128)(2,1)S(1)} %get-tuple-element.68), channel_id=1, source_target_pairs={{0,64},{16,80},{32,96},{48,112},{64,128},{80,144},{96,160},{112,17... | collective-permute-start | bytes 153608 | tf_op jit(solution)/shard_map/ppermute | solution.py:354
  96.6 5.2 %collective-permute-start.15 = (bf16[200,128]{1,0:T(8,128)(2,1)S(1)}, bf16[200,128]{1,0:T(8,128)(2,1)S(1)}, u32[]{:S(2)}, u32[]{:S(2)}) collective-permute-start(bf16[200,128]{1,0:T(8,128)(2,1)S(1)} %get-tuple-element.67), channel_id=1, source_target_pairs={{0,128},{16,144},{32,160},{48,176},{64,192},{80,208},{96,224},{112... | collective-permute-start | bytes 153608 | tf_op jit(solution)/shard_map/ppermute | solution.py:354
  101.8 2.7 %collective-permute-start.16 = (bf16[200,128]{1,0:T(8,128)(2,1)S(1)}, bf16[200,128]{1,0:T(8,128)(2,1)S(1)}, u32[]{:S(2)}, u32[]{:S(2)}) collective-permute-start(bf16[200,128]{1,0:T(8,128)(2,1)S(1)} %get-tuple-element.66), channel_id=1, source_target_pairs={{0,192},{16,208},{32,224},{48,240},{64,0},{80,16},{96,32},{112,48}... | collective-permute-start | bytes 153608 | tf_op jit(solution)/shard_map/ppermute | solution.py:354
  104.5 2.5 %unpack.1 = (bf16[128,2048]{1,0:T(8,128)(2,1)}, bf16[128,2048]{1,0:T(8,128)(2,1)}, bf16[128,2048]{1,0:T(8,128)(2,1)}) custom-call(bf16[16,3,128,128]{3,2,1,0:T(8,128)(2,1)} %all-to-all-done.2.grads), custom_call_target="tpu_custom_call" | custom-call | flops 1 | bytes 1 | tf_op jit(solution)/shard_map/unpack/pallas_call | solution.py:159
  (56 shorter events, 12.2 us)
Async XLA Ops:
  0.6 28.3 %collective-permute-start = (bf16[128,3200]{1,0:T(8,128)(2,1)}, bf16[128,3200]{1,0:T(8,128)(2,1)S(1)}, u32[]{:S(2)}, u32[]{:S(2)}) collective-permute-start(bf16[128,3200]{1,0:T(8,128)(2,1)} %bitcast.39), channel_id=1, source_target_pairs={{0,1},{1,2},{2,3},{3,0},{4,5},{5,6},{6,7},{7,4},{8,9},{9,10},{10,1... | collective-permute-start | bytes 2457608 | tf_op jit(solution)/shard_map/ppermute | solution.py:322
  2.3 26.7 %collective-permute-start.1 = (bf16[128,3200]{1,0:T(8,128)(2,1)}, bf16[128,3200]{1,0:T(8,128)(2,1)S(1)}, u32[]{:S(2)}, u32[]{:S(2)}) collective-permute-start(bf16[128,3200]{1,0:T(8,128)(2,1)} %bitcast.40), channel_id=1, source_target_pairs={{0,3},{1,0},{2,1},{3,2},{4,7},{5,4},{6,5},{7,6},{8,11},{9,8},{10,9... | collective-permute-start | bytes 2457608 | tf_op jit(solution)/shard_map/ppermute | solution.py:322
  3.9 25.1 %collective-permute-start.2 = (bf16[128,3200]{1,0:T(8,128)(2,1)}, bf16[128,3200]{1,0:T(8,128)(2,1)}, u32[]{:S(2)}, u32[]{:S(2)}) collective-permute-start(bf16[128,3200]{1,0:T(8,128)(2,1)} %refs_5_.1), channel_id=1, source_target_pairs={{0,4},{1,5},{2,6},{3,7},{4,8},{5,9},{6,10},{7,11},{8,12},{9,13},{1... | collective-permute-start | bytes 2457608 | tf_op jit(solution)/shard_map/ppermute | solution.py:323
  6.5 22.5 %collective-permute-start.3 = (bf16[64,3200]{1,0:T(8,128)(2,1)S(1)}, bf16[64,3200]{1,0:T(8,128)(2,1)}, u32[]{:S(2)}, u32[]{:S(2)}) collective-permute-start(bf16[64,3200]{1,0:T(8,128)(2,1)S(1)} %constant_dynamic-slice_fusion), channel_id=1, source_target_pairs={{0,8},{1,9},{2,10},{3,11},{4,12},{5,13},{6,14},{7,15},{8,0},{9,1},... | collective-permute-start | bytes 1228808 | tf_op jit(solution)/shard_map/ppermute | solution.py:324
  11.4 17.6 %all-to-all-start = ((bf16[4,128,512]{2,1,0:T(8,128)(2,1)}), bf16[4,128,512]{2,1,0:T(8,128)(2,1)S(1)}, u32[]{:S(2)}, u32[]{:S(2)}) async-start(bf16[4,128,512]{2,1,0:T(8,128)(2,1)} %pack_out.1), calls=%async_computation | async-start | bytes 1048576 | tf_op jit(solution)/shard_map/all_to_all | solution.py:325
  29.0 13.5 %copy-start.8 = (bf16[128,3200]{1,0:T(8,128)(2,1)}, bf16[128,3200]{1,0:T(8,128)(2,1)S(1)}, u32[]{:S(2)}) copy-start(bf16[128,3200]{1,0:T(8,128)(2,1)S(1)} %collective-permute-done.1.refs_2_) | copy-start | bytes 2457604
  29.0 13.4 %collective-permute-start.6 = (bf16[128,3200]{1,0:T(8,128)(2,1)}, bf16[128,3200]{1,0:T(8,128)(2,1)}, u32[]{:S(2)}, u32[]{:S(2)}) collective-permute-start(bf16[128,3200]{1,0:T(8,128)(2,1)} %collective-permute-done.2.refs_6_), channel_id=1, source_target_pairs={{0,16},{16,0},{32,48},{48,32},{64,80},{80,64},{96,112},{112,96},{1... | collective-permute-start | bytes 2457608 | tf_op jit(solution)/shard_map/ppermute | solution.py:331
  29.2 13.3 %collective-permute-start.4 = (bf16[64,3200]{1,0:T(8,128)(2,1)S(1)}, bf16[64,3200]{1,0:T(8,128)(2,1)}, u32[]{:S(2)}, u32[]{:S(2)}) collective-permute-start(bf16[64,3200]{1,0:T(8,128)(2,1)S(1)} %slice.6), channel_id=1, source_target_pairs={{0,1},{1,2},{2,3},{3,0},{4,5},{5,6},{6,7},{7,4},{8,9},{9,10},{10,1... | collective-permute-start | bytes 1228808 | tf_op jit(solution)/shard_map/ppermute | solution.py:330
  30.4 12.0 %collective-permute-start.5 = (bf16[64,3200]{1,0:T(8,128)(2,1)S(1)}, bf16[64,3200]{1,0:T(8,128)(2,1)}, u32[]{:S(2)}, u32[]{:S(2)}) collective-permute-start(bf16[64,3200]{1,0:T(8,128)(2,1)S(1)} %slice.7), channel_id=1, source_target_pairs={{0,3},{1,0},{2,1},{3,2},{4,7},{5,4},{6,5},{7,6},{8,11},{9,8},{10,9... | collective-permute-start | bytes 1228808 | tf_op jit(solution)/shard_map/ppermute | solution.py:330
  32.5 9.9 %collective-permute-start.7 = (bf16[64,3200]{1,0:T(8,128)(2,1)}, bf16[64,3200]{1,0:T(8,128)(2,1)}, u32[]{:S(2)}, u32[]{:S(2)}) collective-permute-start(bf16[64,3200]{1,0:T(8,128)(2,1)} %collective-permute-done.3.refs_8_), channel_id=1, source_target_pairs={{0,16},{16,0},{32,48},{48,32},{64,80},{80,64},{96,112},{112,96},{1... | collective-permute-start | bytes 1228808 | tf_op jit(solution)/shard_map/ppermute | solution.py:331
  35.0 29.8 %all-to-all-start.1 = ((bf16[16,3,128,128]{3,2,1,0:T(8,128)(2,1)}), bf16[16,3,128,128]{3,2,1,0:T(8,128)(2,1)S(1)}, u32[]{:S(2)}, u32[]{:S(2)}) async-start(bf16[16,3,128,128]{3,2,1,0:T(8,128)(2,1)} %pack.1), calls=%async_computation.1 | async-start | bytes 3145728 | tf_op jit(solution)/shard_map/all_to_all | solution.py:332
  52.4 5.4 %collective-permute-start.8 = (bf16[4,200,512]{2,1,0:T(8,128)(2,1)}, bf16[4,200,512]{2,1,0:T(8,128)(2,1)S(1)}, u32[]{:S(2)}, u32[]{:S(2)}) collective-permute-start(bf16[4,200,512]{2,1,0:T(8,128)(2,1)} %get-tuple-element.44), channel_id=1, source_target_pairs={{0,16},{16,0},{32,48},{48,32},{64,80},{80,64},{96,112},{112,96},{1... | collective-permute-start | bytes 2457608 | tf_op jit(solution)/shard_map/ppermute | solution.py:338
  52.5 5.3 %collective-permute-start.9 = (bf16[4,200,512]{2,1,0:T(8,128)(2,1)}, bf16[4,200,512]{2,1,0:T(8,128)(2,1)S(1)}, u32[]{:S(2)}, u32[]{:S(2)}) collective-permute-start(bf16[4,200,512]{2,1,0:T(8,128)(2,1)} %get-tuple-element.45), channel_id=1, source_target_pairs={{0,16},{16,0},{32,48},{48,32},{64,80},{80,64},{96,112},{112,96},{1... | collective-permute-start | bytes 2457608 | tf_op jit(solution)/shard_map/ppermute | solution.py:338
  53.0 11.7 %collective-permute-start.17 = (bf16[528,128]{1,0:T(8,128)(2,1)}, bf16[528,128]{1,0:T(8,128)(2,1)S(1)}, u32[]{:S(2)}, u32[]{:S(2)}) collective-permute-start(bf16[528,128]{1,0:T(8,128)(2,1)} %get-tuple-element.53), channel_id=1, source_target_pairs={{0,12},{1,13},{2,14},{3,15},{4,0},{5,1},{6,2},{7,3},{8,4},{9,5},{1... | collective-permute-start | bytes 405512 | tf_op jit(solution)/shard_map/ppermute | solution.py:336
  53.6 14.7 %collective-permute-start.18 = (bf16[528,128]{1,0:T(8,128)(2,1)}, bf16[528,128]{1,0:T(8,128)(2,1)S(1)}, u32[]{:S(2)}, u32[]{:S(2)}) collective-permute-start(bf16[528,128]{1,0:T(8,128)(2,1)} %get-tuple-element.54), channel_id=1, source_target_pairs={{0,8},{1,9},{2,10},{3,11},{4,12},{5,13},{6,14},{7,15},{8,0},{9,1},... | collective-permute-start | bytes 405512 | tf_op jit(solution)/shard_map/ppermute | solution.py:336
  56.0 12.3 %collective-permute-start.19 = (bf16[528,128]{1,0:T(8,128)(2,1)}, bf16[528,128]{1,0:T(8,128)(2,1)S(1)}, u32[]{:S(2)}, u32[]{:S(2)}) collective-permute-start(bf16[528,128]{1,0:T(8,128)(2,1)} %get-tuple-element.55), channel_id=1, source_target_pairs={{0,4},{1,5},{2,6},{3,7},{4,8},{5,9},{6,10},{7,11},{8,12},{9,13},{1... | collective-permute-start | bytes 405512 | tf_op jit(solution)/shard_map/ppermute | solution.py:336
  62.5 20.2 %collective-permute-start.10 = (bf16[8,200,128]{2,1,0:T(8,128)(2,1)}, bf16[8,200,128]{2,1,0:T(8,128)(2,1)S(1)}, u32[]{:S(2)}, u32[]{:S(2)}) collective-permute-start(bf16[8,200,128]{2,1,0:T(8,128)(2,1)} %get-tuple-element.47), channel_id=1, source_target_pairs={{0,4},{1,5},{2,6},{3,7},{4,8},{5,9},{6,10},{7,11},{8,12},{9,13},{1... | collective-permute-start | bytes 1228808 | tf_op jit(solution)/shard_map/ppermute | solution.py:346
  62.5 20.2 %collective-permute-start.11 = (bf16[8,200,128]{2,1,0:T(8,128)(2,1)}, bf16[8,200,128]{2,1,0:T(8,128)(2,1)S(1)}, u32[]{:S(2)}, u32[]{:S(2)}) collective-permute-start(bf16[8,200,128]{2,1,0:T(8,128)(2,1)} %get-tuple-element.48), channel_id=1, source_target_pairs={{0,8},{1,9},{2,10},{3,11},{4,12},{5,13},{6,14},{7,15},{8,0},{9,1},... | collective-permute-start | bytes 1228808 | tf_op jit(solution)/shard_map/ppermute | solution.py:346
  64.8 21.0 %collective-permute-start.12 = (bf16[8,200,128]{2,1,0:T(8,128)(2,1)}, bf16[8,200,128]{2,1,0:T(8,128)(2,1)S(1)}, u32[]{:S(2)}, u32[]{:S(2)}) collective-permute-start(bf16[8,200,128]{2,1,0:T(8,128)(2,1)} %get-tuple-element.49), channel_id=1, source_target_pairs={{0,12},{1,13},{2,14},{3,15},{4,0},{5,1},{6,2},{7,3},{8,4},{9,5},{1... | collective-permute-start | bytes 1228808 | tf_op jit(solution)/shard_map/ppermute | solution.py:346
  75.9 28.6 %all-to-all-start.2 = ((bf16[16,3,128,128]{3,2,1,0:T(8,128)(2,1)}), bf16[16,3,128,128]{3,2,1,0:T(8,128)(2,1)}, u32[]{:S(2)}, u32[]{:S(2)}) async-start(bf16[16,3,128,128]{3,2,1,0:T(8,128)(2,1)} %attention.1), calls=%async_computation.2 | async-start | bytes 3145728 | tf_op jit(solution)/shard_map/all_to_all | solution.py:341
  86.0 7.1 %collective-permute-start.13 = (bf16[4,200,128]{2,1,0:T(8,128)(2,1)S(1)}, bf16[4,200,128]{2,1,0:T(8,128)(2,1)S(1)}, u32[]{:S(2)}, u32[]{:S(2)}) collective-permute-start(bf16[4,200,128]{2,1,0:T(8,128)(2,1)S(1)} %fusion), channel_id=1, source_target_pairs={{0,32},{16,48},{32,0},{48,16},{64,96},{80,112},{96,64},{112,80},{1... | collective-permute-start | bytes 614408 | tf_op jit(solution)/shard_map/ppermute | solution.py:350
  93.2 13.7 %collective-permute-start.14 = (bf16[200,128]{1,0:T(8,128)(2,1)S(1)}, bf16[200,128]{1,0:T(8,128)(2,1)S(1)}, u32[]{:S(2)}, u32[]{:S(2)}) collective-permute-start(bf16[200,128]{1,0:T(8,128)(2,1)S(1)} %get-tuple-element.68), channel_id=1, source_target_pairs={{0,64},{16,80},{32,96},{48,112},{64,128},{80,144},{96,160},{112,17... | collective-permute-start | bytes 153608 | tf_op jit(solution)/shard_map/ppermute | solution.py:354
  96.6 10.4 %collective-permute-start.15 = (bf16[200,128]{1,0:T(8,128)(2,1)S(1)}, bf16[200,128]{1,0:T(8,128)(2,1)S(1)}, u32[]{:S(2)}, u32[]{:S(2)}) collective-permute-start(bf16[200,128]{1,0:T(8,128)(2,1)S(1)} %get-tuple-element.67), channel_id=1, source_target_pairs={{0,128},{16,144},{32,160},{48,176},{64,192},{80,208},{96,224},{112... | collective-permute-start | bytes 153608 | tf_op jit(solution)/shard_map/ppermute | solution.py:354
  101.8 5.2 %collective-permute-start.16 = (bf16[200,128]{1,0:T(8,128)(2,1)S(1)}, bf16[200,128]{1,0:T(8,128)(2,1)S(1)}, u32[]{:S(2)}, u32[]{:S(2)}) collective-permute-start(bf16[200,128]{1,0:T(8,128)(2,1)S(1)} %get-tuple-element.66), channel_id=1, source_target_pairs={{0,192},{16,208},{32,224},{48,240},{64,0},{80,16},{96,32},{112,48}... | collective-permute-start | bytes 153608 | tf_op jit(solution)/shard_map/ppermute | solution.py:354
  (8 other events, 51.9 us)
